TPU v7x, 32 devices: a whole 2x2x4 slice. The times are simulated.
32 devices in a mesh: row: 4 (over z), col: 8 (over y, x, core).
Axes of the slice: x: 2, y: 2, z: 4, core: 2. Of those that a mesh axis runs over, the one named last changes fastest.
Arguments:
- blocks: bfloat16 [4, 8, 256, 128, 128], P('row', 'col'), may hold values from 0 to 0.0625
- slot_rows: int32 [4, 8, 256], P('row', 'col'), may hold values from 0 to 63, as said below
- slot_cols: int32 [4, 8, 256], P('row', 'col'), may hold values from 0 to 31, as said below
- counts: int32 [4, 8], P('row', 'col'), may hold values from 0 to 256, as said below
- reward_table: bfloat16 [32, 32768], P('row', 'col'), may hold values from -6 to 6
- reward_cols: int32 [16], replicated, may hold values from 0 to 31, as said below
- cotangent: bfloat16 [16, 32768], P(None, ('row', 'col')), may hold values from -6 to 6
Outputs:
- value: float32 [16, 32768], P(None, ('row', 'col'))
- grad: float32 [16, 32768], P('row', 'col')
Inputs may be any that keep to these rules, and one draw needn't show every extreme that they name: `counts`: stored blocks of each grid cell; along every grid row the cells of even index hold 512 of them, and so do the cells of odd index, and some cell of every grid row holds exactly 256. Only the first counts[a, b] slots of a grid cell hold stored blocks; every block row has exactly 16 stored blocks; slot_rows[a, b, s] is even where b is even and odd where b is odd. `slot_cols`: two stored blocks at the same position add. `reward_cols`: distinct candidates.
All inputs are finite; a program needn't handle non-finite values.
Results may differ from a plain program's by a relative error of at most 0.0003.
Values may be sent and summed in bfloat16 or wider, within the bound.
No kernel may reach another device: no remote copies, remote signals or barrier semaphores. Data moves between devices by JAX's collectives and lax.ppermute only.
A program may use at most 64 MiB of HBM per device.

v0:
```python
import jax
import jax.numpy as jnp
from jax import lax
from jax.sharding import PartitionSpec as P

BLK = 128
REWARDS = 16
GROUP = 32


def apply_slots(
    stored,
    rows_here,
    cols_here,
    live_count,
    reward_cells,
    weight_cells,
    value_acc,
    grad_acc,
    passes_mode,
):
    group_count = (live_count + GROUP - 1) // GROUP

    def visit(group_index, totals):
        value_now, grad_now = totals
        first_slot = group_index * GROUP
        block_set = lax.dynamic_slice_in_dim(stored, first_slot, GROUP, 0)
        row_set = lax.dynamic_slice_in_dim(rows_here, first_slot, GROUP, 0)
        col_set = lax.dynamic_slice_in_dim(cols_here, first_slot, GROUP, 0)
        live_mask = (first_slot + jnp.arange(GROUP, dtype=jnp.int32) < live_count).astype(
            jnp.float32
        )[None, :, None]
        if passes_mode != "adjoint":
            picked = jnp.take(reward_cells, col_set, axis=1)
            product = jnp.einsum(
                "kgc,grc->kgr", picked, block_set, preferred_element_type=jnp.float32
            )
            value_now = value_now.at[:, row_set].add(product * live_mask)
        if passes_mode != "forward":
            weights = jnp.take(weight_cells, row_set, axis=1)
            product = jnp.einsum(
                "kgr,grc->kgc", weights, block_set, preferred_element_type=jnp.float32
            )
            grad_now = grad_now.at[:, col_set].add(product * live_mask)
        return (value_now, grad_now)

    return lax.fori_loop(0, group_count, visit, (value_acc, grad_acc))


def on_device(blocks, slot_rows, slot_cols, counts, reward_table, reward_cols, cotangent):
    stored = blocks[0, 0]
    rows_here = slot_rows[0, 0]
    cols_here = slot_cols[0, 0]
    live_count = counts[0, 0]
    reward_full = lax.all_gather(reward_table, "row", axis=0, tiled=True)
    rewards = jnp.take(reward_full, reward_cols, axis=0)
    sb_col = rewards.shape[1] // BLK
    reward_cells = rewards.reshape(REWARDS, sb_col, BLK)
    weight_full = lax.all_gather(cotangent, "col", axis=1, tiled=True)
    sb_row = weight_full.shape[1] // BLK
    weight_cells = weight_full.reshape(REWARDS, sb_row, BLK)
    value_acc = jnp.zeros((REWARDS, sb_row, BLK), jnp.float32)
    grad_acc = jnp.zeros((REWARDS, sb_col, BLK), jnp.float32)
    value_acc, grad_acc = apply_slots(
        stored,
        rows_here,
        cols_here,
        live_count,
        reward_cells,
        weight_cells,
        value_acc,
        grad_acc,
        "forward",
    )
    value = lax.psum_scatter(
        value_acc.reshape(REWARDS, sb_row * BLK), "col", scatter_dimension=1, tiled=True
    )
    value_acc, grad_acc = apply_slots(
        stored,
        rows_here,
        cols_here,
        live_count,
        reward_cells,
        weight_cells,
        value_acc,
        grad_acc,
        "adjoint",
    )
    grad = lax.psum_scatter(
        grad_acc.reshape(REWARDS, sb_col * BLK), "row", scatter_dimension=0, tiled=True
    )
    return (value, grad)


def solution(mesh):
    placed = (
        P("row", "col", None, None, None),
        P("row", "col", None),
        P("row", "col", None),
        P("row", "col"),
        P("row", "col"),
        P(),
        P(None, ("row", "col")),
    )
    return jax.shard_map(
        on_device,
        mesh=mesh,
        in_specs=placed,
        out_specs=(P(None, ("row", "col")), P("row", "col")),
        check_vma=False,
    )
```

profile of v0, /device:TPU:0, one launch (start us, length us, event | category | flops | bytes accessed | tf_op | source)
XLA Modules:
  0.0 179.9 jit_solution(2427035394897533110)
XLA Ops:
  8.7 11.0 %all_gather.7 = bf16[16,8192]{1,0:T(8,128)(2,1)S(1)} all-gather(bf16[16,1024]{1,0:T(8,128)(2,1)} %param.17), channel_id=1, replica_groups=mesh['row'=4,'col'=8] {'col'}, dimensions={1}, use_global_device_ids=true | all-gather | bytes 294912 | tf_op jit(solution)/shard_map/all_gather | solution.py:59
  19.8 49.5 %while.21 = (s32[]{:T(128)}, f32[16,32,128]{2,0,1:T(8,128)S(1)}, s32[]{:T(128)}, s32[256]{0:T(256)}, bf16[256,128,128]{2,1,0:T(8,128)(2,1)}, /*index=5*/s32[256]...) while((s32[]{:T(128)}, f32[16,32,128]{2,0,1:T(8,128)S(1)}, ...), condition=%wide.region_6.7_spmd, body=%wide.region_4.6_spmd.sunk | while | flops 16975236 | bytes 2495863 | solution.py:47
  19.8 1.4 compare_and_fusion.6
  21.8 1.7 fusion.31
  24.3 1.7 scatter_fusion.1
  26.0 1.4 compare_and_fusion.6
  28.0 1.7 fusion.31
  30.4 1.7 scatter_fusion.1
  32.2 1.4 compare_and_fusion.6
  34.2 1.7 fusion.31
  36.6 1.7 scatter_fusion.1
  38.4 1.4 compare_and_fusion.6
  40.4 1.7 fusion.31
  42.8 1.7 scatter_fusion.1
  44.5 1.4 compare_and_fusion.6
  46.6 1.7 fusion.31
  49.0 1.7 scatter_fusion.1
  50.7 1.4 compare_and_fusion.6
  52.7 1.7 fusion.31
  55.2 1.7 scatter_fusion.1
  56.9 1.4 compare_and_fusion.6
  58.9 1.7 fusion.31
  61.4 1.7 scatter_fusion.1
  65.1 1.7 fusion.31
  67.5 1.7 scatter_fusion.1
  70.1 14.4 %all_gather.6 = bf16[32,4096]{1,0:T(8,128)(2,1)S(1)} all-gather(bf16[8,4096]{1,0:T(8,128)(2,1)S(1)} %copy-done), channel_id=1, replica_groups=mesh['row'=4,'col'=8] {'row'}, dimensions={0}, use_global_device_ids=true | all-gather | bytes 327680 | tf_op jit(solution)/shard_map/all_gather | solution.py:55
  85.3 51.4 %while.20 = (s32[]{:T(128)}, f32[16,64,128]{2,0,1:T(8,128)S(1)}, s32[]{:T(128)}, s32[256]{0:T(256)}, bf16[256,128,128]{2,1,0:T(8,128)(2,1)}, /*index=5*/s32[256]...) while((s32[]{:T(128)}, f32[16,64,128]{2,0,1:T(8,128)S(1)}, ...), condition=%wide.region_2.3_spmd, body=%wide.region_0.0_spmd.sunk | while | flops 16975236 | bytes 2495863 | solution.py:47
  85.3 1.4 compare_and_fusion.5
  87.3 1.9 %fusion.28 = f32[32,16,128]{2,1,0:T(8,128)S(1)} fusion(bf16[256,128,128]{2,1,0:T(8,128)(2,1)} %get-tuple-element.284, s32[]{:T(128)S(6)} %select_n.80, bf16[32,16,128]{2,1,0:T(8,128)(2,1)S(1)} %gather_fusion, f32[32]{0:T(128)S(1)} %get-tuple-element.243, pred[32]{0:T(512)(128)(4,1)S(1)} %get-tuple-element.244), kind=kOutput, calls=%fused_computation.6.clone.1 | convolution fusion | flops 16908288 | bytes 1441956 | tf_op jit(solution)/shard_map/while/body/kgc,grc->kgr/dot_general | solution.py:35
  90.0 1.7 scatter_fusion
  91.7 1.4 compare_and_fusion.5
  93.7 1.9 %fusion.28 = f32[32,16,128]{2,1,0:T(8,128)S(1)} fusion(bf16[256,128,128]{2,1,0:T(8,128)(2,1)} %get-tuple-element.284, s32[]{:T(128)S(6)} %select_n.80, bf16[32,16,128]{2,1,0:T(8,128)(2,1)S(1)} %gather_fusion, f32[32]{0:T(128)S(1)} %get-tuple-element.243, pred[32]{0:T(512)(128)(4,1)S(1)} %get-tuple-element.244), kind=kOutput, calls=%fused_computation.6.clone.1 | convolution fusion | flops 16908288 | bytes 1441956 | tf_op jit(solution)/shard_map/while/body/kgc,grc->kgr/dot_general | solution.py:35
  96.4 1.7 scatter_fusion
  100.2 1.9 %fusion.28 = f32[32,16,128]{2,1,0:T(8,128)S(1)} fusion(bf16[256,128,128]{2,1,0:T(8,128)(2,1)} %get-tuple-element.284, s32[]{:T(128)S(6)} %select_n.80, bf16[32,16,128]{2,1,0:T(8,128)(2,1)S(1)} %gather_fusion, f32[32]{0:T(128)S(1)} %get-tuple-element.243, pred[32]{0:T(512)(128)(4,1)S(1)} %get-tuple-element.244), kind=kOutput, calls=%fused_computation.6.clone.1 | convolution fusion | flops 16908288 | bytes 1441956 | tf_op jit(solution)/shard_map/while/body/kgc,grc->kgr/dot_general | solution.py:35
  102.9 1.7 scatter_fusion
  106.6 1.9 %fusion.28 = f32[32,16,128]{2,1,0:T(8,128)S(1)} fusion(bf16[256,128,128]{2,1,0:T(8,128)(2,1)} %get-tuple-element.284, s32[]{:T(128)S(6)} %select_n.80, bf16[32,16,128]{2,1,0:T(8,128)(2,1)S(1)} %gather_fusion, f32[32]{0:T(128)S(1)} %get-tuple-element.243, pred[32]{0:T(512)(128)(4,1)S(1)} %get-tuple-element.244), kind=kOutput, calls=%fused_computation.6.clone.1 | convolution fusion | flops 16908288 | bytes 1441956 | tf_op jit(solution)/shard_map/while/body/kgc,grc->kgr/dot_general | solution.py:35
  109.3 1.7 scatter_fusion
  113.0 1.9 %fusion.28 = f32[32,16,128]{2,1,0:T(8,128)S(1)} fusion(bf16[256,128,128]{2,1,0:T(8,128)(2,1)} %get-tuple-element.284, s32[]{:T(128)S(6)} %select_n.80, bf16[32,16,128]{2,1,0:T(8,128)(2,1)S(1)} %gather_fusion, f32[32]{0:T(128)S(1)} %get-tuple-element.243, pred[32]{0:T(512)(128)(4,1)S(1)} %get-tuple-element.244), kind=kOutput, calls=%fused_computation.6.clone.1 | convolution fusion | flops 16908288 | bytes 1441956 | tf_op jit(solution)/shard_map/while/body/kgc,grc->kgr/dot_general | solution.py:35
  115.7 1.7 scatter_fusion
  119.4 1.9 %fusion.28 = f32[32,16,128]{2,1,0:T(8,128)S(1)} fusion(bf16[256,128,128]{2,1,0:T(8,128)(2,1)} %get-tuple-element.284, s32[]{:T(128)S(6)} %select_n.80, bf16[32,16,128]{2,1,0:T(8,128)(2,1)S(1)} %gather_fusion, f32[32]{0:T(128)S(1)} %get-tuple-element.243, pred[32]{0:T(512)(128)(4,1)S(1)} %get-tuple-element.244), kind=kOutput, calls=%fused_computation.6.clone.1 | convolution fusion | flops 16908288 | bytes 1441956 | tf_op jit(solution)/shard_map/while/body/kgc,grc->kgr/dot_general | solution.py:35
  122.1 1.7 scatter_fusion
  125.9 1.9 %fusion.28 = f32[32,16,128]{2,1,0:T(8,128)S(1)} fusion(bf16[256,128,128]{2,1,0:T(8,128)(2,1)} %get-tuple-element.284, s32[]{:T(128)S(6)} %select_n.80, bf16[32,16,128]{2,1,0:T(8,128)(2,1)S(1)} %gather_fusion, f32[32]{0:T(128)S(1)} %get-tuple-element.243, pred[32]{0:T(512)(128)(4,1)S(1)} %get-tuple-element.244), kind=kOutput, calls=%fused_computation.6.clone.1 | convolution fusion | flops 16908288 | bytes 1441956 | tf_op jit(solution)/shard_map/while/body/kgc,grc->kgr/dot_general | solution.py:35
  128.6 1.7 scatter_fusion
  130.3 1.4 compare_and_fusion.5
  132.3 1.9 %fusion.28 = f32[32,16,128]{2,1,0:T(8,128)S(1)} fusion(bf16[256,128,128]{2,1,0:T(8,128)(2,1)} %get-tuple-element.284, s32[]{:T(128)S(6)} %select_n.80, bf16[32,16,128]{2,1,0:T(8,128)(2,1)S(1)} %gather_fusion, f32[32]{0:T(128)S(1)} %get-tuple-element.243, pred[32]{0:T(512)(128)(4,1)S(1)} %get-tuple-element.244), kind=kOutput, calls=%fused_computation.6.clone.1 | convolution fusion | flops 16908288 | bytes 1441956 | tf_op jit(solution)/shard_map/while/body/kgc,grc->kgr/dot_general | solution.py:35
  135.0 1.7 scatter_fusion
  138.8 1.5 constant_dynamic-slice_fusion
  140.4 32.1 %reduce-scatter.2.cloned.1.call-done = f32[16,1024]{1,0:T(8,128)} async-done(((f32[16,8192]{1,0:T(8,128)}), f32[16,1024]{1,0:T(8,128)}) %reduce-scatter.2.cloned.1.call-update) | async-done | bytes 65552 | tf_op jit(solution)/shard_map/reduce_scatter | solution.py:75
  (76 shorter events, 33.4 us)
Async XLA Ops:
  8.0 130.8 %all-reduce.3.cloned.1.call-start = ((), (), s32[]{:S(2)}) async-start(), calls=%async_computation.2 | async-start | bytes 524288
  19.8 50.3 %copy-start.1 = (s32[16]{0:T(128)S(1)}, s32[16]{0:T(128)}, u32[]{:S(2)}) copy-start(s32[16]{0:T(128)} %param.16) | copy-start | bytes 196
  19.8 50.3 %copy-start = (bf16[8,4096]{1,0:T(8,128)(2,1)S(1)}, bf16[8,4096]{1,0:T(8,128)(2,1)}, u32[]{:S(2)}) copy-start(bf16[8,4096]{1,0:T(8,128)(2,1)} %param.15) | copy-start | bytes 196612
  70.0 102.4 %reduce-scatter.2.cloned.1.call-start = ((), (), s32[]{:S(2)}) async-start(), calls=%async_computation.1 | async-start | bytes 589824 | tf_op jit(solution)/shard_map/reduce_scatter | solution.py:75
  85.3 52.3 %copy-start.2 = (u32[32]{0:T(128)S(1)}, u32[32]{0:T(128)}, u32[]{:S(2)}) copy-start(u32[32]{0:T(128)} %constant.95) | copy-start | bytes 388
Sparse Core Ops, SparseCore 0:
  70.1 36.2 all-reduce.2
Sparse Core Ops, SparseCore 1:
  137.6 34.8 reduce-scatter.1
where the time goes:
time: 181 us; the launch traced here: 180 us
  other arithmetic  62.2 us (34%)
  waiting for transfers between devices  32.1 us (18%)
  matrix products  28.7 us (16%)
  blocking collectives  25.4 us (14%)
  between operations  16.9 us (9%)
  local copies, waits for them, and re-layouts  13.9 us (8%)
    reduce_scatter x1, waiting for transfers between devices, on_device(): lax.psum_scatter(value_acc.reshape(REWARDS, sb_row * BLK), 'col', scatter...  32.1 us
    dot_general x8, matrix products, visit(): jnp.einsum('kgc,grc->kgr', picked, block_set, preferred_element_type=jnp....  15.4 us
    all_gather x1, blocking collectives, on_device(): reward_full = lax.all_gather(reward_table, 'row', axis=0, tiled=True)  14.4 us
    scatter-add x8, other arithmetic, visit(): grad_now = grad_now.at[:, col_set].add(product * live_mask)  13.7 us
    scatter-add x8, other arithmetic, visit(): value_now = value_now.at[:, row_set].add(product * live_mask)  13.6 us
    dot_general x8, matrix products, visit(): jnp.einsum('kgr,grc->kgc', weights, block_set, preferred_element_type=jnp...  13.3 us
    and x8, other arithmetic, visit(): picked = jnp.take(reward_cells, col_set, axis=1)  11.3 us
    and x8, other arithmetic, visit(): weights = jnp.take(weight_cells, row_set, axis=1)  11.3 us
  transfers between devices with their start and end apart: 2, of which 1 were waited for; matrix products, arithmetic and copies ran while one was open for 30% of the time, Pallas kernels for 0%

commit v1 on v0

v1 whole, which is shorter than its diff:
```python
import functools

import jax
import jax.numpy as jnp
from jax import lax
from jax.experimental import pallas as pl
from jax.experimental.pallas import tpu as pltpu
from jax.sharding import PartitionSpec as P

BLK = 128
REWARDS = 16
CHUNK = 64
VMEM_LIMIT = 40 * 2**20


def peers(size, step):
    return [(here, here ^ step) for here in range(size)]


def tile_of(blocks, slots):
    stored = [blocks[0, 0, slot] for slot in slots]
    left = jnp.concatenate(stored[:2], axis=0)
    right = jnp.concatenate(stored[2:], axis=0)
    return jnp.concatenate([left, right], axis=1)


def spread(first, second):
    empty = jnp.zeros((2 * REWARDS, BLK), jnp.bfloat16)
    top = jnp.concatenate([jnp.concatenate(first, axis=0), empty], axis=1)
    bottom = jnp.concatenate([empty, jnp.concatenate(second, axis=0)], axis=1)
    return jnp.concatenate([top, bottom], axis=0)


def each_chunk(live_count, visit):
    chunks = (live_count + CHUNK - 1) // CHUNK
    lax.fori_loop(0, chunks, lambda chunk, carry: (visit(chunk * CHUNK), carry)[1], 0)


def places(slot, live_count, slot_rows, slot_cols, row_cells, col_cells):
    live = slot < live_count
    row = jnp.where(live, slot_rows[0, 0, slot] // 2, row_cells)
    col = jnp.where(live, slot_cols[0, 0, slot], col_cells)
    return row, col


def adjoint_kernel(n_row, n_col, slot_rows, slot_cols, counts, blocks, *refs):
    shards, sends = refs[:n_col], refs[n_col : n_col + n_row]
    weights, totals = refs[n_col + n_row :]
    own_row, own_col = lax.axis_index("row"), lax.axis_index("col")
    row_cells, col_cells = weights.shape[0] - 1, totals.shape[0] - 1
    owned = row_cells // n_col
    parity = own_col % 2
    for step, shard in enumerate(shards):
        first = (own_col ^ step) * owned
        for at in range(owned):
            lane = pl.multiple_of((2 * at + parity) * BLK, BLK)
            weights[first + at] = shard[:, pl.ds(lane, BLK)]
    weights[row_cells] = jnp.zeros((REWARDS, BLK), jnp.bfloat16)
    totals[...] = jnp.zeros_like(totals)
    live_count = counts[0, 0]

    def visit(start):
        found = []
        for quad in range(0, CHUNK, 4):
            slots = [start + quad + at for at in range(4)]
            at = [places(s, live_count, slot_rows, slot_cols, row_cells, col_cells) for s in slots]
            factor = [weights[row] for row, _ in at]
            product = lax.dot_general(
                spread((factor[0], factor[2]), (factor[1], factor[3])),
                tile_of(blocks, slots),
                (((1,), (0,)), ((), ())),
                preferred_element_type=jnp.float32,
            )
            for piece, (which, side) in enumerate(((0, 0), (2, 1), (1, 0), (3, 1))):
                found.append(
                    (
                        at[which][1],
                        product[piece * REWARDS : (piece + 1) * REWARDS, side * BLK : (side + 1) * BLK],
                    )
                )
        for col, part in found:
            totals[col] += part

    each_chunk(live_count, visit)
    group = REWARDS // n_row
    for step, send in enumerate(sends):
        first = (own_row ^ step) * group
        for col in range(col_cells):
            send[:, col * BLK : (col + 1) * BLK] = totals[col, pl.ds(first, group), :]


def forward_kernel(n_row, n_col, slot_rows, slot_cols, counts, reward_cols, blocks, *refs):
    n_chip = n_col // 2
    tables, sends = refs[:n_row], refs[n_row : n_row + n_chip]
    table, rewards, totals = refs[n_row + n_chip :]
    own_row, own_chip = lax.axis_index("row"), lax.axis_index("col") // 2
    row_cells, col_cells = totals.shape[0] - 1, rewards.shape[0] - 1
    group = tables[0].shape[0]
    candidates = group * n_row
    for step, part in enumerate(tables):
        table[step * group : (step + 1) * group, :] = part[...].astype(jnp.float32)
    lane = lax.broadcasted_iota(jnp.int32, (REWARDS, candidates), 1)
    column = lane % group + (own_row ^ (lane // group)) * group
    line = lax.broadcasted_iota(jnp.int32, (REWARDS, candidates), 0)
    wanted = jnp.zeros((REWARDS, candidates), jnp.int32)
    for k in range(REWARDS):
        wanted = jnp.where(line == k, reward_cols[k], wanted)
    pick = (column == wanted).astype(jnp.float32).astype(jnp.bfloat16)
    for col in range(col_cells):
        rewards[col] = jnp.dot(
            pick,
            table[:, col * BLK : (col + 1) * BLK].astype(jnp.bfloat16),
            preferred_element_type=jnp.float32,
        ).astype(jnp.bfloat16)
    rewards[col_cells] = jnp.zeros((REWARDS, BLK), jnp.bfloat16)
    totals[...] = jnp.zeros_like(totals)
    live_count = counts[0, 0]

    def visit(start):
        found = []
        for quad in range(0, CHUNK, 4):
            slots = [start + quad + at for at in range(4)]
            at = [places(s, live_count, slot_rows, slot_cols, row_cells, col_cells) for s in slots]
            factor = [rewards[col] for _, col in at]
            product = lax.dot_general(
                spread((factor[0], factor[1]), (factor[2], factor[3])),
                tile_of(blocks, slots),
                (((1,), (1,)), ((), ())),
                preferred_element_type=jnp.float32,
            )
            for piece, (which, side) in enumerate(((0, 0), (1, 1), (2, 0), (3, 1))):
                found.append(
                    (
                        at[which][0],
                        product[piece * REWARDS : (piece + 1) * REWARDS, side * BLK : (side + 1) * BLK],
                    )
                )
        for row, part in found:
            totals[row] += part

    each_chunk(live_count, visit)
    part = row_cells // n_chip
    for step, send in enumerate(sends):
        send[...] = totals[pl.ds((own_chip ^ step) * part, part)]


def join_kernel(own, other, out):
    parity = lax.axis_index("col") % 2
    part = own.shape[0] // 2
    for at in range(part):
        here, there = own[parity * part + at], other[parity * part + at]
        even = jnp.where(parity == 0, here, there)
        odd = jnp.where(parity == 0, there, here)
        out[:, 2 * at * BLK : (2 * at + 1) * BLK] = even
        out[:, (2 * at + 1) * BLK : (2 * at + 2) * BLK] = odd


def on_device(n_row, n_col, blocks, slot_rows, slot_cols, counts, reward_table, reward_cols, cotangent):
    n_chip = n_col // 2
    row_cells = n_col * (cotangent.shape[1] // BLK) // 2
    col_cells = reward_table.shape[1] // BLK
    smem = pl.BlockSpec(memory_space=pltpu.SMEM)
    vmem = pl.BlockSpec(memory_space=pltpu.VMEM)
    params = pltpu.CompilerParams(vmem_limit_bytes=VMEM_LIMIT)

    tables = [reward_table] + [
        lax.ppermute(reward_table, "row", peers(n_row, step)) for step in range(1, n_row)
    ]
    shards = []
    for chip in range(n_chip):
        here = lax.ppermute(cotangent, "col", peers(n_col, 2 * chip)) if chip else cotangent
        shards += [here, lax.ppermute(here, "col", peers(n_col, 1))]

    group = REWARDS // n_row
    grads = pl.pallas_call(
        functools.partial(adjoint_kernel, n_row, n_col),
        out_shape=[jax.ShapeDtypeStruct((group, col_cells * BLK), jnp.float32)] * n_row,
        in_specs=[smem] * 3 + [vmem] * (1 + n_col),
        out_specs=[vmem] * n_row,
        scratch_shapes=[
            pltpu.VMEM((row_cells + 1, REWARDS, BLK), jnp.bfloat16),
            pltpu.VMEM((col_cells + 1, REWARDS, BLK), jnp.float32),
        ],
        compiler_params=params,
    )(slot_rows, slot_cols, counts, blocks, *shards)
    grad = grads[0]
    for step in range(1, n_row):
        grad = grad + lax.ppermute(grads[step], "row", peers(n_row, step))

    part = row_cells // n_chip
    values = pl.pallas_call(
        functools.partial(forward_kernel, n_row, n_col),
        out_shape=[jax.ShapeDtypeStruct((part, REWARDS, BLK), jnp.float32)] * n_chip,
        in_specs=[smem] * 4 + [vmem] * (1 + n_row),
        out_specs=[vmem] * n_chip,
        scratch_shapes=[
            pltpu.VMEM((reward_table.shape[0] * n_row, col_cells * BLK), jnp.float32),
            pltpu.VMEM((col_cells + 1, REWARDS, BLK), jnp.bfloat16),
            pltpu.VMEM((row_cells + 1, REWARDS, BLK), jnp.float32),
        ],
        compiler_params=params,
    )(slot_rows, slot_cols, counts, reward_cols, blocks, *tables)
    value = values[0]
    for step in range(1, n_chip):
        value = value + lax.ppermute(values[step], "col", peers(n_col, 2 * step))
    other = lax.ppermute(value, "col", peers(n_col, 1))
    value = pl.pallas_call(
        join_kernel,
        out_shape=jax.ShapeDtypeStruct((REWARDS, part * BLK), jnp.float32),
        in_specs=[vmem, vmem],
        out_specs=vmem,
    )(value, other)
    return value, grad


def solution(mesh):
    placed = (
        P("row", "col", None, None, None),
        P("row", "col", None),
        P("row", "col", None),
        P("row", "col"),
        P("row", "col"),
        P(),
        P(None, ("row", "col")),
    )
    return jax.shard_map(
        functools.partial(on_device, mesh.shape["row"], mesh.shape["col"]),
        mesh=mesh,
        in_specs=placed,
        out_specs=(P(None, ("row", "col")), P("row", "col")),
        check_vma=False,
    )
```

time: 181 us -> 44.3 us (0.24)
  other arithmetic: 62.2 us -> 0.69 us
  matrix products: 28.7 us -> 0 us
  waiting for transfers between devices: 32.1 us -> 5.94 us
  blocking collectives: 25.4 us -> 0 us
  starting transfers between devices: 0.08 us -> 20.4 us
  between operations: 16.9 us -> 1.39 us
  Pallas kernels: 0 us -> 8.55 us
  local copies, waits for them, and re-layouts: 13.9 us -> 6.87 us
    reduce_scatter x1 -> x0, waiting for transfers between devices: 32.1 us -> none  [on_device(): lax.psum_scatter(value_acc.reshape(REWARDS, sb_row * BLK), 'col', scatter...]
    dot_general x16 -> x0, matrix products: 28.7 us -> none  [the longest x8 15.4 us: visit(): jnp.einsum('kgc,grc->kgr', picked, block_set, preferred_element_type=jnp....]
    scatter-add x16 -> x0, other arithmetic: 27.3 us -> none  [the longest x8 13.7 us: visit(): grad_now = grad_now.at[:, col_set].add(product * live_mask)]
    all_gather x2 -> x0, blocking collectives: 25.4 us -> none  [the longest x1 14.4 us: on_device(): reward_full = lax.all_gather(reward_table, 'row', axis=0, tiled=True)]
    and x17 -> x0, other arithmetic: 22.5 us -> none  [the longest x8 11.3 us: visit(): picked = jnp.take(reward_cells, col_set, axis=1)]
    ppermute x0 -> x17, starting transfers between devices: none -> 20.4 us  [the longest x3 5.96 us: on_device(): lax.ppermute(cotangent, 'col', peers(n_col, 2 * chip))]
    select_n x18 -> x0, other arithmetic: 12.4 us -> none  [the longest x8 6.15 us: visit(): value_now = value_now.at[:, row_set].add(product * live_mask)]
    gather x17 -> x0, local copies, waits for them, and re-layouts: 10.1 us -> none  [the longest x8 4.73 us: visit(): picked = jnp.take(reward_cells, col_set, axis=1)]
  transfers between devices with their start and end apart: 2 -> 17, of which waited for: 1 -> 5; matrix products, arithmetic and copies ran while one was open for 30% -> 2% of each run, Pallas kernels for 0% -> 16%
where the time goes in v1:
time: 44.3 us; the launch traced here: 43.9 us
  starting transfers between devices  20.4 us (46%)
  Pallas kernels  8.55 us (19%)
  local copies, waits for them, and re-layouts  6.87 us (16%)
  waiting for transfers between devices  5.94 us (13%)
  between operations  1.39 us (3%)
  other arithmetic  0.69 us (2%)
    unnamed x18, local copies, waits for them, and re-layouts  6.87 us
    ppermute x3, starting transfers between devices, on_device(): lax.ppermute(cotangent, 'col', peers(n_col, 2 * chip))  5.96 us
    ppermute x3, starting transfers between devices, on_device(): lax.ppermute(reward_table, 'row', peers(n_row, step))  5.68 us
    ppermute x3, starting transfers between devices, on_device(): grad = grad + lax.ppermute(grads[step], 'row', peers(n_row, step))  4.45 us
    ppermute x3, waiting for transfers between devices, on_device(): grad = grad + lax.ppermute(grads[step], 'row', peers(n_row, step))  4.15 us
    pallas_call x1, Pallas kernels, on_device(): pl.pallas_call(functools.partial(forward_kernel, n_row, n_col), out_shape...  3.9 us
    ppermute x3, starting transfers between devices, on_device(): value = value + lax.ppermute(values[step], 'col', peers(n_col, 2 * step))  3.52 us
    pallas_call x1, Pallas kernels, on_device(): pl.pallas_call(functools.partial(adjoint_kernel, n_row, n_col), out_shape...  3.14 us
  transfers between devices with their start and end apart: 17, of which 5 were waited for; matrix products, arithmetic and copies ran while one was open for 2% of the time, Pallas kernels for 16%

profile of v1, /device:TPU:0, one launch (start us, length us, event | category | flops | bytes accessed | tf_op | source)
XLA Modules:
  0.0 43.9 jit_solution(17741913381217209825)
XLA Ops:
  0.6 4.1 %collective-permute-start.1 = (bf16[8,4096]{1,0:T(8,128)(2,1)}, bf16[8,4096]{1,0:T(8,128)(2,1)S(1)}, u32[]{:S(2)}, u32[]{:S(2)}) collective-permute-start(bf16[8,4096]{1,0:T(8,128)(2,1)} %refs_0_.2), channel_id=1, source_target_pairs={{0,16},{8,24},{16,0},{24,8},{1,17},{9,25},{17,1},{25,9},{2,18},{10... | collective-permute-start | bytes 196616 | tf_op jit(solution)/shard_map/ppermute | solution.py:167
  4.7 1.6 %collective-permute-start = (bf16[8,4096]{1,0:T(8,128)(2,1)}, bf16[8,4096]{1,0:T(8,128)(2,1)S(1)}, u32[]{:S(2)}, u32[]{:S(2)}) collective-permute-start(bf16[8,4096]{1,0:T(8,128)(2,1)} %refs_0_.2), channel_id=1, source_target_pairs={{0,8},{8,0},{16,24},{24,16},{1,9},{9,1},{17,25},{25,17},{2,10},{10... | collective-permute-start | bytes 196616 | tf_op jit(solution)/shard_map/ppermute | solution.py:167
  6.3 0.0 collective-permute-start.2
  6.3 1.7 %collective-permute-start.10 = (bf16[16,1024]{1,0:T(8,128)(2,1)}, bf16[16,1024]{1,0:T(8,128)(2,1)S(1)}, u32[]{:S(2)}, u32[]{:S(2)}) collective-permute-start(bf16[16,1024]{1,0:T(8,128)(2,1)} %refs_0_.3), channel_id=1, source_target_pairs={{0,4},{1,5},{2,6},{3,7},{4,0},{5,1},{6,2},{7,3},{8,12},{9,13},{10,... | collective-permute-start | bytes 98312 | tf_op jit(solution)/shard_map/ppermute | solution.py:171
  8.1 1.5 %collective-permute-start.8 = (bf16[16,1024]{1,0:T(8,128)(2,1)}, bf16[16,1024]{1,0:T(8,128)(2,1)S(1)}, u32[]{:S(2)}, u32[]{:S(2)}) collective-permute-start(bf16[16,1024]{1,0:T(8,128)(2,1)} %refs_0_.3), channel_id=1, source_target_pairs={{0,2},{1,3},{2,0},{3,1},{4,6},{5,7},{6,4},{7,5},{8,10},{9,11},{10,... | collective-permute-start | bytes 98312 | tf_op jit(solution)/shard_map/ppermute | solution.py:171
  9.5 0.9 %collective-permute-done.10.refs_4_ = bf16[16,1024]{1,0:T(8,128)(2,1)S(1)} collective-permute-done((bf16[16,1024]{1,0:T(8,128)(2,1)}, bf16[16,1024]{1,0:T(8,128)(2,1)S(1)}, u32[]{:S(2)}, u32[]{:S(2)}) %collective-permute-start.10) | collective-permute-done | bytes 32800 | tf_op jit(solution)/shard_map/ppermute | solution.py:171
  10.4 0.0 collective-permute-start.7
  11.1 0.0 collective-permute-done.1.refs_2_
  11.1 2.7 %collective-permute-start.12 = (bf16[16,1024]{1,0:T(8,128)(2,1)}, bf16[16,1024]{1,0:T(8,128)(2,1)S(1)}, u32[]{:S(2)}, u32[]{:S(2)}) collective-permute-start(bf16[16,1024]{1,0:T(8,128)(2,1)} %refs_0_.3), channel_id=1, source_target_pairs={{0,6},{1,7},{2,4},{3,5},{4,2},{5,3},{6,0},{7,1},{8,14},{9,15},{10,... | collective-permute-start | bytes 98312 | tf_op jit(solution)/shard_map/ppermute | solution.py:171
  13.8 0.0 collective-permute-done.refs_1_
  13.8 0.2 collective-permute-start.11
  14.1 0.0 collective-permute-done.2.refs_3_
  14.1 3.4 %copy-done = bf16[1,1,256,128,128]{4,3,2,1,0:T(8,128)(2,1)S(1)} copy-done((bf16[1,1,256,128,128]{4,3,2,1,0:T(8,128)(2,1)S(1)}, bf16[1,1,256,128,128]{4,3,2,1,0:T(8,128)(2,1)}, u32[]{:S(2)}) %copy-start) | copy-done | bytes 8388632
  17.5 0.8 %copy-done.2 = bf16[8,4096]{1,0:T(8,128)(2,1)S(1)} copy-done((bf16[8,4096]{1,0:T(8,128)(2,1)S(1)}, bf16[8,4096]{1,0:T(8,128)(2,1)}, u32[]{:S(2)}) %copy-start.2) | copy-done | bytes 65560
  18.3 0.7 %copy-done.4 = s32[1,1,256]{2,1,0:T(1,128)S(1)} copy-done((s32[1,1,256]{2,1,0:T(1,128)S(1)}, s32[1,1,256]{2,1,0:T(1,128)}, u32[]{:S(2)}) %copy-start.4) | copy-done | bytes 1048
  19.0 0.7 %copy-done.5 = s32[1,1,256]{2,1,0:T(1,128)S(1)} copy-done((s32[1,1,256]{2,1,0:T(1,128)S(1)}, s32[1,1,256]{2,1,0:T(1,128)}, u32[]{:S(2)}) %copy-start.5) | copy-done | bytes 1048
  19.7 0.7 %copy-done.6 = s32[16]{0:T(128)S(1)} copy-done((s32[16]{0:T(128)S(1)}, s32[16]{0:T(128)}, u32[]{:S(2)}) %copy-start.6) | copy-done | bytes 88
  20.3 3.9 %shard_map.86 = (f32[8,16,128]{2,1,0:T(8,128)S(1)}, f32[8,16,128]{2,1,0:T(8,128)S(1)}, f32[8,16,128]{2,1,0:T(8,128)S(1)}, f32[8,16,128]{2,1,0:T(8,128)S(1)}) custom-call(s32[1,1,256]{2,1,0:T(1,128)S(1)} %copy-done.4, s32[1,1,256]{2,1,0:T(1,128)S(1)} %copy-done.5, s32[1,1]{1,0:T(1,128)S(6)} %copy.9.counts, s32[16]{0:T(128)S(1)} %copy-done.6, ...), custom_call_target="tpu_custom_call" | custom-call | tf_op jit(solution)/shard_map/pallas_call | solution.py:191
  24.2 0.1 collective-permute-start.3
  24.3 0.0 collective-permute-done.8.refs_2_
  24.3 0.1 collective-permute-start.4
  24.4 0.0 collective-permute-done.7.refs_1_
  24.4 3.4 %collective-permute-start.5 = (f32[8,16,128]{2,1,0:T(8,128)S(1)}, f32[8,16,128]{2,1,0:T(8,128)S(1)}, u32[]{:S(2)}, u32[]{:S(2)}) collective-permute-start(f32[8,16,128]{2,1,0:T(8,128)S(1)} %get-tuple-element.13), channel_id=1, source_target_pairs={{0,6},{1,7},{2,4},{3,5},{4,2},{5,3},{6,0},{7,1},{8,14},{9,15},{10,... | collective-permute-start | bytes 196616 | tf_op jit(solution)/shard_map/ppermute | solution.py:205
  27.8 0.0 collective-permute-done.12.refs_6_
  27.8 0.0 collective-permute-start.9
  27.8 0.0 collective-permute-done.11.refs_5_
  27.8 0.5 %collective-permute-start.13 = (bf16[16,1024]{1,0:T(8,128)(2,1)S(1)}, bf16[16,1024]{1,0:T(8,128)(2,1)S(1)}, u32[]{:S(2)}, u32[]{:S(2)}) collective-permute-start(bf16[16,1024]{1,0:T(8,128)(2,1)S(1)} %collective-permute-done.12.refs_6_), channel_id=1, source_target_pairs={{0,1},{1,0},{2,3},{3,2},{4,5},{5,4},{6,7},{7,6},{8,9},{9,8},{10,11... | collective-permute-start | bytes 98312 | tf_op jit(solution)/shard_map/ppermute | solution.py:172
  28.3 0.7 %collective-permute-done.9.refs_3_ = bf16[16,1024]{1,0:T(8,128)(2,1)S(1)} collective-permute-done((bf16[16,1024]{1,0:T(8,128)(2,1)S(1)}, bf16[16,1024]{1,0:T(8,128)(2,1)S(1)}, u32[]{:S(2)}, u32[]{:S(2)}) %collective-permute-start.9) | collective-permute-done | bytes 32800 | tf_op jit(solution)/shard_map/ppermute | solution.py:172
  29.0 0.2 collective-permute-done.13.refs_7_
  29.2 0.0 copy-done.1
  29.2 0.0 copy-done.3
  29.2 3.1 %shard_map.88 = (f32[4,4096]{1,0:T(4,128)S(1)}, f32[4,4096]{1,0:T(4,128)S(1)}, f32[4,4096]{1,0:T(4,128)S(1)}, f32[4,4096]{1,0:T(4,128)S(1)}) custom-call(s32[1,1,256]{2,1,0:T(1,128)S(1)} %copy-done.4, s32[1,1,256]{2,1,0:T(1,128)S(1)} %copy-done.5, s32[1,1]{1,0:T(1,128)S(6)} %copy.9.counts, bf16[1,1,256,128,128]{4,3,2,1,0:T(8,128)(2,1)S(1)} %copy-done.1, ...), custom_call_target="tpu_custom_call" | custom-call | tf_op jit(solution)/shard_map/pallas_call | solution.py:175
  32.3 0.1 collective-permute-start.14
  32.4 1.8 %collective-permute-start.15 = (f32[4,4096]{1,0:T(4,128)S(1)}, f32[4,4096]{1,0:T(4,128)S(1)}, u32[]{:S(2)}, u32[]{:S(2)}) collective-permute-start(f32[4,4096]{1,0:T(4,128)S(1)} %get-tuple-element.16), channel_id=1, source_target_pairs={{0,16},{8,24},{16,0},{24,8},{1,17},{9,25},{17,1},{25,9},{2,18},{10... | collective-permute-start | bytes 196616 | tf_op jit(solution)/shard_map/ppermute | solution.py:188
  34.2 0.0 collective-permute-done.3
  34.2 2.5 %collective-permute-start.16 = (f32[4,4096]{1,0:T(4,128)S(1)}, f32[4,4096]{1,0:T(4,128)S(1)}, u32[]{:S(2)}, u32[]{:S(2)}) collective-permute-start(f32[4,4096]{1,0:T(4,128)S(1)} %get-tuple-element.17), channel_id=1, source_target_pairs={{0,24},{8,16},{16,8},{24,0},{1,25},{9,17},{17,9},{25,1},{2,26},{10... | collective-permute-start | bytes 196616 | tf_op jit(solution)/shard_map/ppermute | solution.py:188
  36.8 0.0 collective-permute-done.4
  36.8 0.0 collective-permute-done.5
  36.8 0.0 copy-start.7
  36.8 0.1 collective-permute-start.6
  36.9 0.8 %collective-permute-done.14 = f32[4,4096]{1,0:T(4,128)S(1)} collective-permute-done((f32[4,4096]{1,0:T(4,128)S(1)}, f32[4,4096]{1,0:T(4,128)S(1)}, u32[]{:S(2)}, u32[]{:S(2)}) %collective-permute-start.14) | collective-permute-done | bytes 65568 | tf_op jit(solution)/shard_map/ppermute | solution.py:188
  37.7 3.3 %collective-permute-done.15 = f32[4,4096]{1,0:T(4,128)S(1)} collective-permute-done((f32[4,4096]{1,0:T(4,128)S(1)}, f32[4,4096]{1,0:T(4,128)S(1)}, u32[]{:S(2)}, u32[]{:S(2)}) %collective-permute-start.15) | collective-permute-done | bytes 65568 | tf_op jit(solution)/shard_map/ppermute | solution.py:188
  41.0 0.0 collective-permute-done.16
  41.0 0.7 %add_add_fusion = f32[4,4096]{1,0:T(4,128)} fusion(f32[4,4096]{1,0:T(4,128)S(1)} %collective-permute-done.16, f32[4,4096]{1,0:T(4,128)S(1)} %collective-permute-done.15, f32[4,4096]{1,0:T(4,128)S(1)} %get-tuple-element.14, f32[4,4096]{1,0:T(4,128)S(1)} %collective-permute-done.14), kind=kLoop, calls=%fused_computation | loop fusion | flops 49152 | bytes 327680 | tf_op jit(solution)/shard_map/add | solution.py:188
  41.7 0.0 collective-permute-done.6.other
  41.7 0.0 copy-done.7
  41.7 0.6 %copy-done.8 = f32[8,16,128]{2,1,0:T(8,128)} copy-done((f32[8,16,128]{2,1,0:T(8,128)}, f32[8,16,128]{2,1,0:T(8,128)S(1)}, u32[]{:S(2)}) %copy-start.8) | copy-done | bytes 65560
  42.3 1.5 %shard_map.87 = f32[16,1024]{1,0:T(8,128)} custom-call(f32[8,16,128]{2,1,0:T(8,128)} %copy-done.7, f32[8,16,128]{2,1,0:T(8,128)} %copy-done.8), custom_call_target="tpu_custom_call" | custom-call | tf_op jit(solution)/shard_map/pallas_call | solution.py:207
  (9 shorter events, 0.0 us)
Async XLA Ops:
  0.6 10.5 %collective-permute-start.1 = (bf16[8,4096]{1,0:T(8,128)(2,1)}, bf16[8,4096]{1,0:T(8,128)(2,1)S(1)}, u32[]{:S(2)}, u32[]{:S(2)}) collective-permute-start(bf16[8,4096]{1,0:T(8,128)(2,1)} %refs_0_.2), channel_id=1, source_target_pairs={{0,16},{8,24},{16,0},{24,8},{1,17},{9,25},{17,1},{25,9},{2,18},{10... | collective-permute-start | bytes 196616 | tf_op jit(solution)/shard_map/ppermute | solution.py:167
  4.7 9.1 %collective-permute-start = (bf16[8,4096]{1,0:T(8,128)(2,1)}, bf16[8,4096]{1,0:T(8,128)(2,1)S(1)}, u32[]{:S(2)}, u32[]{:S(2)}) collective-permute-start(bf16[8,4096]{1,0:T(8,128)(2,1)} %refs_0_.2), channel_id=1, source_target_pairs={{0,8},{8,0},{16,24},{24,16},{1,9},{9,1},{17,25},{25,17},{2,10},{10... | collective-permute-start | bytes 196616 | tf_op jit(solution)/shard_map/ppermute | solution.py:167
  6.3 7.8 %collective-permute-start.2 = (bf16[8,4096]{1,0:T(8,128)(2,1)}, bf16[8,4096]{1,0:T(8,128)(2,1)S(1)}, u32[]{:S(2)}, u32[]{:S(2)}) collective-permute-start(bf16[8,4096]{1,0:T(8,128)(2,1)} %refs_0_.2), channel_id=1, source_target_pairs={{0,24},{8,16},{16,8},{24,0},{1,25},{9,17},{17,9},{25,1},{2,26},{10... | collective-permute-start | bytes 196616 | tf_op jit(solution)/shard_map/ppermute | solution.py:167
  6.3 4.1 %collective-permute-start.10 = (bf16[16,1024]{1,0:T(8,128)(2,1)}, bf16[16,1024]{1,0:T(8,128)(2,1)S(1)}, u32[]{:S(2)}, u32[]{:S(2)}) collective-permute-start(bf16[16,1024]{1,0:T(8,128)(2,1)} %refs_0_.3), channel_id=1, source_target_pairs={{0,4},{1,5},{2,6},{3,7},{4,0},{5,1},{6,2},{7,3},{8,12},{9,13},{10,... | collective-permute-start | bytes 98312 | tf_op jit(solution)/shard_map/ppermute | solution.py:171
  8.1 16.2 %collective-permute-start.8 = (bf16[16,1024]{1,0:T(8,128)(2,1)}, bf16[16,1024]{1,0:T(8,128)(2,1)S(1)}, u32[]{:S(2)}, u32[]{:S(2)}) collective-permute-start(bf16[16,1024]{1,0:T(8,128)(2,1)} %refs_0_.3), channel_id=1, source_target_pairs={{0,2},{1,3},{2,0},{3,1},{4,6},{5,7},{6,4},{7,5},{8,10},{9,11},{10,... | collective-permute-start | bytes 98312 | tf_op jit(solution)/shard_map/ppermute | solution.py:171
  10.4 14.0 %collective-permute-start.7 = (bf16[16,1024]{1,0:T(8,128)(2,1)}, bf16[16,1024]{1,0:T(8,128)(2,1)S(1)}, u32[]{:S(2)}, u32[]{:S(2)}) collective-permute-start(bf16[16,1024]{1,0:T(8,128)(2,1)} %refs_0_.3), channel_id=1, source_target_pairs={{0,1},{1,0},{2,3},{3,2},{4,5},{5,4},{6,7},{7,6},{8,9},{9,8},{10,11... | collective-permute-start | bytes 98312 | tf_op jit(solution)/shard_map/ppermute | solution.py:172
  11.1 16.7 %collective-permute-start.12 = (bf16[16,1024]{1,0:T(8,128)(2,1)}, bf16[16,1024]{1,0:T(8,128)(2,1)S(1)}, u32[]{:S(2)}, u32[]{:S(2)}) collective-permute-start(bf16[16,1024]{1,0:T(8,128)(2,1)} %refs_0_.3), channel_id=1, source_target_pairs={{0,6},{1,7},{2,4},{3,5},{4,2},{5,3},{6,0},{7,1},{8,14},{9,15},{10,... | collective-permute-start | bytes 98312 | tf_op jit(solution)/shard_map/ppermute | solution.py:171
  13.8 13.9 %collective-permute-start.11 = (bf16[16,1024]{1,0:T(8,128)(2,1)S(1)}, bf16[16,1024]{1,0:T(8,128)(2,1)S(1)}, u32[]{:S(2)}, u32[]{:S(2)}) collective-permute-start(bf16[16,1024]{1,0:T(8,128)(2,1)S(1)} %collective-permute-done.10.refs_4_), channel_id=1, source_target_pairs={{0,1},{1,0},{2,3},{3,2},{4,5},{5,4},{6,7},{7,6},{8,9},{9,8},{10,11... | collective-permute-start | bytes 98312 | tf_op jit(solution)/shard_map/ppermute | solution.py:172
  14.1 3.4 %copy-start = (bf16[1,1,256,128,128]{4,3,2,1,0:T(8,128)(2,1)S(1)}, bf16[1,1,256,128,128]{4,3,2,1,0:T(8,128)(2,1)}, u32[]{:S(2)}) copy-start(bf16[1,1,256,128,128]{4,3,2,1,0:T(8,128)(2,1)} %blocks.3) | copy-start | bytes 25165828
  17.5 0.8 %copy-start.2 = (bf16[8,4096]{1,0:T(8,128)(2,1)S(1)}, bf16[8,4096]{1,0:T(8,128)(2,1)}, u32[]{:S(2)}) copy-start(bf16[8,4096]{1,0:T(8,128)(2,1)} %refs_0_.2) | copy-start | bytes 196612
  18.3 0.7 %copy-start.4 = (s32[1,1,256]{2,1,0:T(1,128)S(1)}, s32[1,1,256]{2,1,0:T(1,128)}, u32[]{:S(2)}) copy-start(s32[1,1,256]{2,1,0:T(1,128)} %slot_rows.3) | copy-start | bytes 3076
  19.0 0.7 %copy-start.5 = (s32[1,1,256]{2,1,0:T(1,128)S(1)}, s32[1,1,256]{2,1,0:T(1,128)}, u32[]{:S(2)}) copy-start(s32[1,1,256]{2,1,0:T(1,128)} %slot_cols.3) | copy-start | bytes 3076
  19.7 0.7 %copy-start.6 = (s32[16]{0:T(128)S(1)}, s32[16]{0:T(128)}, u32[]{:S(2)}) copy-start(s32[16]{0:T(128)} %reward_cols.1) | copy-start | bytes 196
  20.3 8.9 %copy-start.1 = (bf16[1,1,256,128,128]{4,3,2,1,0:T(8,128)(2,1)S(1)}, bf16[1,1,256,128,128]{4,3,2,1,0:T(8,128)(2,1)}, u32[]{:S(2)}) copy-start(bf16[1,1,256,128,128]{4,3,2,1,0:T(8,128)(2,1)} %blocks.3) | copy-start | bytes 25165828
  20.3 8.9 %copy-start.3 = (bf16[16,1024]{1,0:T(8,128)(2,1)S(1)}, bf16[16,1024]{1,0:T(8,128)(2,1)}, u32[]{:S(2)}) copy-start(bf16[16,1024]{1,0:T(8,128)(2,1)} %refs_0_.3) | copy-start | bytes 98308
  24.2 10.0 %collective-permute-start.3 = (f32[8,16,128]{2,1,0:T(8,128)S(1)}, f32[8,16,128]{2,1,0:T(8,128)S(1)}, u32[]{:S(2)}, u32[]{:S(2)}) collective-permute-start(f32[8,16,128]{2,1,0:T(8,128)S(1)} %get-tuple-element.11), channel_id=1, source_target_pairs={{0,2},{1,3},{2,0},{3,1},{4,6},{5,7},{6,4},{7,5},{8,10},{9,11},{10,... | collective-permute-start | bytes 196616 | tf_op jit(solution)/shard_map/ppermute | solution.py:205
  24.3 12.5 %collective-permute-start.4 = (f32[8,16,128]{2,1,0:T(8,128)S(1)}, f32[8,16,128]{2,1,0:T(8,128)S(1)}, u32[]{:S(2)}, u32[]{:S(2)}) collective-permute-start(f32[8,16,128]{2,1,0:T(8,128)S(1)} %get-tuple-element.12), channel_id=1, source_target_pairs={{0,4},{1,5},{2,6},{3,7},{4,0},{5,1},{6,2},{7,3},{8,12},{9,13},{10,... | collective-permute-start | bytes 196616 | tf_op jit(solution)/shard_map/ppermute | solution.py:205
  24.4 12.4 %collective-permute-start.5 = (f32[8,16,128]{2,1,0:T(8,128)S(1)}, f32[8,16,128]{2,1,0:T(8,128)S(1)}, u32[]{:S(2)}, u32[]{:S(2)}) collective-permute-start(f32[8,16,128]{2,1,0:T(8,128)S(1)} %get-tuple-element.13), channel_id=1, source_target_pairs={{0,6},{1,7},{2,4},{3,5},{4,2},{5,3},{6,0},{7,1},{8,14},{9,15},{10,... | collective-permute-start | bytes 196616 | tf_op jit(solution)/shard_map/ppermute | solution.py:205
  27.8 1.2 %collective-permute-start.9 = (bf16[16,1024]{1,0:T(8,128)(2,1)S(1)}, bf16[16,1024]{1,0:T(8,128)(2,1)S(1)}, u32[]{:S(2)}, u32[]{:S(2)}) collective-permute-start(bf16[16,1024]{1,0:T(8,128)(2,1)S(1)} %collective-permute-done.8.refs_2_), channel_id=1, source_target_pairs={{0,1},{1,0},{2,3},{3,2},{4,5},{5,4},{6,7},{7,6},{8,9},{9,8},{10,11... | collective-permute-start | bytes 98312 | tf_op jit(solution)/shard_map/ppermute | solution.py:172
  27.8 1.4 %collective-permute-start.13 = (bf16[16,1024]{1,0:T(8,128)(2,1)S(1)}, bf16[16,1024]{1,0:T(8,128)(2,1)S(1)}, u32[]{:S(2)}, u32[]{:S(2)}) collective-permute-start(bf16[16,1024]{1,0:T(8,128)(2,1)S(1)} %collective-permute-done.12.refs_6_), channel_id=1, source_target_pairs={{0,1},{1,0},{2,3},{3,2},{4,5},{5,4},{6,7},{7,6},{8,9},{9,8},{10,11... | collective-permute-start | bytes 98312 | tf_op jit(solution)/shard_map/ppermute | solution.py:172
  32.3 5.4 %collective-permute-start.14 = (f32[4,4096]{1,0:T(4,128)S(1)}, f32[4,4096]{1,0:T(4,128)S(1)}, u32[]{:S(2)}, u32[]{:S(2)}) collective-permute-start(f32[4,4096]{1,0:T(4,128)S(1)} %get-tuple-element.15), channel_id=1, source_target_pairs={{0,8},{8,0},{16,24},{24,16},{1,9},{9,1},{17,25},{25,17},{2,10},{10... | collective-permute-start | bytes 196616 | tf_op jit(solution)/shard_map/ppermute | solution.py:188
  32.4 8.6 %collective-permute-start.15 = (f32[4,4096]{1,0:T(4,128)S(1)}, f32[4,4096]{1,0:T(4,128)S(1)}, u32[]{:S(2)}, u32[]{:S(2)}) collective-permute-start(f32[4,4096]{1,0:T(4,128)S(1)} %get-tuple-element.16), channel_id=1, source_target_pairs={{0,16},{8,24},{16,0},{24,8},{1,17},{9,25},{17,1},{25,9},{2,18},{10... | collective-permute-start | bytes 196616 | tf_op jit(solution)/shard_map/ppermute | solution.py:188
  34.2 6.8 %collective-permute-start.16 = (f32[4,4096]{1,0:T(4,128)S(1)}, f32[4,4096]{1,0:T(4,128)S(1)}, u32[]{:S(2)}, u32[]{:S(2)}) collective-permute-start(f32[4,4096]{1,0:T(4,128)S(1)} %get-tuple-element.17), channel_id=1, source_target_pairs={{0,24},{8,16},{16,8},{24,0},{1,25},{9,17},{17,9},{25,1},{2,26},{10... | collective-permute-start | bytes 196616 | tf_op jit(solution)/shard_map/ppermute | solution.py:188
  36.8 4.9 %copy-start.7 = (f32[8,16,128]{2,1,0:T(8,128)}, f32[8,16,128]{2,1,0:T(8,128)S(1)}, u32[]{:S(2)}) copy-start(f32[8,16,128]{2,1,0:T(8,128)S(1)} %add_add_fusion.1.own) | copy-start | bytes 196612
  36.8 4.9 %collective-permute-start.6 = (f32[8,16,128]{2,1,0:T(8,128)S(1)}, f32[8,16,128]{2,1,0:T(8,128)S(1)}, u32[]{:S(2)}, u32[]{:S(2)}) collective-permute-start(f32[8,16,128]{2,1,0:T(8,128)S(1)} %add_add_fusion.1.own), channel_id=1, source_target_pairs={{0,1},{1,0},{2,3},{3,2},{4,5},{5,4},{6,7},{7,6},{8,9},{9,8},{10,11... | collective-permute-start | bytes 196616 | tf_op jit(solution)/shard_map/ppermute | solution.py:206
  41.7 0.6 %copy-start.8 = (f32[8,16,128]{2,1,0:T(8,128)}, f32[8,16,128]{2,1,0:T(8,128)S(1)}, u32[]{:S(2)}) copy-start(f32[8,16,128]{2,1,0:T(8,128)S(1)} %collective-permute-done.6.other) | copy-start | bytes 196612

commit v2 on v0

v2 whole, which is shorter than its diff:
```python
import functools

import jax
import jax.numpy as jnp
from jax import lax
from jax.experimental import pallas as pl
from jax.experimental.pallas import tpu as pltpu
from jax.sharding import PartitionSpec as P

BLK = 128
REWARDS = 16
CHUNK = 64
SUMS = 4
VMEM_LIMIT = 40 * 2**20


def peers(size, step):
    return [(here, here ^ step) for here in range(size)]


def crossings(n_row, n_col, step):
    pairs = []
    for row in range(n_row):
        for chip in range(n_col // 2):
            if step < n_col // 2:
                pairs.append((row * n_col + 2 * chip, row * n_col + 2 * (chip ^ step)))
            if step < n_row:
                pairs.append((row * n_col + 2 * chip + 1, (row ^ step) * n_col + 2 * chip + 1))
    return pairs


def by_core(here, there):
    first = lax.axis_index("col") % 2 == 0
    return jnp.where(first, here, there), jnp.where(first, there, here)


def lay(table, width):
    pieces = table.shape[1] // width
    return jnp.concatenate([table[:, at * width : (at + 1) * width] for at in range(pieces)], axis=0)


def gather_kernel(shard_there, table_there, other_shard, other_table, out, shard, table, sems):
    copies = [
        pltpu.make_async_copy(shard_there, shard, sems.at[0]),
        pltpu.make_async_copy(table_there, table, sems.at[1]),
    ]
    for copy in copies:
        copy.start()
    for copy in copies:
        copy.wait()
    core, span, width = lax.axis_index("col") % 2, shard.shape[1], out.shape[1]

    @pl.when(core == 0)
    def _():
        out[:, :span] = shard[...]
        out[:, span : 2 * span] = other_shard[...]

    @pl.when(core == 1)
    def _():
        lines = [lay(part[...].astype(jnp.float32), width) for part in (other_table, table)]
        out[...] = jnp.concatenate(lines, axis=0).astype(out.dtype)


def spread(first, second):
    empty = jnp.zeros((2 * REWARDS, BLK), jnp.bfloat16)
    top = jnp.concatenate([jnp.concatenate(first, axis=0), empty], axis=1)
    bottom = jnp.concatenate([empty, jnp.concatenate(second, axis=0)], axis=1)
    return jnp.concatenate([top, bottom], axis=0)


def products_kernel(n_row, n_col, *refs):
    n_chip = n_col // 2
    steps = max(n_row, n_chip)
    counts, slot_rows_there, slot_cols_there, reward_cols_there, blocks_there = refs[:5]
    mine, others = refs[5 : 5 + steps], refs[5 + steps : 5 + 2 * steps]
    keeps, gives = refs[5 + 2 * steps : 5 + 3 * steps], refs[5 + 3 * steps : 5 + 4 * steps]
    refs = refs[5 + 4 * steps :]
    slot_rows, slot_cols, reward_cols, blocks, table, weights, rewards = refs[:7]
    value_sums, grad_sums = refs[7 : 7 + SUMS], refs[7 + SUMS : 7 + 2 * SUMS]
    sems, block_sems = refs[7 + 2 * SUMS :]
    own_row, own_col = lax.axis_index("row"), lax.axis_index("col")
    own_chip, core = own_col // 2, own_col % 2
    row_cells, col_cells = weights.shape[0] - 1, rewards.shape[0] - 1

    pairs = ((slot_rows_there, slot_rows), (slot_cols_there, slot_cols), (reward_cols_there, reward_cols))
    copies = [pltpu.make_async_copy(there, here, sems.at[at]) for at, (there, here) in enumerate(pairs)]
    for copy in copies:
        copy.start()

    def block_copy(chunk):
        part = pl.ds(pl.multiple_of(chunk * CHUNK, CHUNK), CHUNK)
        return pltpu.make_async_copy(blocks_there.at[:, :, part], blocks.at[:, :, part], block_sems.at[chunk])

    chunk_count = blocks.shape[2] // CHUNK
    for chunk in range(chunk_count):
        block_copy(chunk).start()
    for sums in (*value_sums, *grad_sums):
        sums[...] = jnp.zeros_like(sums)
    weights[row_cells] = jnp.zeros((REWARDS, BLK), jnp.bfloat16)
    rewards[col_cells] = jnp.zeros((REWARDS, BLK), jnp.bfloat16)

    owned = row_cells // n_col
    group = table.shape[0] // n_row
    pieces = REWARDS // 2 // group
    width = col_cells * BLK // pieces

    def take(shards, tables, my_half):
        for step in range(n_chip):
            for half in range(2):
                first = (2 * (own_chip ^ step) + half) * owned
                for at in range(owned):
                    lane = (half * 2 * owned + 2 * at + my_half) * BLK
                    weights[first + at] = shards[step][:, lane : lane + BLK]
        for step in range(n_row):
            for at in range(pieces):
                part = tables[step][...].astype(jnp.float32)
                line = my_half * (REWARDS // 2) + at * group
                table[step * group : (step + 1) * group, at * width : (at + 1) * width] = part[line : line + group]

    @pl.when(core == 0)
    def _():
        take(mine, others, 0)

    @pl.when(core == 1)
    def _():
        take(others, mine, 1)

    for copy in copies:
        copy.wait()
    candidates = group * n_row
    lane = lax.broadcasted_iota(jnp.int32, (REWARDS, candidates), 1)
    column = lane % group + (own_row ^ (lane // group)) * group
    line = lax.broadcasted_iota(jnp.int32, (REWARDS, candidates), 0)
    wanted = jnp.zeros((REWARDS, candidates), jnp.int32)
    for k in range(REWARDS):
        wanted = jnp.where(line == k, reward_cols[k], wanted)
    pick = (column == wanted).astype(jnp.float32).astype(jnp.bfloat16)
    for col in range(col_cells):
        rewards[col] = jnp.dot(
            pick,
            table[:, col * BLK : (col + 1) * BLK].astype(jnp.bfloat16),
            preferred_element_type=jnp.float32,
        ).astype(jnp.bfloat16)

    live_count = counts[0, 0]

    def visit(chunk, carry):
        block_copy(chunk).wait()
        found = []
        for quad in range(CHUNK // 4):
            start = chunk * CHUNK + quad * 4
            rows, cols = [], []
            for at in range(4):
                live = start + at < live_count
                rows.append(jnp.where(live, slot_rows[0, 0, start + at] // 2, row_cells))
                cols.append(jnp.where(live, slot_cols[0, 0, start + at], col_cells))
            stored = [blocks[0, 0, start + at] for at in range(4)]
            tile = jnp.concatenate(
                [jnp.concatenate(stored[:2], axis=0), jnp.concatenate(stored[2:], axis=0)], axis=1
            )
            factor = [weights[row] for row in rows]
            product = lax.dot_general(
                spread((factor[0], factor[2]), (factor[1], factor[3])),
                tile,
                (((1,), (0,)), ((), ())),
                preferred_element_type=jnp.float32,
            )
            for piece, (at, side) in enumerate(((0, 0), (2, 1), (1, 0), (3, 1))):
                part = product[piece * REWARDS : (piece + 1) * REWARDS, side * BLK : (side + 1) * BLK]
                found.append((grad_sums[at % SUMS], cols[at], part))
            factor = [rewards[col] for col in cols]
            product = lax.dot_general(
                spread((factor[0], factor[1]), (factor[2], factor[3])),
                tile,
                (((1,), (1,)), ((), ())),
                preferred_element_type=jnp.float32,
            )
            for piece, (at, side) in enumerate(((0, 0), (1, 1), (2, 0), (3, 1))):
                part = product[piece * REWARDS : (piece + 1) * REWARDS, side * BLK : (side + 1) * BLK]
                found.append((value_sums[at % SUMS], rows[at], part))
        for sums, cell, part in found:
            sums[cell] += part
        return carry

    live_chunks = (live_count + CHUNK - 1) // CHUNK
    lax.fori_loop(0, live_chunks, visit, 0)
    lax.fori_loop(live_chunks, chunk_count, lambda chunk, carry: (block_copy(chunk).wait(), carry)[1], 0)

    lines = REWARDS // n_row
    part = row_cells // n_chip

    def put_grad(step, out):
        for col in range(col_cells):
            here = pl.ds((own_row ^ step) * lines, lines)
            at, line = divmod(col * lines, REWARDS)
            out[at, line : line + lines, :] = sum(sums[col, here, :] for sums in grad_sums)

    def put_value(step, out):
        cells = pl.ds((own_chip ^ step) * part, part)
        out[:part] = sum(sums[cells] for sums in value_sums)

    def put(values, grads):
        for step in range(steps):
            if step < n_chip:
                put_value(step, values[step])
            if step < n_row:
                put_grad(step, grads[step])

    @pl.when(core == 0)
    def _():
        put(keeps, gives)

    @pl.when(core == 1)
    def _():
        put(gives, keeps)


def pair_kernel(*refs):
    count = len(refs) // 3
    for keep, got, out in zip(refs[:count], refs[count : 2 * count], refs[2 * count :]):
        half = keep.shape[0]
        out[:half], out[half:] = by_core(keep[...], got[...])


def total_kernel(n_row, n_chip, *refs):
    parts, (keep, give) = refs[:-2], refs[-2:]
    core = lax.axis_index("col") % 2
    half = keep.shape[0]

    @pl.when(core == 0)
    def _():
        total = sum(part[...] for part in parts[:n_chip])
        cut = half // 2
        keep[:cut], keep[cut:] = total[:cut], total[half : half + cut]
        give[:cut], give[cut:] = total[cut:half], total[half + cut :]

    @pl.when(core == 1)
    def _():
        total = sum(part[...] for part in parts[:n_row])
        give[...], keep[...] = total[:half], total[half:]


def result_kernel(keep, got, value, grad):
    core = lax.axis_index("col") % 2
    lines = grad.shape[0]

    def write(values, grads):
        owned = value.shape[1] // BLK // 2
        for at in range(owned):
            for parity in range(2):
                cell = 2 * at + parity
                value[:, cell * BLK : (cell + 1) * BLK] = values[parity * owned + at]
        for col in range(grad.shape[1] // BLK):
            at, line = divmod(col * lines, REWARDS)
            grad[:, col * BLK : (col + 1) * BLK] = grads[at, line : line + lines, :]

    @pl.when(core == 0)
    def _():
        write(keep, got)

    @pl.when(core == 1)
    def _():
        write(got, keep)


def on_device(n_row, n_col, blocks, slot_rows, slot_cols, counts, reward_table, reward_cols, cotangent):
    n_chip = n_col // 2
    row_cells = n_col * (cotangent.shape[1] // BLK) // 2
    col_cells = reward_table.shape[1] // BLK
    smem = pl.BlockSpec(memory_space=pltpu.SMEM)
    hbm = pl.BlockSpec(memory_space=pltpu.HBM)
    vmem = pl.BlockSpec(memory_space=pltpu.VMEM)
    in_hbm = functools.partial(pltpu.with_memory_space_constraint, memory_space=pltpu.HBM)

    steps = max(n_row, n_chip)
    small = pltpu.CompilerParams(vmem_limit_bytes=8 * 2**20)

    def swap(part):
        return lax.ppermute(part, "col", peers(n_col, 1))

    def cross(part, step):
        return lax.ppermute(part, ("row", "col"), crossings(n_row, n_col, step))

    width = 2 * reward_table.shape[0] * reward_table.shape[1] // REWARDS
    chip_inputs = pl.pallas_call(
        gather_kernel,
        out_shape=jax.ShapeDtypeStruct((REWARDS, width), cotangent.dtype),
        in_specs=[hbm] * 2 + [vmem] * 2,
        out_specs=vmem,
        scratch_shapes=[
            pltpu.VMEM(cotangent.shape, cotangent.dtype),
            pltpu.VMEM(reward_table.shape, reward_table.dtype),
            pltpu.SemaphoreType.DMA((2,)),
        ],
        compiler_params=small,
    )(in_hbm(cotangent), in_hbm(reward_table), swap(cotangent), swap(reward_table))
    mine = [chip_inputs] + [cross(chip_inputs, step) for step in range(1, steps)]
    others = [swap(part) for part in mine]

    lines, part = REWARDS // n_row, row_cells // n_chip
    tiles = jax.ShapeDtypeStruct((max(part, col_cells * lines // REWARDS), REWARDS, BLK), jnp.float32)
    both = jax.ShapeDtypeStruct((2 * tiles.shape[0], REWARDS, BLK), jnp.float32)
    sums = pl.pallas_call(
        functools.partial(products_kernel, n_row, n_col),
        out_shape=[tiles] * (2 * steps),
        in_specs=[smem] + [hbm] * 4 + [vmem] * (2 * steps),
        out_specs=[vmem] * (2 * steps),
        scratch_shapes=[
            pltpu.SMEM(slot_rows.shape, jnp.int32),
            pltpu.SMEM(slot_cols.shape, jnp.int32),
            pltpu.SMEM(reward_cols.shape, jnp.int32),
            pltpu.VMEM(blocks.shape, blocks.dtype),
            pltpu.VMEM((reward_table.shape[0] * n_row, col_cells * BLK), jnp.float32),
            pltpu.VMEM((row_cells + 1, REWARDS, BLK), jnp.bfloat16),
            pltpu.VMEM((col_cells + 1, REWARDS, BLK), jnp.bfloat16),
            *[pltpu.VMEM((row_cells + 1, REWARDS, BLK), jnp.float32)] * SUMS,
            *[pltpu.VMEM((col_cells + 1, REWARDS, BLK), jnp.float32)] * SUMS,
            pltpu.SemaphoreType.DMA((3,)),
            pltpu.SemaphoreType.DMA((blocks.shape[2] // CHUNK,)),
        ],
        compiler_params=pltpu.CompilerParams(vmem_limit_bytes=VMEM_LIMIT),
        cost_estimate=pl.CostEstimate(
            flops=4 * REWARDS * blocks.size, bytes_accessed=4 * blocks.size, transcendentals=0
        ),
    )(counts, *map(in_hbm, (slot_rows, slot_cols, reward_cols, blocks)), *mine, *others)
    keeps, gives = sums[:steps], sums[steps:]
    pairs = pl.pallas_call(
        pair_kernel,
        out_shape=[both] * steps,
        in_specs=[vmem] * (2 * steps),
        out_specs=[vmem] * steps,
        compiler_params=small,
    )(*keeps, *[swap(give) for give in gives])
    parts = [pairs[0]] + [cross(pairs[step], step) for step in range(1, steps)]
    keep, give = pl.pallas_call(
        functools.partial(total_kernel, n_row, n_chip),
        out_shape=[tiles] * 2,
        in_specs=[vmem] * steps,
        out_specs=[vmem] * 2,
        compiler_params=small,
    )(*parts)
    return pl.pallas_call(
        result_kernel,
        out_shape=[
            jax.ShapeDtypeStruct((REWARDS, part * BLK), jnp.float32),
            jax.ShapeDtypeStruct((lines, col_cells * BLK), jnp.float32),
        ],
        in_specs=[vmem] * 2,
        out_specs=[vmem] * 2,
        compiler_params=small,
    )(keep, swap(give))


def solution(mesh):
    placed = (
        P("row", "col", None, None, None),
        P("row", "col", None),
        P("row", "col", None),
        P("row", "col"),
        P("row", "col"),
        P(),
        P(None, ("row", "col")),
    )
    return jax.shard_map(
        functools.partial(on_device, mesh.shape["row"], mesh.shape["col"]),
        mesh=mesh,
        in_specs=placed,
        out_specs=(P(None, ("row", "col")), P("row", "col")),
        check_vma=False,
    )
```

time: 181 us -> 35.2 us (0.19)
  other arithmetic: 62.2 us -> 0 us
  matrix products: 28.7 us -> 0 us
  blocking collectives: 25.4 us -> 0 us
  waiting for transfers between devices: 32.1 us -> 12.7 us
  between operations: 16.9 us -> 1.35 us
  starting transfers between devices: 0.08 us -> 15.1 us
  local copies, waits for them, and re-layouts: 13.9 us -> 0 us
  Pallas kernels: 0 us -> 5.96 us
    reduce_scatter x1 -> x0, waiting for transfers between devices: 32.1 us -> none  [on_device(): lax.psum_scatter(value_acc.reshape(REWARDS, sb_row * BLK), 'col', scatter...]
    dot_general x16 -> x0, matrix products: 28.7 us -> none  [the longest x8 15.4 us: visit(): jnp.einsum('kgc,grc->kgr', picked, block_set, preferred_element_type=jnp....]
    scatter-add x16 -> x0, other arithmetic: 27.3 us -> none  [the longest x8 13.7 us: visit(): grad_now = grad_now.at[:, col_set].add(product * live_mask)]
    all_gather x2 -> x0, blocking collectives: 25.4 us -> none  [the longest x1 14.4 us: on_device(): reward_full = lax.all_gather(reward_table, 'row', axis=0, tiled=True)]
    and x17 -> x0, other arithmetic: 22.5 us -> none  [the longest x8 11.3 us: visit(): picked = jnp.take(reward_cells, col_set, axis=1)]
    ppermute x0 -> x17, starting transfers between devices: none -> 15.1 us  [the longest x6 9.68 us: cross(): return lax.ppermute(part, ('row', 'col'), crossings(n_row, n_col, step))]
    ppermute x0 -> x17, waiting for transfers between devices: none -> 12.7 us  [the longest x6 8.5 us: cross(): return lax.ppermute(part, ('row', 'col'), crossings(n_row, n_col, step))]
    select_n x18 -> x0, other arithmetic: 12.4 us -> none  [the longest x8 6.15 us: visit(): value_now = value_now.at[:, row_set].add(product * live_mask)]
  transfers between devices with their start and end apart: 2 -> 17, of which waited for: 1 -> 13; matrix products, arithmetic and copies ran while one was open for 30% -> 0% of each run, Pallas kernels for 0% -> 0%
where the time goes in v2:
time: 35.2 us; the launch traced here: 35.1 us
  starting transfers between devices  15.1 us (43%)
  waiting for transfers between devices  12.7 us (36%)
  Pallas kernels  5.96 us (17%)
  between operations  1.35 us (4%)
    ppermute x6, starting transfers between devices, cross(): return lax.ppermute(part, ('row', 'col'), crossings(n_row, n_col, step))  9.68 us
    ppermute x6, waiting for transfers between devices, cross(): return lax.ppermute(part, ('row', 'col'), crossings(n_row, n_col, step))  8.5 us
    ppermute x11, starting transfers between devices, swap(): return lax.ppermute(part, 'col', peers(n_col, 1))  5.42 us
    pallas_call x1, Pallas kernels, on_device(): pl.pallas_call(functools.partial(products_kernel, n_row, n_col), out_shap...  4.34 us
    ppermute x11, waiting for transfers between devices, swap(): return lax.ppermute(part, 'col', peers(n_col, 1))  4.16 us
    pallas_call x1, Pallas kernels, on_device(): pl.pallas_call(gather_kernel, out_shape=jax.ShapeDtypeStruct((REWARDS, wi...  0.88 us
  transfers between devices with their start and end apart: 17, of which 13 were waited for; matrix products, arithmetic and copies ran while one was open for 0% of the time, Pallas kernels for 0%

profile of v2, /device:TPU:0, one launch (start us, length us, event | category | flops | bytes accessed | tf_op | source)
XLA Modules:
  0.0 35.1 jit_solution(16621391296544276199)
XLA Ops:
  0.6 0.5 %collective-permute-start.1 = (bf16[8,4096]{1,0:T(8,128)(2,1)}, bf16[8,4096]{1,0:T(8,128)(2,1)S(1)}, u32[]{:S(2)}, u32[]{:S(2)}) collective-permute-start(bf16[8,4096]{1,0:T(8,128)(2,1)} %table_there.1), channel_id=1, source_target_pairs={{0,1},{1,0},{2,3},{3,2},{4,5},{5,4},{6,7},{7,6},{8,9},{9,8},{10,11... | collective-permute-start | bytes 196616 | tf_op jit(solution)/shard_map/ppermute | solution.py:279
  1.1 0.1 collective-permute-start
  1.2 1.3 %collective-permute-done.other_shard = bf16[16,1024]{1,0:T(8,128)(2,1)S(1)} collective-permute-done((bf16[16,1024]{1,0:T(8,128)(2,1)}, bf16[16,1024]{1,0:T(8,128)(2,1)S(1)}, u32[]{:S(2)}, u32[]{:S(2)}) %collective-permute-start) | collective-permute-done | bytes 32800 | tf_op jit(solution)/shard_map/ppermute | solution.py:279
  2.6 0.0 collective-permute-done.1.other_table
  2.6 0.9 %shard_map.86.refs_5_ = bf16[16,4096]{1,0:T(8,128)(2,1)S(1)} custom-call(bf16[16,1024]{1,0:T(8,128)(2,1)} %shard_there.1, bf16[8,4096]{1,0:T(8,128)(2,1)} %table_there.1, bf16[16,1024]{1,0:T(8,128)(2,1)S(1)} %collective-permute-done.other_shard, bf16[8,4096]{1,0:T(8,128)(2,1)S(1)} %collective-permute-done.1.other_table), custom_call_target="tpu_custom_call" | custom-call | tf_op jit(solution)/shard_map/pallas_call | solution.py:285
  3.5 3.7 %collective-permute-start.4 = (bf16[16,4096]{1,0:T(8,128)(2,1)S(1)}, bf16[16,4096]{1,0:T(8,128)(2,1)S(1)}, u32[]{:S(2)}, u32[]{:S(2)}) collective-permute-start(bf16[16,4096]{1,0:T(8,128)(2,1)S(1)} %shard_map.86.refs_5_), channel_id=1, source_target_pairs={{0,6},{1,25},{2,4},{3,27},{4,2},{5,29},{6,0},{7,31},{8,14},{9,17},... | collective-permute-start | bytes 393224 | tf_op jit(solution)/shard_map/ppermute | solution.py:282
  7.1 0.5 %collective-permute-start.3 = (bf16[16,4096]{1,0:T(8,128)(2,1)S(1)}, bf16[16,4096]{1,0:T(8,128)(2,1)S(1)}, u32[]{:S(2)}, u32[]{:S(2)}) collective-permute-start(bf16[16,4096]{1,0:T(8,128)(2,1)S(1)} %shard_map.86.refs_5_), channel_id=1, source_target_pairs={{0,4},{1,17},{2,6},{3,19},{4,0},{5,21},{6,2},{7,23},{8,12},{9,25},... | collective-permute-start | bytes 393224 | tf_op jit(solution)/shard_map/ppermute | solution.py:282
  7.6 0.1 collective-permute-start.2
  7.8 0.9 %collective-permute-start.5 = (bf16[16,4096]{1,0:T(8,128)(2,1)S(1)}, bf16[16,4096]{1,0:T(8,128)(2,1)S(1)}, u32[]{:S(2)}, u32[]{:S(2)}) collective-permute-start(bf16[16,4096]{1,0:T(8,128)(2,1)S(1)} %shard_map.86.refs_5_), channel_id=1, source_target_pairs={{0,1},{1,0},{2,3},{3,2},{4,5},{5,4},{6,7},{7,6},{8,9},{9,8},{10,11... | collective-permute-start | bytes 393224 | tf_op jit(solution)/shard_map/ppermute | solution.py:279
  8.7 1.4 %collective-permute-done.4.refs_8_ = bf16[16,4096]{1,0:T(8,128)(2,1)S(1)} collective-permute-done((bf16[16,4096]{1,0:T(8,128)(2,1)S(1)}, bf16[16,4096]{1,0:T(8,128)(2,1)S(1)}, u32[]{:S(2)}, u32[]{:S(2)}) %collective-permute-start.4) | collective-permute-done | bytes 131104 | tf_op jit(solution)/shard_map/ppermute | solution.py:282
  10.1 0.7 %collective-permute-start.8 = (bf16[16,4096]{1,0:T(8,128)(2,1)S(1)}, bf16[16,4096]{1,0:T(8,128)(2,1)S(1)}, u32[]{:S(2)}, u32[]{:S(2)}) collective-permute-start(bf16[16,4096]{1,0:T(8,128)(2,1)S(1)} %collective-permute-done.4.refs_8_), channel_id=1, source_target_pairs={{0,1},{1,0},{2,3},{3,2},{4,5},{5,4},{6,7},{7,6},{8,9},{9,8},{10,11... | collective-permute-start | bytes 393224 | tf_op jit(solution)/shard_map/ppermute | solution.py:279
  10.8 1.3 %collective-permute-done.3.refs_7_ = bf16[16,4096]{1,0:T(8,128)(2,1)S(1)} collective-permute-done((bf16[16,4096]{1,0:T(8,128)(2,1)S(1)}, bf16[16,4096]{1,0:T(8,128)(2,1)S(1)}, u32[]{:S(2)}, u32[]{:S(2)}) %collective-permute-start.3) | collective-permute-done | bytes 131104 | tf_op jit(solution)/shard_map/ppermute | solution.py:282
  12.1 2.0 %collective-permute-start.7 = (bf16[16,4096]{1,0:T(8,128)(2,1)S(1)}, bf16[16,4096]{1,0:T(8,128)(2,1)S(1)}, u32[]{:S(2)}, u32[]{:S(2)}) collective-permute-start(bf16[16,4096]{1,0:T(8,128)(2,1)S(1)} %collective-permute-done.3.refs_7_), channel_id=1, source_target_pairs={{0,1},{1,0},{2,3},{3,2},{4,5},{5,4},{6,7},{7,6},{8,9},{9,8},{10,11... | collective-permute-start | bytes 393224 | tf_op jit(solution)/shard_map/ppermute | solution.py:279
  14.1 0.0 collective-permute-done.2.refs_6_
  14.1 0.0 collective-permute-start.6
  14.7 0.0 collective-permute-done.5.refs_9_
  14.7 0.0 collective-permute-done.8.refs_12_
  14.8 0.3 collective-permute-done.7.refs_11_
  15.1 0.4 %collective-permute-done.6.refs_10_ = bf16[16,4096]{1,0:T(8,128)(2,1)S(1)} collective-permute-done((bf16[16,4096]{1,0:T(8,128)(2,1)S(1)}, bf16[16,4096]{1,0:T(8,128)(2,1)S(1)}, u32[]{:S(2)}, u32[]{:S(2)}) %collective-permute-start.6) | collective-permute-done | bytes 131104 | tf_op jit(solution)/shard_map/ppermute | solution.py:279
  15.4 4.3 %shard_map.87 = (f32[8,16,128]{2,1,0:T(8,128)S(1)}, f32[8,16,128]{2,1,0:T(8,128)S(1)}, f32[8,16,128]{2,1,0:T(8,128)S(1)}, f32[8,16,128]{2,1,0:T(8,128)S(1)}, f32...) custom-call(s32[1,1]{1,0:T(1,128)S(6)} %copy.9.refs_0_, ...), custom_call_target="tpu_custom_call" | custom-call | flops 268435456 | bytes 16777216 | tf_op jit(solution)/shard_map/pallas_call | solution.py:303
  19.8 0.2 collective-permute-start.9
  20.0 0.4 %collective-permute-start.10 = (f32[8,16,128]{2,1,0:T(8,128)S(1)}, f32[8,16,128]{2,1,0:T(8,128)S(1)}, u32[]{:S(2)}, u32[]{:S(2)}) collective-permute-start(f32[8,16,128]{2,1,0:T(8,128)S(1)} %get-tuple-element.21), channel_id=1, source_target_pairs={{0,1},{1,0},{2,3},{3,2},{4,5},{5,4},{6,7},{7,6},{8,9},{9,8},{10,11... | collective-permute-start | bytes 196616 | tf_op jit(solution)/shard_map/ppermute | solution.py:279
  20.4 0.1 collective-permute-start.11
  20.5 0.4 %collective-permute-start.12 = (f32[8,16,128]{2,1,0:T(8,128)S(1)}, f32[8,16,128]{2,1,0:T(8,128)S(1)}, u32[]{:S(2)}, u32[]{:S(2)}) collective-permute-start(f32[8,16,128]{2,1,0:T(8,128)S(1)} %get-tuple-element.23), channel_id=1, source_target_pairs={{0,1},{1,0},{2,3},{3,2},{4,5},{5,4},{6,7},{7,6},{8,9},{9,8},{10,11... | collective-permute-start | bytes 196616 | tf_op jit(solution)/shard_map/ppermute | solution.py:279
  20.9 0.2 collective-permute-done.9.refs_4_
  21.1 0.2 collective-permute-done.10.refs_5_
  21.3 0.4 %collective-permute-done.11.refs_6_ = f32[8,16,128]{2,1,0:T(8,128)S(1)} collective-permute-done((f32[8,16,128]{2,1,0:T(8,128)S(1)}, f32[8,16,128]{2,1,0:T(8,128)S(1)}, u32[]{:S(2)}, u32[]{:S(2)}) %collective-permute-start.11) | collective-permute-done | bytes 65568 | tf_op jit(solution)/shard_map/ppermute | solution.py:279
  21.6 0.2 collective-permute-done.12.refs_7_
  21.8 2.8 %collective-permute-start.13 = (f32[16,16,128]{2,1,0:T(8,128)S(1)}, f32[16,16,128]{2,1,0:T(8,128)S(1)}, u32[]{:S(2)}, u32[]{:S(2)}) collective-permute-start(f32[16,16,128]{2,1,0:T(8,128)S(1)} %get-tuple-element.25), channel_id=1, source_target_pairs={{0,2},{1,9},{2,0},{3,11},{4,6},{5,13},{6,4},{7,15},{8,10},{9,1},{1... | collective-permute-start | bytes 393224 | tf_op jit(solution)/shard_map/ppermute | solution.py:282
  24.6 2.6 %collective-permute-start.14 = (f32[16,16,128]{2,1,0:T(8,128)S(1)}, f32[16,16,128]{2,1,0:T(8,128)S(1)}, u32[]{:S(2)}, u32[]{:S(2)}) collective-permute-start(f32[16,16,128]{2,1,0:T(8,128)S(1)} %get-tuple-element.26), channel_id=1, source_target_pairs={{0,4},{1,17},{2,6},{3,19},{4,0},{5,21},{6,2},{7,23},{8,12},{9,25},... | collective-permute-start | bytes 393224 | tf_op jit(solution)/shard_map/ppermute | solution.py:282
  27.2 0.0 collective-permute-start.15
  27.2 0.3 collective-permute-done.13.refs_1_
  27.5 3.6 %collective-permute-done.14.refs_2_ = f32[16,16,128]{2,1,0:T(8,128)S(1)} collective-permute-done((f32[16,16,128]{2,1,0:T(8,128)S(1)}, f32[16,16,128]{2,1,0:T(8,128)S(1)}, u32[]{:S(2)}, u32[]{:S(2)}) %collective-permute-start.14) | collective-permute-done | bytes 131104 | tf_op jit(solution)/shard_map/ppermute | solution.py:282
  31.1 1.9 %collective-permute-done.15.refs_3_ = f32[16,16,128]{2,1,0:T(8,128)S(1)} collective-permute-done((f32[16,16,128]{2,1,0:T(8,128)S(1)}, f32[16,16,128]{2,1,0:T(8,128)S(1)}, u32[]{:S(2)}, u32[]{:S(2)}) %collective-permute-start.15) | collective-permute-done | bytes 131104 | tf_op jit(solution)/shard_map/ppermute | solution.py:282
  33.1 0.1 collective-permute-start.16
  33.2 1.2 %collective-permute-done.16.got = f32[8,16,128]{2,1,0:T(8,128)S(1)} collective-permute-done((f32[8,16,128]{2,1,0:T(8,128)S(1)}, f32[8,16,128]{2,1,0:T(8,128)S(1)}, u32[]{:S(2)}, u32[]{:S(2)}) %collective-permute-start.16) | collective-permute-done | bytes 65568 | tf_op jit(solution)/shard_map/ppermute | solution.py:279
  34.4 0.7 %shard_map.90 = (f32[16,1024]{1,0:T(8,128)}, f32[4,4096]{1,0:T(4,128)}) custom-call(f32[8,16,128]{2,1,0:T(8,128)S(1)} %get-tuple-element.28.keep, f32[8,16,128]{2,1,0:T(8,128)S(1)} %collective-permute-done.16.got), custom_call_target="tpu_custom_call" | custom-call | tf_op jit(solution)/shard_map/pallas_call | solution.py:342
  (2 shorter events, 0.1 us)
Async XLA Ops:
  0.6 1.9 %collective-permute-start.1 = (bf16[8,4096]{1,0:T(8,128)(2,1)}, bf16[8,4096]{1,0:T(8,128)(2,1)S(1)}, u32[]{:S(2)}, u32[]{:S(2)}) collective-permute-start(bf16[8,4096]{1,0:T(8,128)(2,1)} %table_there.1), channel_id=1, source_target_pairs={{0,1},{1,0},{2,3},{3,2},{4,5},{5,4},{6,7},{7,6},{8,9},{9,8},{10,11... | collective-permute-start | bytes 196616 | tf_op jit(solution)/shard_map/ppermute | solution.py:279
  1.1 1.4 %collective-permute-start = (bf16[16,1024]{1,0:T(8,128)(2,1)}, bf16[16,1024]{1,0:T(8,128)(2,1)S(1)}, u32[]{:S(2)}, u32[]{:S(2)}) collective-permute-start(bf16[16,1024]{1,0:T(8,128)(2,1)} %shard_there.1), channel_id=1, source_target_pairs={{0,1},{1,0},{2,3},{3,2},{4,5},{5,4},{6,7},{7,6},{8,9},{9,8},{10,11... | collective-permute-start | bytes 98312 | tf_op jit(solution)/shard_map/ppermute | solution.py:279
  3.5 6.6 %collective-permute-start.4 = (bf16[16,4096]{1,0:T(8,128)(2,1)S(1)}, bf16[16,4096]{1,0:T(8,128)(2,1)S(1)}, u32[]{:S(2)}, u32[]{:S(2)}) collective-permute-start(bf16[16,4096]{1,0:T(8,128)(2,1)S(1)} %shard_map.86.refs_5_), channel_id=1, source_target_pairs={{0,6},{1,25},{2,4},{3,27},{4,2},{5,29},{6,0},{7,31},{8,14},{9,17},... | collective-permute-start | bytes 393224 | tf_op jit(solution)/shard_map/ppermute | solution.py:282
  7.1 5.0 %collective-permute-start.3 = (bf16[16,4096]{1,0:T(8,128)(2,1)S(1)}, bf16[16,4096]{1,0:T(8,128)(2,1)S(1)}, u32[]{:S(2)}, u32[]{:S(2)}) collective-permute-start(bf16[16,4096]{1,0:T(8,128)(2,1)S(1)} %shard_map.86.refs_5_), channel_id=1, source_target_pairs={{0,4},{1,17},{2,6},{3,19},{4,0},{5,21},{6,2},{7,23},{8,12},{9,25},... | collective-permute-start | bytes 393224 | tf_op jit(solution)/shard_map/ppermute | solution.py:282
  7.6 6.4 %collective-permute-start.2 = (bf16[16,4096]{1,0:T(8,128)(2,1)S(1)}, bf16[16,4096]{1,0:T(8,128)(2,1)S(1)}, u32[]{:S(2)}, u32[]{:S(2)}) collective-permute-start(bf16[16,4096]{1,0:T(8,128)(2,1)S(1)} %shard_map.86.refs_5_), channel_id=1, source_target_pairs={{0,2},{1,9},{2,0},{3,11},{4,6},{5,13},{6,4},{7,15},{8,10},{9,1},{1... | collective-permute-start | bytes 393224 | tf_op jit(solution)/shard_map/ppermute | solution.py:282
  7.8 7.0 %collective-permute-start.5 = (bf16[16,4096]{1,0:T(8,128)(2,1)S(1)}, bf16[16,4096]{1,0:T(8,128)(2,1)S(1)}, u32[]{:S(2)}, u32[]{:S(2)}) collective-permute-start(bf16[16,4096]{1,0:T(8,128)(2,1)S(1)} %shard_map.86.refs_5_), channel_id=1, source_target_pairs={{0,1},{1,0},{2,3},{3,2},{4,5},{5,4},{6,7},{7,6},{8,9},{9,8},{10,11... | collective-permute-start | bytes 393224 | tf_op jit(solution)/shard_map/ppermute | solution.py:279
  10.1 4.7 %collective-permute-start.8 = (bf16[16,4096]{1,0:T(8,128)(2,1)S(1)}, bf16[16,4096]{1,0:T(8,128)(2,1)S(1)}, u32[]{:S(2)}, u32[]{:S(2)}) collective-permute-start(bf16[16,4096]{1,0:T(8,128)(2,1)S(1)} %collective-permute-done.4.refs_8_), channel_id=1, source_target_pairs={{0,1},{1,0},{2,3},{3,2},{4,5},{5,4},{6,7},{7,6},{8,9},{9,8},{10,11... | collective-permute-start | bytes 393224 | tf_op jit(solution)/shard_map/ppermute | solution.py:279
  12.1 3.0 %collective-permute-start.7 = (bf16[16,4096]{1,0:T(8,128)(2,1)S(1)}, bf16[16,4096]{1,0:T(8,128)(2,1)S(1)}, u32[]{:S(2)}, u32[]{:S(2)}) collective-permute-start(bf16[16,4096]{1,0:T(8,128)(2,1)S(1)} %collective-permute-done.3.refs_7_), channel_id=1, source_target_pairs={{0,1},{1,0},{2,3},{3,2},{4,5},{5,4},{6,7},{7,6},{8,9},{9,8},{10,11... | collective-permute-start | bytes 393224 | tf_op jit(solution)/shard_map/ppermute | solution.py:279
  14.1 1.3 %collective-permute-start.6 = (bf16[16,4096]{1,0:T(8,128)(2,1)S(1)}, bf16[16,4096]{1,0:T(8,128)(2,1)S(1)}, u32[]{:S(2)}, u32[]{:S(2)}) collective-permute-start(bf16[16,4096]{1,0:T(8,128)(2,1)S(1)} %collective-permute-done.2.refs_6_), channel_id=1, source_target_pairs={{0,1},{1,0},{2,3},{3,2},{4,5},{5,4},{6,7},{7,6},{8,9},{9,8},{10,11... | collective-permute-start | bytes 393224 | tf_op jit(solution)/shard_map/ppermute | solution.py:279
  19.8 1.3 %collective-permute-start.9 = (f32[8,16,128]{2,1,0:T(8,128)S(1)}, f32[8,16,128]{2,1,0:T(8,128)S(1)}, u32[]{:S(2)}, u32[]{:S(2)}) collective-permute-start(f32[8,16,128]{2,1,0:T(8,128)S(1)} %get-tuple-element.20), channel_id=1, source_target_pairs={{0,1},{1,0},{2,3},{3,2},{4,5},{5,4},{6,7},{7,6},{8,9},{9,8},{10,11... | collective-permute-start | bytes 196616 | tf_op jit(solution)/shard_map/ppermute | solution.py:279
  20.0 1.3 %collective-permute-start.10 = (f32[8,16,128]{2,1,0:T(8,128)S(1)}, f32[8,16,128]{2,1,0:T(8,128)S(1)}, u32[]{:S(2)}, u32[]{:S(2)}) collective-permute-start(f32[8,16,128]{2,1,0:T(8,128)S(1)} %get-tuple-element.21), channel_id=1, source_target_pairs={{0,1},{1,0},{2,3},{3,2},{4,5},{5,4},{6,7},{7,6},{8,9},{9,8},{10,11... | collective-permute-start | bytes 196616 | tf_op jit(solution)/shard_map/ppermute | solution.py:279
  20.4 1.3 %collective-permute-start.11 = (f32[8,16,128]{2,1,0:T(8,128)S(1)}, f32[8,16,128]{2,1,0:T(8,128)S(1)}, u32[]{:S(2)}, u32[]{:S(2)}) collective-permute-start(f32[8,16,128]{2,1,0:T(8,128)S(1)} %get-tuple-element.22), channel_id=1, source_target_pairs={{0,1},{1,0},{2,3},{3,2},{4,5},{5,4},{6,7},{7,6},{8,9},{9,8},{10,11... | collective-permute-start | bytes 196616 | tf_op jit(solution)/shard_map/ppermute | solution.py:279
  20.5 1.3 %collective-permute-start.12 = (f32[8,16,128]{2,1,0:T(8,128)S(1)}, f32[8,16,128]{2,1,0:T(8,128)S(1)}, u32[]{:S(2)}, u32[]{:S(2)}) collective-permute-start(f32[8,16,128]{2,1,0:T(8,128)S(1)} %get-tuple-element.23), channel_id=1, source_target_pairs={{0,1},{1,0},{2,3},{3,2},{4,5},{5,4},{6,7},{7,6},{8,9},{9,8},{10,11... | collective-permute-start | bytes 196616 | tf_op jit(solution)/shard_map/ppermute | solution.py:279
  21.8 5.7 %collective-permute-start.13 = (f32[16,16,128]{2,1,0:T(8,128)S(1)}, f32[16,16,128]{2,1,0:T(8,128)S(1)}, u32[]{:S(2)}, u32[]{:S(2)}) collective-permute-start(f32[16,16,128]{2,1,0:T(8,128)S(1)} %get-tuple-element.25), channel_id=1, source_target_pairs={{0,2},{1,9},{2,0},{3,11},{4,6},{5,13},{6,4},{7,15},{8,10},{9,1},{1... | collective-permute-start | bytes 393224 | tf_op jit(solution)/shard_map/ppermute | solution.py:282
  24.6 6.5 %collective-permute-start.14 = (f32[16,16,128]{2,1,0:T(8,128)S(1)}, f32[16,16,128]{2,1,0:T(8,128)S(1)}, u32[]{:S(2)}, u32[]{:S(2)}) collective-permute-start(f32[16,16,128]{2,1,0:T(8,128)S(1)} %get-tuple-element.26), channel_id=1, source_target_pairs={{0,4},{1,17},{2,6},{3,19},{4,0},{5,21},{6,2},{7,23},{8,12},{9,25},... | collective-permute-start | bytes 393224 | tf_op jit(solution)/shard_map/ppermute | solution.py:282
  27.2 5.9 %collective-permute-start.15 = (f32[16,16,128]{2,1,0:T(8,128)S(1)}, f32[16,16,128]{2,1,0:T(8,128)S(1)}, u32[]{:S(2)}, u32[]{:S(2)}) collective-permute-start(f32[16,16,128]{2,1,0:T(8,128)S(1)} %get-tuple-element.27), channel_id=1, source_target_pairs={{0,6},{1,25},{2,4},{3,27},{4,2},{5,29},{6,0},{7,31},{8,14},{9,17},... | collective-permute-start | bytes 393224 | tf_op jit(solution)/shard_map/ppermute | solution.py:282
  33.1 1.3 %collective-permute-start.16 = (f32[8,16,128]{2,1,0:T(8,128)S(1)}, f32[8,16,128]{2,1,0:T(8,128)S(1)}, u32[]{:S(2)}, u32[]{:S(2)}) collective-permute-start(f32[8,16,128]{2,1,0:T(8,128)S(1)} %get-tuple-element.29), channel_id=1, source_target_pairs={{0,1},{1,0},{2,3},{3,2},{4,5},{5,4},{6,7},{7,6},{8,9},{9,8},{10,11... | collective-permute-start | bytes 196616 | tf_op jit(solution)/shard_map/ppermute | solution.py:279

commit v3 on v2

--- a/solution.py
+++ b/solution.py
@@ -9,8 +9,11 @@
 
 BLK = 128
 REWARDS = 16
-CHUNK = 64
-SUMS = 4
+CHUNK = 128
+PART = 32
+SUMS = 1
+LAG = 2
+DEEP = 4
 VMEM_LIMIT = 40 * 2**20
 
 
@@ -39,7 +42,7 @@
     return jnp.concatenate([table[:, at * width : (at + 1) * width] for at in range(pieces)], axis=0)
 
 
-def gather_kernel(shard_there, table_there, other_shard, other_table, out, shard, table, sems):
+def load_kernel(shard_there, table_there, shard, table, sems):
     copies = [
         pltpu.make_async_copy(shard_there, shard, sems.at[0]),
         pltpu.make_async_copy(table_there, table, sems.at[1]),
@@ -48,17 +51,24 @@
         copy.start()
     for copy in copies:
         copy.wait()
-    core, span, width = lax.axis_index("col") % 2, shard.shape[1], out.shape[1]
+
+
+def gather_kernel(shard, table, other_shard, other_table, mine, other):
+    core, span, width = lax.axis_index("col") % 2, shard.shape[1], mine.shape[1]
+
+    def write(shards, tables, shards_out, tables_out):
+        for half in range(2):
+            shards_out[:, half * span : (half + 1) * span] = shards[half][...]
+        lines = [lay(part[...].astype(jnp.float32), width) for part in tables]
+        tables_out[...] = jnp.concatenate(lines, axis=0).astype(tables_out.dtype)
 
     @pl.when(core == 0)
     def _():
-        out[:, :span] = shard[...]
-        out[:, span : 2 * span] = other_shard[...]
+        write((shard, other_shard), (table, other_table), mine, other)
 
     @pl.when(core == 1)
     def _():
-        lines = [lay(part[...].astype(jnp.float32), width) for part in (other_table, table)]
-        out[...] = jnp.concatenate(lines, axis=0).astype(out.dtype)
+        write((other_shard, shard), (other_table, table), other, mine)
 
 
 def spread(first, second):
@@ -87,13 +97,13 @@
     for copy in copies:
         copy.start()
 
-    def block_copy(chunk):
-        part = pl.ds(pl.multiple_of(chunk * CHUNK, CHUNK), CHUNK)
-        return pltpu.make_async_copy(blocks_there.at[:, :, part], blocks.at[:, :, part], block_sems.at[chunk])
-
-    chunk_count = blocks.shape[2] // CHUNK
-    for chunk in range(chunk_count):
-        block_copy(chunk).start()
+    def block_copy(part):
+        slots = pl.ds(pl.multiple_of(part * PART, PART), PART)
+        return pltpu.make_async_copy(blocks_there.at[:, :, slots], blocks.at[:, :, slots], block_sems.at[part])
+
+    part_count = blocks.shape[2] // PART
+    for part in range(part_count):
+        block_copy(part).start()
     for sums in (*value_sums, *grad_sums):
         sums[...] = jnp.zeros_like(sums)
     weights[row_cells] = jnp.zeros((REWARDS, BLK), jnp.bfloat16)
@@ -127,28 +137,51 @@
 
     for copy in copies:
         copy.wait()
-    candidates = group * n_row
-    lane = lax.broadcasted_iota(jnp.int32, (REWARDS, candidates), 1)
-    column = lane % group + (own_row ^ (lane // group)) * group
-    line = lax.broadcasted_iota(jnp.int32, (REWARDS, candidates), 0)
-    wanted = jnp.zeros((REWARDS, candidates), jnp.int32)
+    candidates, side = group * n_row, 2 * BLK
+    bands = side // candidates
+    lane = lax.broadcasted_iota(jnp.int32, (REWARDS, side), 1)
+    at = lane % candidates
+    column = at % group + (own_row ^ (at // group)) * group
+    line = lax.broadcasted_iota(jnp.int32, (REWARDS, side), 0)
+    wanted = jnp.zeros((REWARDS, side), jnp.int32)
     for k in range(REWARDS):
         wanted = jnp.where(line == k, reward_cols[k], wanted)
-    pick = (column == wanted).astype(jnp.float32).astype(jnp.bfloat16)
-    for col in range(col_cells):
-        rewards[col] = jnp.dot(
-            pick,
-            table[:, col * BLK : (col + 1) * BLK].astype(jnp.bfloat16),
-            preferred_element_type=jnp.float32,
-        ).astype(jnp.bfloat16)
+    hit = column == wanted
+    pick = [jnp.where(hit & (lane // candidates == band), 1.0, 0.0) for band in range(bands)]
+    pick = jnp.concatenate(pick, axis=0).astype(jnp.bfloat16)
+
+    def pick_rewards(*units):
+        for turn in range(col_cells * BLK // (bands * side)):
+            unit = turn % 2
+            lanes = [pl.ds((turn * bands + band) * side, side) for band in range(bands)]
+            tile = jnp.concatenate([table[:, here] for here in lanes], axis=0).astype(jnp.bfloat16)
+            pltpu.matmul_push_rhs(tile, 0, unit)
+            pltpu.matmul_acc_lhs(units[unit], pick, load_staged_rhs=0)
+            product = pltpu.matmul_pop(units[unit]).astype(jnp.bfloat16)
+            for cell in range(2 * bands):
+                band, half = divmod(cell, 2)
+                rewards[turn * 2 * bands + cell] = product[
+                    band * REWARDS : (band + 1) * REWARDS, half * BLK : (half + 1) * BLK
+                ]
+
+    pl.run_scoped(pick_rewards, *[pltpu.ACC(unit)((bands * REWARDS, side), jnp.float32) for unit in (0, 1)])
 
     live_count = counts[0, 0]
 
-    def visit(chunk, carry):
-        block_copy(chunk).wait()
-        found = []
+    def visit(units, chunk, carry):
+        queued = []
+
+        def add_next():
+            totals, order, cells, unit = queued.pop(0)
+            product = pltpu.matmul_pop(unit)
+            for piece, (at, side) in enumerate(order):
+                part = product[piece * REWARDS : (piece + 1) * REWARDS, side * BLK : (side + 1) * BLK]
+                totals[at % SUMS][cells[at]] += part
+
         for quad in range(CHUNK // 4):
             start = chunk * CHUNK + quad * 4
+            if quad * 4 % PART == 0:
+                block_copy(chunk * (CHUNK // PART) + quad * 4 // PART).wait()
             rows, cols = [], []
             for at in range(4):
                 live = start + at < live_count
@@ -158,33 +191,35 @@
             tile = jnp.concatenate(
                 [jnp.concatenate(stored[:2], axis=0), jnp.concatenate(stored[2:], axis=0)], axis=1
             )
+            plain, turned, stage = quad % 2, 1 - quad % 2, quad % 2
+            pltpu.matmul_push_rhs(tile, stage, plain)
+            pltpu.matmul_push_rhs(tile, stage, turned, transpose=True)
             factor = [weights[row] for row in rows]
-            product = lax.dot_general(
-                spread((factor[0], factor[2]), (factor[1], factor[3])),
-                tile,
-                (((1,), (0,)), ((), ())),
-                preferred_element_type=jnp.float32,
-            )
-            for piece, (at, side) in enumerate(((0, 0), (2, 1), (1, 0), (3, 1))):
-                part = product[piece * REWARDS : (piece + 1) * REWARDS, side * BLK : (side + 1) * BLK]
-                found.append((grad_sums[at % SUMS], cols[at], part))
+            unit = units[plain][quad % DEEP]
+            left = spread((factor[0], factor[2]), (factor[1], factor[3]))
+            pltpu.matmul_acc_lhs(unit, left, load_staged_rhs=stage)
+            queued.append((grad_sums, ((0, 0), (2, 1), (1, 0), (3, 1)), cols, unit))
             factor = [rewards[col] for col in cols]
-            product = lax.dot_general(
-                spread((factor[0], factor[1]), (factor[2], factor[3])),
-                tile,
-                (((1,), (1,)), ((), ())),
-                preferred_element_type=jnp.float32,
-            )
-            for piece, (at, side) in enumerate(((0, 0), (1, 1), (2, 0), (3, 1))):
-                part = product[piece * REWARDS : (piece + 1) * REWARDS, side * BLK : (side + 1) * BLK]
-                found.append((value_sums[at % SUMS], rows[at], part))
-        for sums, cell, part in found:
-            sums[cell] += part
+            unit = units[turned][quad % DEEP]
+            left = spread((factor[0], factor[1]), (factor[2], factor[3]))
+            pltpu.matmul_acc_lhs(unit, left, load_staged_rhs=stage)
+            queued.append((value_sums, ((0, 0), (1, 1), (2, 0), (3, 1)), rows, unit))
+            while len(queued) > 2 * LAG:
+                add_next()
+        while queued:
+            add_next()
         return carry
 
     live_chunks = (live_count + CHUNK - 1) // CHUNK
-    lax.fori_loop(0, live_chunks, visit, 0)
-    lax.fori_loop(live_chunks, chunk_count, lambda chunk, carry: (block_copy(chunk).wait(), carry)[1], 0)
+
+    def multiply(*units):
+        held = (units[:DEEP], units[DEEP:])
+        lax.fori_loop(0, live_chunks, functools.partial(visit, held), 0)
+
+    pl.run_scoped(multiply, *[pltpu.ACC(unit)((4 * REWARDS, 2 * BLK), jnp.float32) for unit in (0, 1) for _ in range(DEEP)])
+    lax.fori_loop(
+        live_chunks * (CHUNK // PART), part_count, lambda part, carry: (block_copy(part).wait(), carry)[1], 0
+    )
 
     lines = REWARDS // n_row
     part = row_cells // n_chip
@@ -215,11 +250,9 @@
         put(gives, keeps)
 
 
-def pair_kernel(*refs):
-    count = len(refs) // 3
-    for keep, got, out in zip(refs[:count], refs[count : 2 * count], refs[2 * count :]):
-        half = keep.shape[0]
-        out[:half], out[half:] = by_core(keep[...], got[...])
+def pair_kernel(keep, got, out):
+    half = keep.shape[0]
+    out[:half], out[half:] = by_core(keep[...], got[...])
 
 
 def total_kernel(n_row, n_chip, *refs):
@@ -282,20 +315,24 @@
         return lax.ppermute(part, ("row", "col"), crossings(n_row, n_col, step))
 
     width = 2 * reward_table.shape[0] * reward_table.shape[1] // REWARDS
-    chip_inputs = pl.pallas_call(
+    loaded = pl.pallas_call(
+        load_kernel,
+        out_shape=[jax.ShapeDtypeStruct(arg.shape, arg.dtype) for arg in (cotangent, reward_table)],
+        in_specs=[hbm] * 2,
+        out_specs=[vmem] * 2,
+        scratch_shapes=[pltpu.SemaphoreType.DMA((2,))],
+        compiler_params=small,
+        cost_estimate=pl.CostEstimate(flops=0, bytes_accessed=4 * 2**20, transcendentals=0),
+    )(in_hbm(cotangent), in_hbm(reward_table))
+    mine, other = pl.pallas_call(
         gather_kernel,
-        out_shape=jax.ShapeDtypeStruct((REWARDS, width), cotangent.dtype),
-        in_specs=[hbm] * 2 + [vmem] * 2,
-        out_specs=vmem,
-        scratch_shapes=[
-            pltpu.VMEM(cotangent.shape, cotangent.dtype),
-            pltpu.VMEM(reward_table.shape, reward_table.dtype),
-            pltpu.SemaphoreType.DMA((2,)),
-        ],
+        out_shape=[jax.ShapeDtypeStruct((REWARDS, width), cotangent.dtype)] * 2,
+        in_specs=[vmem] * 4,
+        out_specs=[vmem] * 2,
         compiler_params=small,
-    )(in_hbm(cotangent), in_hbm(reward_table), swap(cotangent), swap(reward_table))
-    mine = [chip_inputs] + [cross(chip_inputs, step) for step in range(1, steps)]
-    others = [swap(part) for part in mine]
+    )(*loaded, swap(cotangent), swap(reward_table))
+    mine = [mine] + [cross(mine, step) for step in range(1, steps)]
+    others = [other] + [swap(part) for part in mine[1:]]
 
     lines, part = REWARDS // n_row, row_cells // n_chip
     tiles = jax.ShapeDtypeStruct((max(part, col_cells * lines // REWARDS), REWARDS, BLK), jnp.float32)
@@ -316,7 +353,7 @@
             *[pltpu.VMEM((row_cells + 1, REWARDS, BLK), jnp.float32)] * SUMS,
             *[pltpu.VMEM((col_cells + 1, REWARDS, BLK), jnp.float32)] * SUMS,
             pltpu.SemaphoreType.DMA((3,)),
-            pltpu.SemaphoreType.DMA((blocks.shape[2] // CHUNK,)),
+            pltpu.SemaphoreType.DMA((blocks.shape[2] // PART,)),
         ],
         compiler_params=pltpu.CompilerParams(vmem_limit_bytes=VMEM_LIMIT),
         cost_estimate=pl.CostEstimate(
@@ -324,14 +361,16 @@
         ),
     )(counts, *map(in_hbm, (slot_rows, slot_cols, reward_cols, blocks)), *mine, *others)
     keeps, gives = sums[:steps], sums[steps:]
-    pairs = pl.pallas_call(
-        pair_kernel,
-        out_shape=[both] * steps,
-        in_specs=[vmem] * (2 * steps),
-        out_specs=[vmem] * steps,
-        compiler_params=small,
-    )(*keeps, *[swap(give) for give in gives])
-    parts = [pairs[0]] + [cross(pairs[step], step) for step in range(1, steps)]
+    parts = []
+    for step in reversed(range(steps)):
+        pair = pl.pallas_call(
+            pair_kernel,
+            out_shape=both,
+            in_specs=[vmem] * 2,
+            out_specs=vmem,
+            compiler_params=small,
+        )(keeps[step], swap(gives[step]))
+        parts.insert(0, cross(pair, step) if step else pair)
     keep, give = pl.pallas_call(
         functools.partial(total_kernel, n_row, n_chip),
         out_shape=[tiles] * 2,

time: 35.2 us -> 31.9 us (0.906)
  waiting for transfers between devices: 12.7 us -> 10.1 us
  starting transfers between devices: 15.1 us -> 13.1 us
  Pallas kernels: 5.96 us -> 7.39 us
    ppermute x6, waiting for transfers between devices: 8.5 us -> 6.56 us  [cross(): return lax.ppermute(part, ('row', 'col'), crossings(n_row, n_col, step))]
    ppermute x6, starting transfers between devices: 9.68 us -> 8 us  [cross(): return lax.ppermute(part, ('row', 'col'), crossings(n_row, n_col, step))]
    pallas_call x1, Pallas kernels: 4.34 us -> 5.74 us  [on_device(): pl.pallas_call(functools.partial(products_kernel, n_row, n_col), out_shap...]
    ppermute x11 -> x10, waiting for transfers between devices: 4.16 us -> 3.57 us  [swap(): return lax.ppermute(part, 'col', peers(n_col, 1))]
    ppermute x11 -> x10, starting transfers between devices: 5.42 us -> 5.14 us  [swap(): return lax.ppermute(part, 'col', peers(n_col, 1))]
    pallas_call x2 -> x6, Pallas kernels: 0.92 us -> 0.96 us  [the longest x1 0.88 us: on_device(): pl.pallas_call(load_kernel, out_shape=[jax.ShapeDtypeStruct(arg.shape, ar...]
  transfers between devices with their start and end apart: 17 -> 16, of which waited for: 13 -> 11; matrix products, arithmetic and copies ran while one was open for 0% -> 0% of each run, Pallas kernels for 0% -> 3%
where the time goes in v3:
time: 31.9 us; the launch traced here: 32 us
  starting transfers between devices  13.1 us (41%)
  waiting for transfers between devices  10.1 us (32%)
  Pallas kernels  7.39 us (23%)
  between operations  1.36 us (4%)
    ppermute x6, starting transfers between devices, cross(): return lax.ppermute(part, ('row', 'col'), crossings(n_row, n_col, step))  8 us
    ppermute x6, waiting for transfers between devices, cross(): return lax.ppermute(part, ('row', 'col'), crossings(n_row, n_col, step))  6.56 us
    pallas_call x1, Pallas kernels, on_device(): pl.pallas_call(functools.partial(products_kernel, n_row, n_col), out_shap...  5.74 us
    ppermute x10, starting transfers between devices, swap(): return lax.ppermute(part, 'col', peers(n_col, 1))  5.14 us
    ppermute x10, waiting for transfers between devices, swap(): return lax.ppermute(part, 'col', peers(n_col, 1))  3.57 us
    pallas_call x1, Pallas kernels, on_device(): pl.pallas_call(load_kernel, out_shape=[jax.ShapeDtypeStruct(arg.shape, ar...  0.88 us
    pallas_call x1, Pallas kernels, on_device(): pl.pallas_call(result_kernel, out_shape=[jax.ShapeDtypeStruct((REWARDS, p...  0.66 us
  transfers between devices with their start and end apart: 16, of which 11 were waited for; matrix products, arithmetic and copies ran while one was open for 0% of the time, Pallas kernels for 3%

profile of v3, /device:TPU:0, one launch (start us, length us, event | category | flops | bytes accessed | tf_op | source)
XLA Modules:
  0.0 32.0 jit_solution(7349572936552421940)
XLA Ops:
  0.6 0.5 %collective-permute-start.1 = (bf16[8,4096]{1,0:T(8,128)(2,1)}, bf16[8,4096]{1,0:T(8,128)(2,1)S(1)}, u32[]{:S(2)}, u32[]{:S(2)}) collective-permute-start(bf16[8,4096]{1,0:T(8,128)(2,1)} %table_there.1), channel_id=1, source_target_pairs={{0,1},{1,0},{2,3},{3,2},{4,5},{5,4},{6,7},{7,6},{8,9},{9,8},{10,11... | collective-permute-start | bytes 196616 | tf_op jit(solution)/shard_map/ppermute | solution.py:312
  1.1 0.1 collective-permute-start
  1.2 0.9 %shard_map.86 = (bf16[16,1024]{1,0:T(8,128)(2,1)S(1)}, bf16[8,4096]{1,0:T(8,128)(2,1)S(1)}) custom-call(bf16[16,1024]{1,0:T(8,128)(2,1)} %shard_there.1, bf16[8,4096]{1,0:T(8,128)(2,1)} %table_there.1), custom_call_target="tpu_custom_call" | custom-call | bytes 4194304 | tf_op jit(solution)/shard_map/pallas_call | solution.py:318
  2.1 0.5 %collective-permute-done.other_shard = bf16[16,1024]{1,0:T(8,128)(2,1)S(1)} collective-permute-done((bf16[16,1024]{1,0:T(8,128)(2,1)}, bf16[16,1024]{1,0:T(8,128)(2,1)S(1)}, u32[]{:S(2)}, u32[]{:S(2)}) %collective-permute-start) | collective-permute-done | bytes 32800 | tf_op jit(solution)/shard_map/ppermute | solution.py:312
  2.6 0.0 collective-permute-done.1.other_table
  2.6 3.7 %collective-permute-start.4 = (bf16[16,4096]{1,0:T(8,128)(2,1)S(1)}, bf16[16,4096]{1,0:T(8,128)(2,1)S(1)}, u32[]{:S(2)}, u32[]{:S(2)}) collective-permute-start(bf16[16,4096]{1,0:T(8,128)(2,1)S(1)} %get-tuple-element.18.refs_5_), channel_id=1, source_target_pairs={{0,6},{1,25},{2,4},{3,27},{4,2},{5,29},{6,0},{7,31},{8,14},{9,17},... | collective-permute-start | bytes 393224 | tf_op jit(solution)/shard_map/ppermute | solution.py:315
  6.3 0.5 %collective-permute-start.3 = (bf16[16,4096]{1,0:T(8,128)(2,1)S(1)}, bf16[16,4096]{1,0:T(8,128)(2,1)S(1)}, u32[]{:S(2)}, u32[]{:S(2)}) collective-permute-start(bf16[16,4096]{1,0:T(8,128)(2,1)S(1)} %get-tuple-element.18.refs_5_), channel_id=1, source_target_pairs={{0,4},{1,17},{2,6},{3,19},{4,0},{5,21},{6,2},{7,23},{8,12},{9,25},... | collective-permute-start | bytes 393224 | tf_op jit(solution)/shard_map/ppermute | solution.py:315
  6.8 0.1 collective-permute-start.2
  6.9 2.3 %collective-permute-done.4.refs_8_ = bf16[16,4096]{1,0:T(8,128)(2,1)S(1)} collective-permute-done((bf16[16,4096]{1,0:T(8,128)(2,1)S(1)}, bf16[16,4096]{1,0:T(8,128)(2,1)S(1)}, u32[]{:S(2)}, u32[]{:S(2)}) %collective-permute-start.4) | collective-permute-done | bytes 131104 | tf_op jit(solution)/shard_map/ppermute | solution.py:315
  9.2 0.7 %collective-permute-start.7 = (bf16[16,4096]{1,0:T(8,128)(2,1)S(1)}, bf16[16,4096]{1,0:T(8,128)(2,1)S(1)}, u32[]{:S(2)}, u32[]{:S(2)}) collective-permute-start(bf16[16,4096]{1,0:T(8,128)(2,1)S(1)} %collective-permute-done.4.refs_8_), channel_id=1, source_target_pairs={{0,1},{1,0},{2,3},{3,2},{4,5},{5,4},{6,7},{7,6},{8,9},{9,8},{10,11... | collective-permute-start | bytes 393224 | tf_op jit(solution)/shard_map/ppermute | solution.py:312
  9.9 1.3 %collective-permute-done.3.refs_7_ = bf16[16,4096]{1,0:T(8,128)(2,1)S(1)} collective-permute-done((bf16[16,4096]{1,0:T(8,128)(2,1)S(1)}, bf16[16,4096]{1,0:T(8,128)(2,1)S(1)}, u32[]{:S(2)}, u32[]{:S(2)}) %collective-permute-start.3) | collective-permute-done | bytes 131104 | tf_op jit(solution)/shard_map/ppermute | solution.py:315
  11.2 2.0 %collective-permute-start.6 = (bf16[16,4096]{1,0:T(8,128)(2,1)S(1)}, bf16[16,4096]{1,0:T(8,128)(2,1)S(1)}, u32[]{:S(2)}, u32[]{:S(2)}) collective-permute-start(bf16[16,4096]{1,0:T(8,128)(2,1)S(1)} %collective-permute-done.3.refs_7_), channel_id=1, source_target_pairs={{0,1},{1,0},{2,3},{3,2},{4,5},{5,4},{6,7},{7,6},{8,9},{9,8},{10,11... | collective-permute-start | bytes 393224 | tf_op jit(solution)/shard_map/ppermute | solution.py:312
  13.2 0.0 collective-permute-done.2.refs_6_
  13.2 0.0 collective-permute-start.5
  13.9 0.0 collective-permute-done.7.refs_12_
  13.9 0.3 collective-permute-done.6.refs_11_
  14.2 0.4 %collective-permute-done.5.refs_10_ = bf16[16,4096]{1,0:T(8,128)(2,1)S(1)} collective-permute-done((bf16[16,4096]{1,0:T(8,128)(2,1)S(1)}, bf16[16,4096]{1,0:T(8,128)(2,1)S(1)}, u32[]{:S(2)}, u32[]{:S(2)}) %collective-permute-start.5) | collective-permute-done | bytes 131104 | tf_op jit(solution)/shard_map/ppermute | solution.py:312
  14.6 5.7 %shard_map.88 = (f32[8,16,128]{2,1,0:T(8,128)S(1)}, f32[8,16,128]{2,1,0:T(8,128)S(1)}, f32[8,16,128]{2,1,0:T(8,128)S(1)}, f32[8,16,128]{2,1,0:T(8,128)S(1)}, f32...) custom-call(s32[1,1]{1,0:T(1,128)S(6)} %copy.9.refs_0_, ...), custom_call_target="tpu_custom_call" | custom-call | flops 268435456 | bytes 16777216 | tf_op jit(solution)/shard_map/pallas_call | solution.py:340
  20.3 0.3 collective-permute-start.13
  20.6 0.3 collective-permute-start.11
  20.9 0.2 collective-permute-start.9
  21.1 0.5 %collective-permute-done.13.got = f32[8,16,128]{2,1,0:T(8,128)S(1)} collective-permute-done((f32[8,16,128]{2,1,0:T(8,128)S(1)}, f32[8,16,128]{2,1,0:T(8,128)S(1)}, u32[]{:S(2)}, u32[]{:S(2)}) %collective-permute-start.13) | collective-permute-done | bytes 65568 | tf_op jit(solution)/shard_map/ppermute | solution.py:312
  21.6 2.5 %collective-permute-start.14 = (f32[16,16,128]{2,1,0:T(8,128)S(1)}, f32[16,16,128]{2,1,0:T(8,128)S(1)}, u32[]{:S(2)}, u32[]{:S(2)}) collective-permute-start(f32[16,16,128]{2,1,0:T(8,128)S(1)} %shard_map.92), channel_id=1, source_target_pairs={{0,6},{1,25},{2,4},{3,27},{4,2},{5,29},{6,0},{7,31},{8,14},{9,17},... | collective-permute-start | bytes 393224 | tf_op jit(solution)/shard_map/ppermute | solution.py:315
  24.1 0.0 collective-permute-done.11.got
  24.2 0.4 %collective-permute-start.12 = (f32[16,16,128]{2,1,0:T(8,128)S(1)}, f32[16,16,128]{2,1,0:T(8,128)S(1)}, u32[]{:S(2)}, u32[]{:S(2)}) collective-permute-start(f32[16,16,128]{2,1,0:T(8,128)S(1)} %shard_map.91), channel_id=1, source_target_pairs={{0,4},{1,17},{2,6},{3,19},{4,0},{5,21},{6,2},{7,23},{8,12},{9,25},... | collective-permute-start | bytes 393224 | tf_op jit(solution)/shard_map/ppermute | solution.py:315
  24.6 0.0 collective-permute-done.9.got
  24.6 0.8 %collective-permute-start.10 = (f32[16,16,128]{2,1,0:T(8,128)S(1)}, f32[16,16,128]{2,1,0:T(8,128)S(1)}, u32[]{:S(2)}, u32[]{:S(2)}) collective-permute-start(f32[16,16,128]{2,1,0:T(8,128)S(1)} %shard_map.90), channel_id=1, source_target_pairs={{0,2},{1,9},{2,0},{3,11},{4,6},{5,13},{6,4},{7,15},{8,10},{9,1},{1... | collective-permute-start | bytes 393224 | tf_op jit(solution)/shard_map/ppermute | solution.py:315
  25.4 0.3 collective-permute-start.8
  25.7 1.0 %collective-permute-done.8.got = f32[8,16,128]{2,1,0:T(8,128)S(1)} collective-permute-done((f32[8,16,128]{2,1,0:T(8,128)S(1)}, f32[8,16,128]{2,1,0:T(8,128)S(1)}, u32[]{:S(2)}, u32[]{:S(2)}) %collective-permute-start.8) | collective-permute-done | bytes 65568 | tf_op jit(solution)/shard_map/ppermute | solution.py:312
  26.7 0.9 %collective-permute-done.14.refs_3_ = f32[16,16,128]{2,1,0:T(8,128)S(1)} collective-permute-done((f32[16,16,128]{2,1,0:T(8,128)S(1)}, f32[16,16,128]{2,1,0:T(8,128)S(1)}, u32[]{:S(2)}, u32[]{:S(2)}) %collective-permute-start.14) | collective-permute-done | bytes 131104 | tf_op jit(solution)/shard_map/ppermute | solution.py:315
  27.6 1.6 %collective-permute-done.12.refs_2_ = f32[16,16,128]{2,1,0:T(8,128)S(1)} collective-permute-done((f32[16,16,128]{2,1,0:T(8,128)S(1)}, f32[16,16,128]{2,1,0:T(8,128)S(1)}, u32[]{:S(2)}, u32[]{:S(2)}) %collective-permute-start.12) | collective-permute-done | bytes 131104 | tf_op jit(solution)/shard_map/ppermute | solution.py:315
  29.2 0.4 %collective-permute-done.10.refs_1_ = f32[16,16,128]{2,1,0:T(8,128)S(1)} collective-permute-done((f32[16,16,128]{2,1,0:T(8,128)S(1)}, f32[16,16,128]{2,1,0:T(8,128)S(1)}, u32[]{:S(2)}, u32[]{:S(2)}) %collective-permute-start.10) | collective-permute-done | bytes 131104 | tf_op jit(solution)/shard_map/ppermute | solution.py:315
  29.7 0.8 %collective-permute-start.15 = (f32[8,16,128]{2,1,0:T(8,128)S(1)}, f32[8,16,128]{2,1,0:T(8,128)S(1)}, u32[]{:S(2)}, u32[]{:S(2)}) collective-permute-start(f32[8,16,128]{2,1,0:T(8,128)S(1)} %get-tuple-element.29), channel_id=1, source_target_pairs={{0,1},{1,0},{2,3},{3,2},{4,5},{5,4},{6,7},{7,6},{8,9},{9,8},{10,11... | collective-permute-start | bytes 196616 | tf_op jit(solution)/shard_map/ppermute | solution.py:312
  30.4 0.9 %collective-permute-done.15.got = f32[8,16,128]{2,1,0:T(8,128)S(1)} collective-permute-done((f32[8,16,128]{2,1,0:T(8,128)S(1)}, f32[8,16,128]{2,1,0:T(8,128)S(1)}, u32[]{:S(2)}, u32[]{:S(2)}) %collective-permute-start.15) | collective-permute-done | bytes 65568 | tf_op jit(solution)/shard_map/ppermute | solution.py:312
  31.4 0.7 %shard_map.94 = (f32[16,1024]{1,0:T(8,128)}, f32[4,4096]{1,0:T(4,128)}) custom-call(f32[8,16,128]{2,1,0:T(8,128)S(1)} %get-tuple-element.28.keep, f32[8,16,128]{2,1,0:T(8,128)S(1)} %collective-permute-done.15.got), custom_call_target="tpu_custom_call" | custom-call | tf_op jit(solution)/shard_map/pallas_call | solution.py:381
  (6 shorter events, 0.1 us)
Async XLA Ops:
  0.6 1.9 %collective-permute-start.1 = (bf16[8,4096]{1,0:T(8,128)(2,1)}, bf16[8,4096]{1,0:T(8,128)(2,1)S(1)}, u32[]{:S(2)}, u32[]{:S(2)}) collective-permute-start(bf16[8,4096]{1,0:T(8,128)(2,1)} %table_there.1), channel_id=1, source_target_pairs={{0,1},{1,0},{2,3},{3,2},{4,5},{5,4},{6,7},{7,6},{8,9},{9,8},{10,11... | collective-permute-start | bytes 196616 | tf_op jit(solution)/shard_map/ppermute | solution.py:312
  1.1 1.4 %collective-permute-start = (bf16[16,1024]{1,0:T(8,128)(2,1)}, bf16[16,1024]{1,0:T(8,128)(2,1)S(1)}, u32[]{:S(2)}, u32[]{:S(2)}) collective-permute-start(bf16[16,1024]{1,0:T(8,128)(2,1)} %shard_there.1), channel_id=1, source_target_pairs={{0,1},{1,0},{2,3},{3,2},{4,5},{5,4},{6,7},{7,6},{8,9},{9,8},{10,11... | collective-permute-start | bytes 98312 | tf_op jit(solution)/shard_map/ppermute | solution.py:312
  2.6 6.6 %collective-permute-start.4 = (bf16[16,4096]{1,0:T(8,128)(2,1)S(1)}, bf16[16,4096]{1,0:T(8,128)(2,1)S(1)}, u32[]{:S(2)}, u32[]{:S(2)}) collective-permute-start(bf16[16,4096]{1,0:T(8,128)(2,1)S(1)} %get-tuple-element.18.refs_5_), channel_id=1, source_target_pairs={{0,6},{1,25},{2,4},{3,27},{4,2},{5,29},{6,0},{7,31},{8,14},{9,17},... | collective-permute-start | bytes 393224 | tf_op jit(solution)/shard_map/ppermute | solution.py:315
  6.3 5.0 %collective-permute-start.3 = (bf16[16,4096]{1,0:T(8,128)(2,1)S(1)}, bf16[16,4096]{1,0:T(8,128)(2,1)S(1)}, u32[]{:S(2)}, u32[]{:S(2)}) collective-permute-start(bf16[16,4096]{1,0:T(8,128)(2,1)S(1)} %get-tuple-element.18.refs_5_), channel_id=1, source_target_pairs={{0,4},{1,17},{2,6},{3,19},{4,0},{5,21},{6,2},{7,23},{8,12},{9,25},... | collective-permute-start | bytes 393224 | tf_op jit(solution)/shard_map/ppermute | solution.py:315
  6.8 6.4 %collective-permute-start.2 = (bf16[16,4096]{1,0:T(8,128)(2,1)S(1)}, bf16[16,4096]{1,0:T(8,128)(2,1)S(1)}, u32[]{:S(2)}, u32[]{:S(2)}) collective-permute-start(bf16[16,4096]{1,0:T(8,128)(2,1)S(1)} %get-tuple-element.18.refs_5_), channel_id=1, source_target_pairs={{0,2},{1,9},{2,0},{3,11},{4,6},{5,13},{6,4},{7,15},{8,10},{9,1},{1... | collective-permute-start | bytes 393224 | tf_op jit(solution)/shard_map/ppermute | solution.py:315
  9.2 4.7 %collective-permute-start.7 = (bf16[16,4096]{1,0:T(8,128)(2,1)S(1)}, bf16[16,4096]{1,0:T(8,128)(2,1)S(1)}, u32[]{:S(2)}, u32[]{:S(2)}) collective-permute-start(bf16[16,4096]{1,0:T(8,128)(2,1)S(1)} %collective-permute-done.4.refs_8_), channel_id=1, source_target_pairs={{0,1},{1,0},{2,3},{3,2},{4,5},{5,4},{6,7},{7,6},{8,9},{9,8},{10,11... | collective-permute-start | bytes 393224 | tf_op jit(solution)/shard_map/ppermute | solution.py:312
  11.2 3.0 %collective-permute-start.6 = (bf16[16,4096]{1,0:T(8,128)(2,1)S(1)}, bf16[16,4096]{1,0:T(8,128)(2,1)S(1)}, u32[]{:S(2)}, u32[]{:S(2)}) collective-permute-start(bf16[16,4096]{1,0:T(8,128)(2,1)S(1)} %collective-permute-done.3.refs_7_), channel_id=1, source_target_pairs={{0,1},{1,0},{2,3},{3,2},{4,5},{5,4},{6,7},{7,6},{8,9},{9,8},{10,11... | collective-permute-start | bytes 393224 | tf_op jit(solution)/shard_map/ppermute | solution.py:312
  13.2 1.3 %collective-permute-start.5 = (bf16[16,4096]{1,0:T(8,128)(2,1)S(1)}, bf16[16,4096]{1,0:T(8,128)(2,1)S(1)}, u32[]{:S(2)}, u32[]{:S(2)}) collective-permute-start(bf16[16,4096]{1,0:T(8,128)(2,1)S(1)} %collective-permute-done.2.refs_6_), channel_id=1, source_target_pairs={{0,1},{1,0},{2,3},{3,2},{4,5},{5,4},{6,7},{7,6},{8,9},{9,8},{10,11... | collective-permute-start | bytes 393224 | tf_op jit(solution)/shard_map/ppermute | solution.py:312
  20.3 1.3 %collective-permute-start.13 = (f32[8,16,128]{2,1,0:T(8,128)S(1)}, f32[8,16,128]{2,1,0:T(8,128)S(1)}, u32[]{:S(2)}, u32[]{:S(2)}) collective-permute-start(f32[8,16,128]{2,1,0:T(8,128)S(1)} %get-tuple-element.27), channel_id=1, source_target_pairs={{0,1},{1,0},{2,3},{3,2},{4,5},{5,4},{6,7},{7,6},{8,9},{9,8},{10,11... | collective-permute-start | bytes 196616 | tf_op jit(solution)/shard_map/ppermute | solution.py:312
  20.6 3.6 %collective-permute-start.11 = (f32[8,16,128]{2,1,0:T(8,128)S(1)}, f32[8,16,128]{2,1,0:T(8,128)S(1)}, u32[]{:S(2)}, u32[]{:S(2)}) collective-permute-start(f32[8,16,128]{2,1,0:T(8,128)S(1)} %get-tuple-element.25), channel_id=1, source_target_pairs={{0,1},{1,0},{2,3},{3,2},{4,5},{5,4},{6,7},{7,6},{8,9},{9,8},{10,11... | collective-permute-start | bytes 196616 | tf_op jit(solution)/shard_map/ppermute | solution.py:312
  20.9 3.7 %collective-permute-start.9 = (f32[8,16,128]{2,1,0:T(8,128)S(1)}, f32[8,16,128]{2,1,0:T(8,128)S(1)}, u32[]{:S(2)}, u32[]{:S(2)}) collective-permute-start(f32[8,16,128]{2,1,0:T(8,128)S(1)} %get-tuple-element.23), channel_id=1, source_target_pairs={{0,1},{1,0},{2,3},{3,2},{4,5},{5,4},{6,7},{7,6},{8,9},{9,8},{10,11... | collective-permute-start | bytes 196616 | tf_op jit(solution)/shard_map/ppermute | solution.py:312
  21.6 5.9 %collective-permute-start.14 = (f32[16,16,128]{2,1,0:T(8,128)S(1)}, f32[16,16,128]{2,1,0:T(8,128)S(1)}, u32[]{:S(2)}, u32[]{:S(2)}) collective-permute-start(f32[16,16,128]{2,1,0:T(8,128)S(1)} %shard_map.92), channel_id=1, source_target_pairs={{0,6},{1,25},{2,4},{3,27},{4,2},{5,29},{6,0},{7,31},{8,14},{9,17},... | collective-permute-start | bytes 393224 | tf_op jit(solution)/shard_map/ppermute | solution.py:315
  24.2 5.0 %collective-permute-start.12 = (f32[16,16,128]{2,1,0:T(8,128)S(1)}, f32[16,16,128]{2,1,0:T(8,128)S(1)}, u32[]{:S(2)}, u32[]{:S(2)}) collective-permute-start(f32[16,16,128]{2,1,0:T(8,128)S(1)} %shard_map.91), channel_id=1, source_target_pairs={{0,4},{1,17},{2,6},{3,19},{4,0},{5,21},{6,2},{7,23},{8,12},{9,25},... | collective-permute-start | bytes 393224 | tf_op jit(solution)/shard_map/ppermute | solution.py:315
  24.6 5.0 %collective-permute-start.10 = (f32[16,16,128]{2,1,0:T(8,128)S(1)}, f32[16,16,128]{2,1,0:T(8,128)S(1)}, u32[]{:S(2)}, u32[]{:S(2)}) collective-permute-start(f32[16,16,128]{2,1,0:T(8,128)S(1)} %shard_map.90), channel_id=1, source_target_pairs={{0,2},{1,9},{2,0},{3,11},{4,6},{5,13},{6,4},{7,15},{8,10},{9,1},{1... | collective-permute-start | bytes 393224 | tf_op jit(solution)/shard_map/ppermute | solution.py:315
  25.4 1.3 %collective-permute-start.8 = (f32[8,16,128]{2,1,0:T(8,128)S(1)}, f32[8,16,128]{2,1,0:T(8,128)S(1)}, u32[]{:S(2)}, u32[]{:S(2)}) collective-permute-start(f32[8,16,128]{2,1,0:T(8,128)S(1)} %get-tuple-element.21), channel_id=1, source_target_pairs={{0,1},{1,0},{2,3},{3,2},{4,5},{5,4},{6,7},{7,6},{8,9},{9,8},{10,11... | collective-permute-start | bytes 196616 | tf_op jit(solution)/shard_map/ppermute | solution.py:312
  29.7 1.7 %collective-permute-start.15 = (f32[8,16,128]{2,1,0:T(8,128)S(1)}, f32[8,16,128]{2,1,0:T(8,128)S(1)}, u32[]{:S(2)}, u32[]{:S(2)}) collective-permute-start(f32[8,16,128]{2,1,0:T(8,128)S(1)} %get-tuple-element.29), channel_id=1, source_target_pairs={{0,1},{1,0},{2,3},{3,2},{4,5},{5,4},{6,7},{7,6},{8,9},{9,8},{10,11... | collective-permute-start | bytes 196616 | tf_op jit(solution)/shard_map/ppermute | solution.py:312

commit v4 on v3

--- a/solution.py
+++ b/solution.py
@@ -10,11 +10,11 @@
 BLK = 128
 REWARDS = 16
 CHUNK = 128
-PART = 32
 SUMS = 1
+GRAIN = 128
+MOST = 32767.0
 LAG = 2
 DEEP = 4
-VMEM_LIMIT = 40 * 2**20
 
 
 def peers(size, step):
@@ -53,6 +53,38 @@
         copy.wait()
 
 
+def prefetch_kernel(after, rows_there, cols_there, reward_cols_there, blocks_there, rows, cols, pick, blocks, reward_cols, sems):
+    pairs = (
+        (reward_cols_there, reward_cols),
+        (rows_there, rows),
+        (cols_there, cols),
+        (blocks_there, blocks),
+    )
+    copies = [pltpu.make_async_copy(there, here, sems.at[at]) for at, (there, here) in enumerate(pairs)]
+    for copy in copies:
+        copy.start()
+    copies[0].wait()
+    own_row = lax.axis_index("row")
+    candidates = pick.shape[1] * REWARDS // pick.shape[0]
+    group = candidates // lax.axis_size("row")
+    lane = lax.broadcasted_iota(jnp.int32, (REWARDS, pick.shape[1]), 1)
+    at = lane % candidates
+    column = at % group + (own_row ^ (at // group)) * group
+    line = lax.broadcasted_iota(jnp.int32, (REWARDS, pick.shape[1]), 0)
+    wanted = jnp.zeros(lane.shape, jnp.int32)
+    for k in range(REWARDS):
+        wanted = jnp.where(line == k, reward_cols[k], wanted)
+    hit = column == wanted
+    bands = [jnp.where(hit & (lane // candidates == band), 1.0, 0.0) for band in range(pick.shape[1] // candidates)]
+    pick[...] = jnp.concatenate(bands, axis=0).astype(jnp.bfloat16)
+    for copy in copies[1:]:
+        copy.wait()
+
+
+def after_kernel(part, after, out):
+    out[...] = part[...]
+
+
 def gather_kernel(shard, table, other_shard, other_table, mine, other):
     core, span, width = lax.axis_index("col") % 2, shard.shape[1], mine.shape[1]
 
@@ -81,29 +113,22 @@
 def products_kernel(n_row, n_col, *refs):
     n_chip = n_col // 2
     steps = max(n_row, n_chip)
-    counts, slot_rows_there, slot_cols_there, reward_cols_there, blocks_there = refs[:5]
+    counts, slot_rows_there, slot_cols_there, pick, blocks = refs[:5]
     mine, others = refs[5 : 5 + steps], refs[5 + steps : 5 + 2 * steps]
     keeps, gives = refs[5 + 2 * steps : 5 + 3 * steps], refs[5 + 3 * steps : 5 + 4 * steps]
     refs = refs[5 + 4 * steps :]
-    slot_rows, slot_cols, reward_cols, blocks, table, weights, rewards = refs[:7]
-    value_sums, grad_sums = refs[7 : 7 + SUMS], refs[7 + SUMS : 7 + 2 * SUMS]
-    sems, block_sems = refs[7 + 2 * SUMS :]
+    slot_rows, slot_cols, table, weights, rewards = refs[:5]
+    value_sums, grad_sums = refs[5 : 5 + SUMS], refs[5 + SUMS : 5 + 2 * SUMS]
+    draft, sems = refs[5 + 2 * SUMS :]
     own_row, own_col = lax.axis_index("row"), lax.axis_index("col")
     own_chip, core = own_col // 2, own_col % 2
     row_cells, col_cells = weights.shape[0] - 1, rewards.shape[0] - 1
 
-    pairs = ((slot_rows_there, slot_rows), (slot_cols_there, slot_cols), (reward_cols_there, reward_cols))
+    pairs = ((slot_rows_there, slot_rows), (slot_cols_there, slot_cols))
     copies = [pltpu.make_async_copy(there, here, sems.at[at]) for at, (there, here) in enumerate(pairs)]
     for copy in copies:
         copy.start()
 
-    def block_copy(part):
-        slots = pl.ds(pl.multiple_of(part * PART, PART), PART)
-        return pltpu.make_async_copy(blocks_there.at[:, :, slots], blocks.at[:, :, slots], block_sems.at[part])
-
-    part_count = blocks.shape[2] // PART
-    for part in range(part_count):
-        block_copy(part).start()
     for sums in (*value_sums, *grad_sums):
         sums[...] = jnp.zeros_like(sums)
     weights[row_cells] = jnp.zeros((REWARDS, BLK), jnp.bfloat16)
@@ -135,20 +160,8 @@
     def _():
         take(others, mine, 1)
 
-    for copy in copies:
-        copy.wait()
-    candidates, side = group * n_row, 2 * BLK
-    bands = side // candidates
-    lane = lax.broadcasted_iota(jnp.int32, (REWARDS, side), 1)
-    at = lane % candidates
-    column = at % group + (own_row ^ (at // group)) * group
-    line = lax.broadcasted_iota(jnp.int32, (REWARDS, side), 0)
-    wanted = jnp.zeros((REWARDS, side), jnp.int32)
-    for k in range(REWARDS):
-        wanted = jnp.where(line == k, reward_cols[k], wanted)
-    hit = column == wanted
-    pick = [jnp.where(hit & (lane // candidates == band), 1.0, 0.0) for band in range(bands)]
-    pick = jnp.concatenate(pick, axis=0).astype(jnp.bfloat16)
+    side = 2 * BLK
+    bands = side // (group * n_row)
 
     def pick_rewards(*units):
         for turn in range(col_cells * BLK // (bands * side)):
@@ -156,7 +169,7 @@
             lanes = [pl.ds((turn * bands + band) * side, side) for band in range(bands)]
             tile = jnp.concatenate([table[:, here] for here in lanes], axis=0).astype(jnp.bfloat16)
             pltpu.matmul_push_rhs(tile, 0, unit)
-            pltpu.matmul_acc_lhs(units[unit], pick, load_staged_rhs=0)
+            pltpu.matmul_acc_lhs(units[unit], pick[...], load_staged_rhs=0)
             product = pltpu.matmul_pop(units[unit]).astype(jnp.bfloat16)
             for cell in range(2 * bands):
                 band, half = divmod(cell, 2)
@@ -166,6 +179,8 @@
 
     pl.run_scoped(pick_rewards, *[pltpu.ACC(unit)((bands * REWARDS, side), jnp.float32) for unit in (0, 1)])
 
+    for copy in copies:
+        copy.wait()
     live_count = counts[0, 0]
 
     def visit(units, chunk, carry):
@@ -180,8 +195,6 @@
 
         for quad in range(CHUNK // 4):
             start = chunk * CHUNK + quad * 4
-            if quad * 4 % PART == 0:
-                block_copy(chunk * (CHUNK // PART) + quad * 4 // PART).wait()
             rows, cols = [], []
             for at in range(4):
                 live = start + at < live_count
@@ -217,22 +230,26 @@
         lax.fori_loop(0, live_chunks, functools.partial(visit, held), 0)
 
     pl.run_scoped(multiply, *[pltpu.ACC(unit)((4 * REWARDS, 2 * BLK), jnp.float32) for unit in (0, 1) for _ in range(DEEP)])
-    lax.fori_loop(
-        live_chunks * (CHUNK // PART), part_count, lambda part, carry: (block_copy(part).wait(), carry)[1], 0
-    )
 
     lines = REWARDS // n_row
     part = row_cells // n_chip
 
     def put_grad(step, out):
+        tiles = out if step == 0 else draft
         for col in range(col_cells):
             here = pl.ds((own_row ^ step) * lines, lines)
             at, line = divmod(col * lines, REWARDS)
-            out[at, line : line + lines, :] = sum(sums[col, here, :] for sums in grad_sums)
+            tiles[at, line : line + lines, :] = sum(sums[col, here, :] for sums in grad_sums)
+        if step:
+            encode(draft, out)
 
     def put_value(step, out):
         cells = pl.ds((own_chip ^ step) * part, part)
-        out[:part] = sum(sums[cells] for sums in value_sums)
+        value = sum(sums[cells] for sums in value_sums)
+        if step:
+            encode(value, out)
+        else:
+            out[...] = value
 
     def put(values, grads):
         for step in range(steps):
@@ -250,6 +267,23 @@
         put(gives, keeps)
 
 
+def encode(tiles, out):
+    values = [tiles[at] for at in range(out.shape[0] - 1)]
+    top = functools.reduce(jnp.maximum, [jnp.abs(value) for value in values])
+    power = jnp.ceil(jnp.log2(jnp.maximum(top, 2.0**-100)) * GRAIN)
+    out[len(values)] = power.astype(jnp.int32).astype(jnp.int16)
+    factor = MOST / jnp.exp2(power / GRAIN)
+    for at, value in enumerate(values):
+        whole = jnp.clip(jnp.round(value * factor), -MOST, MOST)
+        out[at] = whole.astype(jnp.int32).astype(jnp.int16)
+
+
+def decode(coded, first, count):
+    power = coded[first + count].astype(jnp.int32).astype(jnp.float32)
+    factor = jnp.exp2(power / GRAIN) / MOST
+    return [coded[first + at].astype(jnp.int32).astype(jnp.float32) * factor for at in range(count)]
+
+
 def pair_kernel(keep, got, out):
     half = keep.shape[0]
     out[:half], out[half:] = by_core(keep[...], got[...])
@@ -260,17 +294,26 @@
     core = lax.axis_index("col") % 2
     half = keep.shape[0]
 
+    def total(count, side):
+        sums = [parts[0][side * half + at] for at in range(half)]
+        for part in parts[1:count]:
+            arrived = decode(part, side * (half + 1), half)
+            sums = [one + other for one, other in zip(sums, arrived)]
+        return sums
+
     @pl.when(core == 0)
     def _():
-        total = sum(part[...] for part in parts[:n_chip])
         cut = half // 2
-        keep[:cut], keep[cut:] = total[:cut], total[half : half + cut]
-        give[:cut], give[cut:] = total[cut:half], total[half + cut :]
+        for side in range(2):
+            sums = total(n_chip, side)
+            for at in range(cut):
+                keep[side * cut + at], give[side * cut + at] = sums[at], sums[cut + at]
 
     @pl.when(core == 1)
     def _():
-        total = sum(part[...] for part in parts[:n_row])
-        give[...], keep[...] = total[:half], total[half:]
+        for side, out in enumerate((give, keep)):
+            for at, one in enumerate(total(n_row, side)):
+                out[at] = one
 
 
 def result_kernel(keep, got, value, grad):
@@ -332,40 +375,60 @@
         compiler_params=small,
     )(*loaded, swap(cotangent), swap(reward_table))
     mine = [mine] + [cross(mine, step) for step in range(1, steps)]
-    others = [other] + [swap(part) for part in mine[1:]]
+    side = 2 * BLK
+    rows, cols, pick, stored = pl.pallas_call(
+        prefetch_kernel,
+        out_shape=[
+            jax.ShapeDtypeStruct(slot_rows.shape, slot_rows.dtype),
+            jax.ShapeDtypeStruct(slot_cols.shape, slot_cols.dtype),
+            jax.ShapeDtypeStruct((side // (reward_table.shape[0] * n_row) * REWARDS, side), jnp.bfloat16),
+            jax.ShapeDtypeStruct(blocks.shape, blocks.dtype),
+        ],
+        in_specs=[vmem] + [hbm] * 4,
+        out_specs=[vmem] * 4,
+        scratch_shapes=[pltpu.SMEM(reward_cols.shape, jnp.int32), pltpu.SemaphoreType.DMA((4,))],
+        compiler_params=pltpu.CompilerParams(vmem_limit_bytes=24 * 2**20),
+        cost_estimate=pl.CostEstimate(flops=0, bytes_accessed=2 * blocks.size * 2, transcendentals=0),
+    )(mine[0], *map(in_hbm, (slot_rows, slot_cols, reward_cols, blocks)))
+    first = pl.pallas_call(
+        after_kernel,
+        out_shape=jax.ShapeDtypeStruct(mine[-1].shape, mine[-1].dtype),
+        in_specs=[vmem] * 2,
+        out_specs=vmem,
+        compiler_params=small,
+    )(mine[-1], pick)
+    others = [other] + [swap(part) for part in (*mine[1:-1], first)]
 
     lines, part = REWARDS // n_row, row_cells // n_chip
     tiles = jax.ShapeDtypeStruct((max(part, col_cells * lines // REWARDS), REWARDS, BLK), jnp.float32)
-    both = jax.ShapeDtypeStruct((2 * tiles.shape[0], REWARDS, BLK), jnp.float32)
+    coded = jax.ShapeDtypeStruct((tiles.shape[0] + 1, REWARDS, BLK), jnp.int16)
     sums = pl.pallas_call(
         functools.partial(products_kernel, n_row, n_col),
-        out_shape=[tiles] * (2 * steps),
-        in_specs=[smem] + [hbm] * 4 + [vmem] * (2 * steps),
+        out_shape=[tiles, *[coded] * (steps - 1)] * 2,
+        in_specs=[smem] + [vmem] * (4 + 2 * steps),
         out_specs=[vmem] * (2 * steps),
         scratch_shapes=[
             pltpu.SMEM(slot_rows.shape, jnp.int32),
             pltpu.SMEM(slot_cols.shape, jnp.int32),
-            pltpu.SMEM(reward_cols.shape, jnp.int32),
-            pltpu.VMEM(blocks.shape, blocks.dtype),
             pltpu.VMEM((reward_table.shape[0] * n_row, col_cells * BLK), jnp.float32),
             pltpu.VMEM((row_cells + 1, REWARDS, BLK), jnp.bfloat16),
             pltpu.VMEM((col_cells + 1, REWARDS, BLK), jnp.bfloat16),
             *[pltpu.VMEM((row_cells + 1, REWARDS, BLK), jnp.float32)] * SUMS,
             *[pltpu.VMEM((col_cells + 1, REWARDS, BLK), jnp.float32)] * SUMS,
-            pltpu.SemaphoreType.DMA((3,)),
-            pltpu.SemaphoreType.DMA((blocks.shape[2] // PART,)),
+            pltpu.VMEM(tiles.shape, jnp.float32),
+            pltpu.SemaphoreType.DMA((2,)),
         ],
-        compiler_params=pltpu.CompilerParams(vmem_limit_bytes=VMEM_LIMIT),
+        compiler_params=pltpu.CompilerParams(vmem_limit_bytes=24 * 2**20),
         cost_estimate=pl.CostEstimate(
             flops=4 * REWARDS * blocks.size, bytes_accessed=4 * blocks.size, transcendentals=0
         ),
-    )(counts, *map(in_hbm, (slot_rows, slot_cols, reward_cols, blocks)), *mine, *others)
+    )(counts, rows, cols, pick, stored, *mine, *others)
     keeps, gives = sums[:steps], sums[steps:]
     parts = []
     for step in reversed(range(steps)):
         pair = pl.pallas_call(
             pair_kernel,
-            out_shape=both,
+            out_shape=jax.ShapeDtypeStruct((2 * keeps[step].shape[0], REWARDS, BLK), keeps[step].dtype),
             in_specs=[vmem] * 2,
             out_specs=vmem,
             compiler_params=small,

time: 31.9 us -> 30.4 us (0.953)
  waiting for transfers between devices: 10.1 us -> 7.08 us
  starting transfers between devices: 13.1 us -> 13.9 us
  Pallas kernels: 7.39 us -> 8.04 us
    pallas_call x4 -> x6, Pallas kernels: 0.07 us -> 3.53 us  [the longest x1 3.45 us: on_device(): pl.pallas_call(prefetch_kernel, out_shape=[jax.ShapeDtypeStruct(slot_rows...]
    pallas_call x1, Pallas kernels: 5.74 us -> 2.89 us  [on_device(): pl.pallas_call(functools.partial(products_kernel, n_row, n_col), out_shap...]
    ppermute x6, waiting for transfers between devices: 6.56 us -> 3.8 us  [cross(): return lax.ppermute(part, ('row', 'col'), crossings(n_row, n_col, step))]
    ppermute x10, starting transfers between devices: 5.14 us -> 5.98 us  [swap(): return lax.ppermute(part, 'col', peers(n_col, 1))]
  transfers between devices with their start and end apart: 16 -> 16, of which waited for: 11 -> 9; matrix products, arithmetic and copies ran while one was open for 0% -> 0% of each run, Pallas kernels for 3% -> 14%
where the time goes in v4:
time: 30.4 us; the launch traced here: 30.5 us
  starting transfers between devices  13.9 us (46%)
  Pallas kernels  8.04 us (26%)
  waiting for transfers between devices  7.08 us (23%)
  between operations  1.39 us (5%)
    ppermute x6, starting transfers between devices, cross(): return lax.ppermute(part, ('row', 'col'), crossings(n_row, n_col, step))  7.97 us
    ppermute x10, starting transfers between devices, swap(): return lax.ppermute(part, 'col', peers(n_col, 1))  5.98 us
    ppermute x6, waiting for transfers between devices, cross(): return lax.ppermute(part, ('row', 'col'), crossings(n_row, n_col, step))  3.8 us
    pallas_call x1, Pallas kernels, on_device(): pl.pallas_call(prefetch_kernel, out_shape=[jax.ShapeDtypeStruct(slot_rows...  3.45 us
    ppermute x10, waiting for transfers between devices, swap(): return lax.ppermute(part, 'col', peers(n_col, 1))  3.28 us
    pallas_call x1, Pallas kernels, on_device(): pl.pallas_call(functools.partial(products_kernel, n_row, n_col), out_shap...  2.89 us
    pallas_call x1, Pallas kernels, on_device(): pl.pallas_call(load_kernel, out_shape=[jax.ShapeDtypeStruct(arg.shape, ar...  0.88 us
    pallas_call x1, Pallas kernels, on_device(): pl.pallas_call(result_kernel, out_shape=[jax.ShapeDtypeStruct((REWARDS, p...  0.66 us
  transfers between devices with their start and end apart: 16, of which 9 were waited for; matrix products, arithmetic and copies ran while one was open for 0% of the time, Pallas kernels for 14%

profile of v4, /device:TPU:0, one launch (start us, length us, event | category | flops | bytes accessed | tf_op | source)
XLA Modules:
  0.0 30.5 jit_solution(13744372013420852509)
XLA Ops:
  0.6 0.5 %collective-permute-start.1 = (bf16[8,4096]{1,0:T(8,128)(2,1)}, bf16[8,4096]{1,0:T(8,128)(2,1)S(1)}, u32[]{:S(2)}, u32[]{:S(2)}) collective-permute-start(bf16[8,4096]{1,0:T(8,128)(2,1)} %table_there.1), channel_id=1, source_target_pairs={{0,1},{1,0},{2,3},{3,2},{4,5},{5,4},{6,7},{7,6},{8,9},{9,8},{10,11... | collective-permute-start | bytes 196616 | tf_op jit(solution)/shard_map/ppermute | solution.py:355
  1.1 0.1 collective-permute-start
  1.2 0.9 %shard_map.86 = (bf16[16,1024]{1,0:T(8,128)(2,1)S(1)}, bf16[8,4096]{1,0:T(8,128)(2,1)S(1)}) custom-call(bf16[16,1024]{1,0:T(8,128)(2,1)} %shard_there.1, bf16[8,4096]{1,0:T(8,128)(2,1)} %table_there.1), custom_call_target="tpu_custom_call" | custom-call | bytes 4194304 | tf_op jit(solution)/shard_map/pallas_call | solution.py:361
  2.1 0.5 %collective-permute-done.other_shard = bf16[16,1024]{1,0:T(8,128)(2,1)S(1)} collective-permute-done((bf16[16,1024]{1,0:T(8,128)(2,1)}, bf16[16,1024]{1,0:T(8,128)(2,1)S(1)}, u32[]{:S(2)}, u32[]{:S(2)}) %collective-permute-start) | collective-permute-done | bytes 32800 | tf_op jit(solution)/shard_map/ppermute | solution.py:355
  2.6 0.0 collective-permute-done.1.other_table
  2.6 2.7 %collective-permute-start.3 = (bf16[16,4096]{1,0:T(8,128)(2,1)S(1)}, bf16[16,4096]{1,0:T(8,128)(2,1)S(1)}, u32[]{:S(2)}, u32[]{:S(2)}) collective-permute-start(bf16[16,4096]{1,0:T(8,128)(2,1)S(1)} %get-tuple-element.22.after.refs_5_), channel_id=1, source_target_pairs={{0,4},{1,17},{2,6},{3,19},{4,0},{5,21},{6,2},{7,23},{8,12},{9,25},... | collective-permute-start | bytes 393224 | tf_op jit(solution)/shard_map/ppermute | solution.py:358
  5.3 1.5 %collective-permute-start.2 = (bf16[16,4096]{1,0:T(8,128)(2,1)S(1)}, bf16[16,4096]{1,0:T(8,128)(2,1)S(1)}, u32[]{:S(2)}, u32[]{:S(2)}) collective-permute-start(bf16[16,4096]{1,0:T(8,128)(2,1)S(1)} %get-tuple-element.22.after.refs_5_), channel_id=1, source_target_pairs={{0,2},{1,9},{2,0},{3,11},{4,6},{5,13},{6,4},{7,15},{8,10},{9,1},{1... | collective-permute-start | bytes 393224 | tf_op jit(solution)/shard_map/ppermute | solution.py:358
  6.8 0.0 collective-permute-start.4
  6.9 3.4 %shard_map.88 = (s32[1,1,256]{2,1,0:T(1,128)S(1)}, s32[1,1,256]{2,1,0:T(1,128)S(1)}, bf16[128,256]{1,0:T(8,128)(2,1)S(1)}, bf16[1,1,256,128,128]{4,3,2,1,0:T(8,128)(2,1)S(1)}) custom-call(bf16[16,4096]{1,0:T(8,128)(2,1)S(1)} %get-tuple-element.22.after.refs_5_, s32[1,1,256]{2,1,0:T(1,128)} %rows_there.1, s32[1,1,256]{2,1,0:T(1,128)} %cols_there.1, ...), custom_call_target="tpu_custom_call" | custom-call | bytes 16777216 | tf_op jit(solution)/shard_map/pallas_call | solution.py:379
  10.3 0.0 collective-permute-done.3.refs_7_
  10.3 1.0 %collective-permute-start.6 = (bf16[16,4096]{1,0:T(8,128)(2,1)S(1)}, bf16[16,4096]{1,0:T(8,128)(2,1)S(1)}, u32[]{:S(2)}, u32[]{:S(2)}) collective-permute-start(bf16[16,4096]{1,0:T(8,128)(2,1)S(1)} %collective-permute-done.3.refs_7_), channel_id=1, source_target_pairs={{0,1},{1,0},{2,3},{3,2},{4,5},{5,4},{6,7},{7,6},{8,9},{9,8},{10,11... | collective-permute-start | bytes 393224 | tf_op jit(solution)/shard_map/ppermute | solution.py:355
  11.3 0.0 collective-permute-done.2.refs_6_
  11.3 0.1 collective-permute-start.5
  11.4 1.3 %collective-permute-done.4.part.refs_8_ = bf16[16,4096]{1,0:T(8,128)(2,1)S(1)} collective-permute-done((bf16[16,4096]{1,0:T(8,128)(2,1)S(1)}, bf16[16,4096]{1,0:T(8,128)(2,1)S(1)}, u32[]{:S(2)}, u32[]{:S(2)}) %collective-permute-start.4) | collective-permute-done | bytes 131104 | tf_op jit(solution)/shard_map/ppermute | solution.py:358
  12.7 0.8 %collective-permute-start.7 = (bf16[16,4096]{1,0:T(8,128)(2,1)S(1)}, bf16[16,4096]{1,0:T(8,128)(2,1)S(1)}, u32[]{:S(2)}, u32[]{:S(2)}) collective-permute-start(bf16[16,4096]{1,0:T(8,128)(2,1)S(1)} %shard_map.89), channel_id=1, source_target_pairs={{0,1},{1,0},{2,3},{3,2},{4,5},{5,4},{6,7},{7,6},{8,9},{9,8},{10,11... | collective-permute-start | bytes 393224 | tf_op jit(solution)/shard_map/ppermute | solution.py:355
  14.1 0.0 collective-permute-done.6.refs_11_
  14.1 0.0 collective-permute-done.5.refs_10_
  14.1 0.3 %collective-permute-done.7.refs_12_ = bf16[16,4096]{1,0:T(8,128)(2,1)S(1)} collective-permute-done((bf16[16,4096]{1,0:T(8,128)(2,1)S(1)}, bf16[16,4096]{1,0:T(8,128)(2,1)S(1)}, u32[]{:S(2)}, u32[]{:S(2)}) %collective-permute-start.7) | collective-permute-done | bytes 131104 | tf_op jit(solution)/shard_map/ppermute | solution.py:355
  14.4 2.9 %shard_map.90 = (f32[8,16,128]{2,1,0:T(8,128)S(1)}, s16[9,16,128]{2,1,0:T(8,128)(2,1)S(1)}, s16[9,16,128]{2,1,0:T(8,128)(2,1)S(1)}, s16[9,16,128]{2,1,0:T(8,128)...) custom-call(s32[1,1]{1,0:T(1,128)S(6)} %copy.9.refs_0_, ...), custom_call_target="tpu_custom_call" | custom-call | flops 268435456 | bytes 16777216 | tf_op jit(solution)/shard_map/pallas_call | solution.py:405
  17.3 2.6 %collective-permute-start.13 = (s16[9,16,128]{2,1,0:T(8,128)(2,1)S(1)}, s16[9,16,128]{2,1,0:T(8,128)(2,1)S(1)}, u32[]{:S(2)}, u32[]{:S(2)}) collective-permute-start(s16[9,16,128]{2,1,0:T(8,128)(2,1)S(1)} %get-tuple-element.35), channel_id=1, source_target_pairs={{0,1},{1,0},{2,3},{3,2},{4,5},{5,4},{6,7},{7,6},{8,9},{9,8},{10,11... | collective-permute-start | bytes 110600 | tf_op jit(solution)/shard_map/ppermute | solution.py:355
  19.9 0.1 collective-permute-start.11
  20.0 0.4 %collective-permute-start.9 = (s16[9,16,128]{2,1,0:T(8,128)(2,1)S(1)}, s16[9,16,128]{2,1,0:T(8,128)(2,1)S(1)}, u32[]{:S(2)}, u32[]{:S(2)}) collective-permute-start(s16[9,16,128]{2,1,0:T(8,128)(2,1)S(1)} %get-tuple-element.31), channel_id=1, source_target_pairs={{0,1},{1,0},{2,3},{3,2},{4,5},{5,4},{6,7},{7,6},{8,9},{9,8},{10,11... | collective-permute-start | bytes 110600 | tf_op jit(solution)/shard_map/ppermute | solution.py:355
  20.5 0.4 %collective-permute-done.13.got = s16[9,16,128]{2,1,0:T(8,128)(2,1)S(1)} collective-permute-done((s16[9,16,128]{2,1,0:T(8,128)(2,1)S(1)}, s16[9,16,128]{2,1,0:T(8,128)(2,1)S(1)}, u32[]{:S(2)}, u32[]{:S(2)}) %collective-permute-start.13) | collective-permute-done | bytes 36896 | tf_op jit(solution)/shard_map/ppermute | solution.py:355
  20.8 2.4 %collective-permute-start.14 = (s16[18,16,128]{2,1,0:T(8,128)(2,1)S(1)}, s16[18,16,128]{2,1,0:T(8,128)(2,1)S(1)}, u32[]{:S(2)}, u32[]{:S(2)}) collective-permute-start(s16[18,16,128]{2,1,0:T(8,128)(2,1)S(1)} %shard_map.94), channel_id=1, source_target_pairs={{0,6},{1,25},{2,4},{3,27},{4,2},{5,29},{6,0},{7,31},{8,14},{9,17},... | collective-permute-start | bytes 221192 | tf_op jit(solution)/shard_map/ppermute | solution.py:358
  23.2 0.0 collective-permute-done.11.got
  23.3 0.7 %collective-permute-start.12 = (s16[18,16,128]{2,1,0:T(8,128)(2,1)S(1)}, s16[18,16,128]{2,1,0:T(8,128)(2,1)S(1)}, u32[]{:S(2)}, u32[]{:S(2)}) collective-permute-start(s16[18,16,128]{2,1,0:T(8,128)(2,1)S(1)} %shard_map.93), channel_id=1, source_target_pairs={{0,4},{1,17},{2,6},{3,19},{4,0},{5,21},{6,2},{7,23},{8,12},{9,25},... | collective-permute-start | bytes 221192 | tf_op jit(solution)/shard_map/ppermute | solution.py:358
  24.0 0.0 collective-permute-done.9.got
  24.0 0.6 %collective-permute-start.10 = (s16[18,16,128]{2,1,0:T(8,128)(2,1)S(1)}, s16[18,16,128]{2,1,0:T(8,128)(2,1)S(1)}, u32[]{:S(2)}, u32[]{:S(2)}) collective-permute-start(s16[18,16,128]{2,1,0:T(8,128)(2,1)S(1)} %shard_map.92), channel_id=1, source_target_pairs={{0,2},{1,9},{2,0},{3,11},{4,6},{5,13},{6,4},{7,15},{8,10},{9,1},{1... | collective-permute-start | bytes 221192 | tf_op jit(solution)/shard_map/ppermute | solution.py:358
  24.6 0.4 %collective-permute-start.8 = (f32[8,16,128]{2,1,0:T(8,128)S(1)}, f32[8,16,128]{2,1,0:T(8,128)S(1)}, u32[]{:S(2)}, u32[]{:S(2)}) collective-permute-start(f32[8,16,128]{2,1,0:T(8,128)S(1)} %get-tuple-element.29), channel_id=1, source_target_pairs={{0,1},{1,0},{2,3},{3,2},{4,5},{5,4},{6,7},{7,6},{8,9},{9,8},{10,11... | collective-permute-start | bytes 196616 | tf_op jit(solution)/shard_map/ppermute | solution.py:355
  25.0 0.9 %collective-permute-done.8.got = f32[8,16,128]{2,1,0:T(8,128)S(1)} collective-permute-done((f32[8,16,128]{2,1,0:T(8,128)S(1)}, f32[8,16,128]{2,1,0:T(8,128)S(1)}, u32[]{:S(2)}, u32[]{:S(2)}) %collective-permute-start.8) | collective-permute-done | bytes 65568 | tf_op jit(solution)/shard_map/ppermute | solution.py:355
  25.9 0.2 collective-permute-done.14.refs_3_
  26.1 1.5 %collective-permute-done.12.refs_2_ = s16[18,16,128]{2,1,0:T(8,128)(2,1)S(1)} collective-permute-done((s16[18,16,128]{2,1,0:T(8,128)(2,1)S(1)}, s16[18,16,128]{2,1,0:T(8,128)(2,1)S(1)}, u32[]{:S(2)}, u32[]{:S(2)}) %collective-permute-start.12) | collective-permute-done | bytes 73760 | tf_op jit(solution)/shard_map/ppermute | solution.py:358
  27.7 0.7 %collective-permute-done.10.refs_1_ = s16[18,16,128]{2,1,0:T(8,128)(2,1)S(1)} collective-permute-done((s16[18,16,128]{2,1,0:T(8,128)(2,1)S(1)}, s16[18,16,128]{2,1,0:T(8,128)(2,1)S(1)}, u32[]{:S(2)}, u32[]{:S(2)}) %collective-permute-start.10) | collective-permute-done | bytes 73760 | tf_op jit(solution)/shard_map/ppermute | solution.py:358
  28.4 0.1 shard_map.95
  28.5 0.1 collective-permute-start.15
  28.6 1.2 %collective-permute-done.15.got = f32[8,16,128]{2,1,0:T(8,128)S(1)} collective-permute-done((f32[8,16,128]{2,1,0:T(8,128)S(1)}, f32[8,16,128]{2,1,0:T(8,128)S(1)}, u32[]{:S(2)}, u32[]{:S(2)}) %collective-permute-start.15) | collective-permute-done | bytes 65568 | tf_op jit(solution)/shard_map/ppermute | solution.py:355
  29.8 0.7 %shard_map.96 = (f32[16,1024]{1,0:T(8,128)}, f32[4,4096]{1,0:T(4,128)}) custom-call(f32[8,16,128]{2,1,0:T(8,128)S(1)} %get-tuple-element.36.keep, f32[8,16,128]{2,1,0:T(8,128)S(1)} %collective-permute-done.15.got), custom_call_target="tpu_custom_call" | custom-call | tf_op jit(solution)/shard_map/pallas_call | solution.py:444
  (6 shorter events, 0.1 us)
Async XLA Ops:
  0.6 1.9 %collective-permute-start.1 = (bf16[8,4096]{1,0:T(8,128)(2,1)}, bf16[8,4096]{1,0:T(8,128)(2,1)S(1)}, u32[]{:S(2)}, u32[]{:S(2)}) collective-permute-start(bf16[8,4096]{1,0:T(8,128)(2,1)} %table_there.1), channel_id=1, source_target_pairs={{0,1},{1,0},{2,3},{3,2},{4,5},{5,4},{6,7},{7,6},{8,9},{9,8},{10,11... | collective-permute-start | bytes 196616 | tf_op jit(solution)/shard_map/ppermute | solution.py:355
  1.1 1.4 %collective-permute-start = (bf16[16,1024]{1,0:T(8,128)(2,1)}, bf16[16,1024]{1,0:T(8,128)(2,1)S(1)}, u32[]{:S(2)}, u32[]{:S(2)}) collective-permute-start(bf16[16,1024]{1,0:T(8,128)(2,1)} %shard_there.1), channel_id=1, source_target_pairs={{0,1},{1,0},{2,3},{3,2},{4,5},{5,4},{6,7},{7,6},{8,9},{9,8},{10,11... | collective-permute-start | bytes 98312 | tf_op jit(solution)/shard_map/ppermute | solution.py:355
  2.6 7.7 %collective-permute-start.3 = (bf16[16,4096]{1,0:T(8,128)(2,1)S(1)}, bf16[16,4096]{1,0:T(8,128)(2,1)S(1)}, u32[]{:S(2)}, u32[]{:S(2)}) collective-permute-start(bf16[16,4096]{1,0:T(8,128)(2,1)S(1)} %get-tuple-element.22.after.refs_5_), channel_id=1, source_target_pairs={{0,4},{1,17},{2,6},{3,19},{4,0},{5,21},{6,2},{7,23},{8,12},{9,25},... | collective-permute-start | bytes 393224 | tf_op jit(solution)/shard_map/ppermute | solution.py:358
  5.3 6.0 %collective-permute-start.2 = (bf16[16,4096]{1,0:T(8,128)(2,1)S(1)}, bf16[16,4096]{1,0:T(8,128)(2,1)S(1)}, u32[]{:S(2)}, u32[]{:S(2)}) collective-permute-start(bf16[16,4096]{1,0:T(8,128)(2,1)S(1)} %get-tuple-element.22.after.refs_5_), channel_id=1, source_target_pairs={{0,2},{1,9},{2,0},{3,11},{4,6},{5,13},{6,4},{7,15},{8,10},{9,1},{1... | collective-permute-start | bytes 393224 | tf_op jit(solution)/shard_map/ppermute | solution.py:358
  6.8 5.9 %collective-permute-start.4 = (bf16[16,4096]{1,0:T(8,128)(2,1)S(1)}, bf16[16,4096]{1,0:T(8,128)(2,1)S(1)}, u32[]{:S(2)}, u32[]{:S(2)}) collective-permute-start(bf16[16,4096]{1,0:T(8,128)(2,1)S(1)} %get-tuple-element.22.after.refs_5_), channel_id=1, source_target_pairs={{0,6},{1,25},{2,4},{3,27},{4,2},{5,29},{6,0},{7,31},{8,14},{9,17},... | collective-permute-start | bytes 393224 | tf_op jit(solution)/shard_map/ppermute | solution.py:358
  10.3 3.8 %collective-permute-start.6 = (bf16[16,4096]{1,0:T(8,128)(2,1)S(1)}, bf16[16,4096]{1,0:T(8,128)(2,1)S(1)}, u32[]{:S(2)}, u32[]{:S(2)}) collective-permute-start(bf16[16,4096]{1,0:T(8,128)(2,1)S(1)} %collective-permute-done.3.refs_7_), channel_id=1, source_target_pairs={{0,1},{1,0},{2,3},{3,2},{4,5},{5,4},{6,7},{7,6},{8,9},{9,8},{10,11... | collective-permute-start | bytes 393224 | tf_op jit(solution)/shard_map/ppermute | solution.py:355
  11.3 2.8 %collective-permute-start.5 = (bf16[16,4096]{1,0:T(8,128)(2,1)S(1)}, bf16[16,4096]{1,0:T(8,128)(2,1)S(1)}, u32[]{:S(2)}, u32[]{:S(2)}) collective-permute-start(bf16[16,4096]{1,0:T(8,128)(2,1)S(1)} %collective-permute-done.2.refs_6_), channel_id=1, source_target_pairs={{0,1},{1,0},{2,3},{3,2},{4,5},{5,4},{6,7},{7,6},{8,9},{9,8},{10,11... | collective-permute-start | bytes 393224 | tf_op jit(solution)/shard_map/ppermute | solution.py:355
  12.7 1.7 %collective-permute-start.7 = (bf16[16,4096]{1,0:T(8,128)(2,1)S(1)}, bf16[16,4096]{1,0:T(8,128)(2,1)S(1)}, u32[]{:S(2)}, u32[]{:S(2)}) collective-permute-start(bf16[16,4096]{1,0:T(8,128)(2,1)S(1)} %shard_map.89), channel_id=1, source_target_pairs={{0,1},{1,0},{2,3},{3,2},{4,5},{5,4},{6,7},{7,6},{8,9},{9,8},{10,11... | collective-permute-start | bytes 393224 | tf_op jit(solution)/shard_map/ppermute | solution.py:355
  17.3 3.5 %collective-permute-start.13 = (s16[9,16,128]{2,1,0:T(8,128)(2,1)S(1)}, s16[9,16,128]{2,1,0:T(8,128)(2,1)S(1)}, u32[]{:S(2)}, u32[]{:S(2)}) collective-permute-start(s16[9,16,128]{2,1,0:T(8,128)(2,1)S(1)} %get-tuple-element.35), channel_id=1, source_target_pairs={{0,1},{1,0},{2,3},{3,2},{4,5},{5,4},{6,7},{7,6},{8,9},{9,8},{10,11... | collective-permute-start | bytes 110600 | tf_op jit(solution)/shard_map/ppermute | solution.py:355
  19.9 3.3 %collective-permute-start.11 = (s16[9,16,128]{2,1,0:T(8,128)(2,1)S(1)}, s16[9,16,128]{2,1,0:T(8,128)(2,1)S(1)}, u32[]{:S(2)}, u32[]{:S(2)}) collective-permute-start(s16[9,16,128]{2,1,0:T(8,128)(2,1)S(1)} %get-tuple-element.33), channel_id=1, source_target_pairs={{0,1},{1,0},{2,3},{3,2},{4,5},{5,4},{6,7},{7,6},{8,9},{9,8},{10,11... | collective-permute-start | bytes 110600 | tf_op jit(solution)/shard_map/ppermute | solution.py:355
  20.0 3.9 %collective-permute-start.9 = (s16[9,16,128]{2,1,0:T(8,128)(2,1)S(1)}, s16[9,16,128]{2,1,0:T(8,128)(2,1)S(1)}, u32[]{:S(2)}, u32[]{:S(2)}) collective-permute-start(s16[9,16,128]{2,1,0:T(8,128)(2,1)S(1)} %get-tuple-element.31), channel_id=1, source_target_pairs={{0,1},{1,0},{2,3},{3,2},{4,5},{5,4},{6,7},{7,6},{8,9},{9,8},{10,11... | collective-permute-start | bytes 110600 | tf_op jit(solution)/shard_map/ppermute | solution.py:355
  20.8 5.3 %collective-permute-start.14 = (s16[18,16,128]{2,1,0:T(8,128)(2,1)S(1)}, s16[18,16,128]{2,1,0:T(8,128)(2,1)S(1)}, u32[]{:S(2)}, u32[]{:S(2)}) collective-permute-start(s16[18,16,128]{2,1,0:T(8,128)(2,1)S(1)} %shard_map.94), channel_id=1, source_target_pairs={{0,6},{1,25},{2,4},{3,27},{4,2},{5,29},{6,0},{7,31},{8,14},{9,17},... | collective-permute-start | bytes 221192 | tf_op jit(solution)/shard_map/ppermute | solution.py:358
  23.3 4.4 %collective-permute-start.12 = (s16[18,16,128]{2,1,0:T(8,128)(2,1)S(1)}, s16[18,16,128]{2,1,0:T(8,128)(2,1)S(1)}, u32[]{:S(2)}, u32[]{:S(2)}) collective-permute-start(s16[18,16,128]{2,1,0:T(8,128)(2,1)S(1)} %shard_map.93), channel_id=1, source_target_pairs={{0,4},{1,17},{2,6},{3,19},{4,0},{5,21},{6,2},{7,23},{8,12},{9,25},... | collective-permute-start | bytes 221192 | tf_op jit(solution)/shard_map/ppermute | solution.py:358
  24.0 4.4 %collective-permute-start.10 = (s16[18,16,128]{2,1,0:T(8,128)(2,1)S(1)}, s16[18,16,128]{2,1,0:T(8,128)(2,1)S(1)}, u32[]{:S(2)}, u32[]{:S(2)}) collective-permute-start(s16[18,16,128]{2,1,0:T(8,128)(2,1)S(1)} %shard_map.92), channel_id=1, source_target_pairs={{0,2},{1,9},{2,0},{3,11},{4,6},{5,13},{6,4},{7,15},{8,10},{9,1},{1... | collective-permute-start | bytes 221192 | tf_op jit(solution)/shard_map/ppermute | solution.py:358
  24.6 1.3 %collective-permute-start.8 = (f32[8,16,128]{2,1,0:T(8,128)S(1)}, f32[8,16,128]{2,1,0:T(8,128)S(1)}, u32[]{:S(2)}, u32[]{:S(2)}) collective-permute-start(f32[8,16,128]{2,1,0:T(8,128)S(1)} %get-tuple-element.29), channel_id=1, source_target_pairs={{0,1},{1,0},{2,3},{3,2},{4,5},{5,4},{6,7},{7,6},{8,9},{9,8},{10,11... | collective-permute-start | bytes 196616 | tf_op jit(solution)/shard_map/ppermute | solution.py:355
  28.5 1.3 %collective-permute-start.15 = (f32[8,16,128]{2,1,0:T(8,128)S(1)}, f32[8,16,128]{2,1,0:T(8,128)S(1)}, u32[]{:S(2)}, u32[]{:S(2)}) collective-permute-start(f32[8,16,128]{2,1,0:T(8,128)S(1)} %get-tuple-element.37), channel_id=1, source_target_pairs={{0,1},{1,0},{2,3},{3,2},{4,5},{5,4},{6,7},{7,6},{8,9},{9,8},{10,11... | collective-permute-start | bytes 196616 | tf_op jit(solution)/shard_map/ppermute | solution.py:355

commit v5 on v4

--- a/solution.py
+++ b/solution.py
@@ -9,10 +9,11 @@
 
 BLK = 128
 REWARDS = 16
-CHUNK = 128
+LATE = 128
 SUMS = 1
 GRAIN = 128
 MOST = 32767.0
+SPARE = 8
 LAG = 2
 DEEP = 4
 
@@ -58,7 +59,7 @@
         (reward_cols_there, reward_cols),
         (rows_there, rows),
         (cols_there, cols),
-        (blocks_there, blocks),
+        (blocks_there.at[:, :, pl.ds(0, blocks.shape[2])], blocks),
     )
     copies = [pltpu.make_async_copy(there, here, sems.at[at]) for at, (there, here) in enumerate(pairs)]
     for copy in copies:
@@ -113,26 +114,25 @@
 def products_kernel(n_row, n_col, *refs):
     n_chip = n_col // 2
     steps = max(n_row, n_chip)
-    counts, slot_rows_there, slot_cols_there, pick, blocks = refs[:5]
-    mine, others = refs[5 : 5 + steps], refs[5 + steps : 5 + 2 * steps]
-    keeps, gives = refs[5 + 2 * steps : 5 + 3 * steps], refs[5 + 3 * steps : 5 + 4 * steps]
-    refs = refs[5 + 4 * steps :]
-    slot_rows, slot_cols, table, weights, rewards = refs[:5]
-    value_sums, grad_sums = refs[5 : 5 + SUMS], refs[5 + SUMS : 5 + 2 * SUMS]
-    draft, sems = refs[5 + 2 * SUMS :]
+    counts, slot_rows, slot_cols, blocks_there, pick, blocks = refs[:6]
+    mine, others = refs[6 : 6 + steps], refs[6 + steps : 6 + 2 * steps]
+    keeps, gives = refs[6 + 2 * steps : 6 + 3 * steps], refs[6 + 3 * steps : 6 + 4 * steps]
+    refs = refs[6 + 4 * steps :]
+    table, weights, rewards = refs[:3]
+    value_sums, grad_sums = refs[3 : 3 + SUMS], refs[3 + SUMS : 3 + 2 * SUMS]
+    draft, late, late_sem = refs[3 + 2 * SUMS :]
     own_row, own_col = lax.axis_index("row"), lax.axis_index("col")
     own_chip, core = own_col // 2, own_col % 2
-    row_cells, col_cells = weights.shape[0] - 1, rewards.shape[0] - 1
-
-    pairs = ((slot_rows_there, slot_rows), (slot_cols_there, slot_cols))
-    copies = [pltpu.make_async_copy(there, here, sems.at[at]) for at, (there, here) in enumerate(pairs)]
-    for copy in copies:
-        copy.start()
-
+    row_cells, col_cells = weights.shape[0] - SPARE, rewards.shape[0] - SPARE
+
+    early = blocks.shape[2]
+    late_copy = pltpu.make_async_copy(blocks_there.at[:, :, pl.ds(early, LATE)], late, late_sem)
+    late_copy.start()
     for sums in (*value_sums, *grad_sums):
         sums[...] = jnp.zeros_like(sums)
-    weights[row_cells] = jnp.zeros((REWARDS, BLK), jnp.bfloat16)
-    rewards[col_cells] = jnp.zeros((REWARDS, BLK), jnp.bfloat16)
+    for spare in range(SPARE):
+        weights[row_cells + spare] = jnp.zeros((REWARDS, BLK), jnp.bfloat16)
+        rewards[col_cells + spare] = jnp.zeros((REWARDS, BLK), jnp.bfloat16)
 
     owned = row_cells // n_col
     group = table.shape[0] // n_row
@@ -179,11 +179,10 @@
 
     pl.run_scoped(pick_rewards, *[pltpu.ACC(unit)((bands * REWARDS, side), jnp.float32) for unit in (0, 1)])
 
-    for copy in copies:
-        copy.wait()
     live_count = counts[0, 0]
 
-    def visit(units, chunk, carry):
+    def multiply(*held):
+        units = (held[:DEEP], held[DEEP:])
         queued = []
 
         def add_next():
@@ -193,14 +192,17 @@
                 part = product[piece * REWARDS : (piece + 1) * REWARDS, side * BLK : (side + 1) * BLK]
                 totals[at % SUMS][cells[at]] += part
 
-        for quad in range(CHUNK // 4):
-            start = chunk * CHUNK + quad * 4
+        for quad in range((early + LATE) // 4):
+            start = quad * 4
+            if start == early:
+                late_copy.wait()
             rows, cols = [], []
             for at in range(4):
                 live = start + at < live_count
-                rows.append(jnp.where(live, slot_rows[0, 0, start + at] // 2, row_cells))
-                cols.append(jnp.where(live, slot_cols[0, 0, start + at], col_cells))
-            stored = [blocks[0, 0, start + at] for at in range(4)]
+                rows.append(jnp.where(live, slot_rows[0, 0, start + at] // 2, row_cells + (start + at) % SPARE))
+                cols.append(jnp.where(live, slot_cols[0, 0, start + at], col_cells + (start + at) % SPARE))
+            held_in, first = (blocks, start) if start < early else (late, start - early)
+            stored = [held_in[0, 0, first + at] for at in range(4)]
             tile = jnp.concatenate(
                 [jnp.concatenate(stored[:2], axis=0), jnp.concatenate(stored[2:], axis=0)], axis=1
             )
@@ -221,13 +223,6 @@
                 add_next()
         while queued:
             add_next()
-        return carry
-
-    live_chunks = (live_count + CHUNK - 1) // CHUNK
-
-    def multiply(*units):
-        held = (units[:DEEP], units[DEEP:])
-        lax.fori_loop(0, live_chunks, functools.partial(visit, held), 0)
 
     pl.run_scoped(multiply, *[pltpu.ACC(unit)((4 * REWARDS, 2 * BLK), jnp.float32) for unit in (0, 1) for _ in range(DEEP)])
 
@@ -346,6 +341,7 @@
     smem = pl.BlockSpec(memory_space=pltpu.SMEM)
     hbm = pl.BlockSpec(memory_space=pltpu.HBM)
     vmem = pl.BlockSpec(memory_space=pltpu.VMEM)
+    in_smem = functools.partial(pltpu.with_memory_space_constraint, memory_space=pltpu.SMEM)
     in_hbm = functools.partial(pltpu.with_memory_space_constraint, memory_space=pltpu.HBM)
 
     steps = max(n_row, n_chip)
@@ -379,13 +375,13 @@
     rows, cols, pick, stored = pl.pallas_call(
         prefetch_kernel,
         out_shape=[
-            jax.ShapeDtypeStruct(slot_rows.shape, slot_rows.dtype),
-            jax.ShapeDtypeStruct(slot_cols.shape, slot_cols.dtype),
+            pltpu.SMEM(slot_rows.shape, slot_rows.dtype),
+            pltpu.SMEM(slot_cols.shape, slot_cols.dtype),
             jax.ShapeDtypeStruct((side // (reward_table.shape[0] * n_row) * REWARDS, side), jnp.bfloat16),
-            jax.ShapeDtypeStruct(blocks.shape, blocks.dtype),
+            jax.ShapeDtypeStruct((1, 1, blocks.shape[2] - LATE, BLK, BLK), blocks.dtype),
         ],
         in_specs=[vmem] + [hbm] * 4,
-        out_specs=[vmem] * 4,
+        out_specs=[smem] * 2 + [vmem] * 2,
         scratch_shapes=[pltpu.SMEM(reward_cols.shape, jnp.int32), pltpu.SemaphoreType.DMA((4,))],
         compiler_params=pltpu.CompilerParams(vmem_limit_bytes=24 * 2**20),
         cost_estimate=pl.CostEstimate(flops=0, bytes_accessed=2 * blocks.size * 2, transcendentals=0),
@@ -405,24 +401,23 @@
     sums = pl.pallas_call(
         functools.partial(products_kernel, n_row, n_col),
         out_shape=[tiles, *[coded] * (steps - 1)] * 2,
-        in_specs=[smem] + [vmem] * (4 + 2 * steps),
+        in_specs=[smem] * 3 + [hbm] + [vmem] * (2 + 2 * steps),
         out_specs=[vmem] * (2 * steps),
         scratch_shapes=[
-            pltpu.SMEM(slot_rows.shape, jnp.int32),
-            pltpu.SMEM(slot_cols.shape, jnp.int32),
             pltpu.VMEM((reward_table.shape[0] * n_row, col_cells * BLK), jnp.float32),
-            pltpu.VMEM((row_cells + 1, REWARDS, BLK), jnp.bfloat16),
-            pltpu.VMEM((col_cells + 1, REWARDS, BLK), jnp.bfloat16),
-            *[pltpu.VMEM((row_cells + 1, REWARDS, BLK), jnp.float32)] * SUMS,
-            *[pltpu.VMEM((col_cells + 1, REWARDS, BLK), jnp.float32)] * SUMS,
+            pltpu.VMEM((row_cells + SPARE, REWARDS, BLK), jnp.bfloat16),
+            pltpu.VMEM((col_cells + SPARE, REWARDS, BLK), jnp.bfloat16),
+            *[pltpu.VMEM((row_cells + SPARE, REWARDS, BLK), jnp.float32)] * SUMS,
+            *[pltpu.VMEM((col_cells + SPARE, REWARDS, BLK), jnp.float32)] * SUMS,
             pltpu.VMEM(tiles.shape, jnp.float32),
-            pltpu.SemaphoreType.DMA((2,)),
+            pltpu.VMEM((1, 1, LATE, BLK, BLK), blocks.dtype),
+            pltpu.SemaphoreType.DMA,
         ],
         compiler_params=pltpu.CompilerParams(vmem_limit_bytes=24 * 2**20),
         cost_estimate=pl.CostEstimate(
             flops=4 * REWARDS * blocks.size, bytes_accessed=4 * blocks.size, transcendentals=0
         ),
-    )(counts, rows, cols, pick, stored, *mine, *others)
+    )(counts, *map(in_smem, (rows, cols)), in_hbm(blocks), pick, stored, *mine, *others)
     keeps, gives = sums[:steps], sums[steps:]
     parts = []
     for step in reversed(range(steps)):

time: 30.4 us -> 30.1 us (level)
  starting transfers between devices: 13.9 us -> 12.1 us
  waiting for transfers between devices: 7.08 us -> 7.93 us
  Pallas kernels: 8.04 us -> 8.4 us
    ppermute x10, starting transfers between devices: 5.98 us -> 4.18 us  [swap(): return lax.ppermute(part, 'col', peers(n_col, 1))]
    pallas_call x1, Pallas kernels: 2.89 us -> 4.48 us  [on_device(): pl.pallas_call(functools.partial(products_kernel, n_row, n_col), out_shap...]
    pallas_call x1, Pallas kernels: 3.45 us -> 2.22 us  [on_device(): pl.pallas_call(prefetch_kernel, out_shape=[pltpu.SMEM(slot_rows.shape, sl...]
    ppermute x6, waiting for transfers between devices: 3.8 us -> 4.65 us  [cross(): return lax.ppermute(part, ('row', 'col'), crossings(n_row, n_col, step))]
  transfers between devices with their start and end apart: 16 -> 16, of which waited for: 9 -> 9; matrix products, arithmetic and copies ran while one was open for 0% -> 0% of each run, Pallas kernels for 14% -> 11%
where the time goes in v5:
time: 30.1 us; the launch traced here: 29.9 us
  starting transfers between devices  12.1 us (40%)
  Pallas kernels  8.4 us (28%)
  waiting for transfers between devices  7.93 us (26%)
  between operations  1.39 us (5%)
    ppermute x6, starting transfers between devices, cross(): return lax.ppermute(part, ('row', 'col'), crossings(n_row, n_col, step))  7.97 us
    ppermute x6, waiting for transfers between devices, cross(): return lax.ppermute(part, ('row', 'col'), crossings(n_row, n_col, step))  4.65 us
    pallas_call x1, Pallas kernels, on_device(): pl.pallas_call(functools.partial(products_kernel, n_row, n_col), out_shap...  4.48 us
    ppermute x10, starting transfers between devices, swap(): return lax.ppermute(part, 'col', peers(n_col, 1))  4.18 us
    ppermute x10, waiting for transfers between devices, swap(): return lax.ppermute(part, 'col', peers(n_col, 1))  3.28 us
    pallas_call x1, Pallas kernels, on_device(): pl.pallas_call(prefetch_kernel, out_shape=[pltpu.SMEM(slot_rows.shape, sl...  2.22 us
    pallas_call x1, Pallas kernels, on_device(): pl.pallas_call(load_kernel, out_shape=[jax.ShapeDtypeStruct(arg.shape, ar...  0.88 us
    pallas_call x1, Pallas kernels, on_device(): pl.pallas_call(result_kernel, out_shape=[jax.ShapeDtypeStruct((REWARDS, p...  0.66 us
  transfers between devices with their start and end apart: 16, of which 9 were waited for; matrix products, arithmetic and copies ran while one was open for 0% of the time, Pallas kernels for 11%

profile of v5, /device:TPU:0, one launch (start us, length us, event | category | flops | bytes accessed | tf_op | source)
XLA Modules:
  0.0 29.9 jit_solution(9891413544957372114)
XLA Ops:
  0.6 0.5 %collective-permute-start.1 = (bf16[8,4096]{1,0:T(8,128)(2,1)}, bf16[8,4096]{1,0:T(8,128)(2,1)S(1)}, u32[]{:S(2)}, u32[]{:S(2)}) collective-permute-start(bf16[8,4096]{1,0:T(8,128)(2,1)} %table_there.1), channel_id=1, source_target_pairs={{0,1},{1,0},{2,3},{3,2},{4,5},{5,4},{6,7},{7,6},{8,9},{9,8},{10,11... | collective-permute-start | bytes 196616 | tf_op jit(solution)/shard_map/ppermute | solution.py:351
  1.1 0.1 collective-permute-start
  1.2 0.9 %shard_map.86 = (bf16[16,1024]{1,0:T(8,128)(2,1)S(1)}, bf16[8,4096]{1,0:T(8,128)(2,1)S(1)}) custom-call(bf16[16,1024]{1,0:T(8,128)(2,1)} %shard_there.1, bf16[8,4096]{1,0:T(8,128)(2,1)} %table_there.1), custom_call_target="tpu_custom_call" | custom-call | bytes 4194304 | tf_op jit(solution)/shard_map/pallas_call | solution.py:357
  2.1 0.5 %collective-permute-done.other_shard = bf16[16,1024]{1,0:T(8,128)(2,1)S(1)} collective-permute-done((bf16[16,1024]{1,0:T(8,128)(2,1)}, bf16[16,1024]{1,0:T(8,128)(2,1)S(1)}, u32[]{:S(2)}, u32[]{:S(2)}) %collective-permute-start) | collective-permute-done | bytes 32800 | tf_op jit(solution)/shard_map/ppermute | solution.py:351
  2.6 0.0 collective-permute-done.1.other_table
  2.6 2.7 %collective-permute-start.3 = (bf16[16,4096]{1,0:T(8,128)(2,1)S(1)}, bf16[16,4096]{1,0:T(8,128)(2,1)S(1)}, u32[]{:S(2)}, u32[]{:S(2)}) collective-permute-start(bf16[16,4096]{1,0:T(8,128)(2,1)S(1)} %get-tuple-element.22.after.refs_6_), channel_id=1, source_target_pairs={{0,4},{1,17},{2,6},{3,19},{4,0},{5,21},{6,2},{7,23},{8,12},{9,25},... | collective-permute-start | bytes 393224 | tf_op jit(solution)/shard_map/ppermute | solution.py:354
  5.3 1.5 %collective-permute-start.2 = (bf16[16,4096]{1,0:T(8,128)(2,1)S(1)}, bf16[16,4096]{1,0:T(8,128)(2,1)S(1)}, u32[]{:S(2)}, u32[]{:S(2)}) collective-permute-start(bf16[16,4096]{1,0:T(8,128)(2,1)S(1)} %get-tuple-element.22.after.refs_6_), channel_id=1, source_target_pairs={{0,2},{1,9},{2,0},{3,11},{4,6},{5,13},{6,4},{7,15},{8,10},{9,1},{1... | collective-permute-start | bytes 393224 | tf_op jit(solution)/shard_map/ppermute | solution.py:354
  6.8 0.0 collective-permute-start.4
  6.9 2.2 %shard_map.88 = (s32[1,1,256]{2,1,0:T(1,128)S(4)}, s32[1,1,256]{2,1,0:T(1,128)S(4)}, bf16[128,256]{1,0:T(8,128)(2,1)S(1)}, bf16[1,1,128,128,128]{4,3,2,1,0:T(8,128)(2,1)S(1)}) custom-call(bf16[16,4096]{1,0:T(8,128)(2,1)S(1)} %get-tuple-element.22.after.refs_6_, s32[1,1,256]{2,1,0:T(1,128)} %rows_there.1, s32[1,1,256]{2,1,0:T(1,128)} %cols_there.1, ...), custom_call_target="tpu_custom_call" | custom-call | bytes 16777216 | tf_op jit(solution)/shard_map/pallas_call | solution.py:375
  9.1 0.0 collective-permute-done.3.refs_8_
  9.1 1.2 %collective-permute-start.6 = (bf16[16,4096]{1,0:T(8,128)(2,1)S(1)}, bf16[16,4096]{1,0:T(8,128)(2,1)S(1)}, u32[]{:S(2)}, u32[]{:S(2)}) collective-permute-start(bf16[16,4096]{1,0:T(8,128)(2,1)S(1)} %collective-permute-done.3.refs_8_), channel_id=1, source_target_pairs={{0,1},{1,0},{2,3},{3,2},{4,5},{5,4},{6,7},{7,6},{8,9},{9,8},{10,11... | collective-permute-start | bytes 393224 | tf_op jit(solution)/shard_map/ppermute | solution.py:351
  10.3 0.0 collective-permute-done.2.refs_7_
  10.3 0.2 collective-permute-start.5
  10.5 2.2 %collective-permute-done.4.part.refs_9_ = bf16[16,4096]{1,0:T(8,128)(2,1)S(1)} collective-permute-done((bf16[16,4096]{1,0:T(8,128)(2,1)S(1)}, bf16[16,4096]{1,0:T(8,128)(2,1)S(1)}, u32[]{:S(2)}, u32[]{:S(2)}) %collective-permute-start.4) | collective-permute-done | bytes 131104 | tf_op jit(solution)/shard_map/ppermute | solution.py:354
  12.7 0.8 %collective-permute-start.7 = (bf16[16,4096]{1,0:T(8,128)(2,1)S(1)}, bf16[16,4096]{1,0:T(8,128)(2,1)S(1)}, u32[]{:S(2)}, u32[]{:S(2)}) collective-permute-start(bf16[16,4096]{1,0:T(8,128)(2,1)S(1)} %shard_map.89), channel_id=1, source_target_pairs={{0,1},{1,0},{2,3},{3,2},{4,5},{5,4},{6,7},{7,6},{8,9},{9,8},{10,11... | collective-permute-start | bytes 393224 | tf_op jit(solution)/shard_map/ppermute | solution.py:351
  14.1 0.0 collective-permute-done.6.refs_12_
  14.1 0.0 collective-permute-done.5.refs_11_
  14.1 0.3 %collective-permute-done.7.refs_13_ = bf16[16,4096]{1,0:T(8,128)(2,1)S(1)} collective-permute-done((bf16[16,4096]{1,0:T(8,128)(2,1)S(1)}, bf16[16,4096]{1,0:T(8,128)(2,1)S(1)}, u32[]{:S(2)}, u32[]{:S(2)}) %collective-permute-start.7) | collective-permute-done | bytes 131104 | tf_op jit(solution)/shard_map/ppermute | solution.py:351
  14.4 4.5 %shard_map.90 = (f32[8,16,128]{2,1,0:T(8,128)S(1)}, s16[9,16,128]{2,1,0:T(8,128)(2,1)S(1)}, s16[9,16,128]{2,1,0:T(8,128)(2,1)S(1)}, s16[9,16,128]{2,1,0:T(8,128)...) custom-call(s32[1,1]{1,0:T(1,128)S(6)} %copy.9.refs_0_, ...), custom_call_target="tpu_custom_call" | custom-call | flops 268435456 | bytes 16777216 | tf_op jit(solution)/shard_map/pallas_call | solution.py:401
  18.9 0.4 %collective-permute-start.13 = (s16[9,16,128]{2,1,0:T(8,128)(2,1)S(1)}, s16[9,16,128]{2,1,0:T(8,128)(2,1)S(1)}, u32[]{:S(2)}, u32[]{:S(2)}) collective-permute-start(s16[9,16,128]{2,1,0:T(8,128)(2,1)S(1)} %get-tuple-element.35), channel_id=1, source_target_pairs={{0,1},{1,0},{2,3},{3,2},{4,5},{5,4},{6,7},{7,6},{8,9},{9,8},{10,11... | collective-permute-start | bytes 110600 | tf_op jit(solution)/shard_map/ppermute | solution.py:351
  19.4 0.1 collective-permute-start.11
  19.5 0.4 %collective-permute-start.9 = (s16[9,16,128]{2,1,0:T(8,128)(2,1)S(1)}, s16[9,16,128]{2,1,0:T(8,128)(2,1)S(1)}, u32[]{:S(2)}, u32[]{:S(2)}) collective-permute-start(s16[9,16,128]{2,1,0:T(8,128)(2,1)S(1)} %get-tuple-element.31), channel_id=1, source_target_pairs={{0,1},{1,0},{2,3},{3,2},{4,5},{5,4},{6,7},{7,6},{8,9},{9,8},{10,11... | collective-permute-start | bytes 110600 | tf_op jit(solution)/shard_map/ppermute | solution.py:351
  19.9 0.4 %collective-permute-done.13.got = s16[9,16,128]{2,1,0:T(8,128)(2,1)S(1)} collective-permute-done((s16[9,16,128]{2,1,0:T(8,128)(2,1)S(1)}, s16[9,16,128]{2,1,0:T(8,128)(2,1)S(1)}, u32[]{:S(2)}, u32[]{:S(2)}) %collective-permute-start.13) | collective-permute-done | bytes 36896 | tf_op jit(solution)/shard_map/ppermute | solution.py:351
  20.2 2.5 %collective-permute-start.14 = (s16[18,16,128]{2,1,0:T(8,128)(2,1)S(1)}, s16[18,16,128]{2,1,0:T(8,128)(2,1)S(1)}, u32[]{:S(2)}, u32[]{:S(2)}) collective-permute-start(s16[18,16,128]{2,1,0:T(8,128)(2,1)S(1)} %shard_map.94), channel_id=1, source_target_pairs={{0,6},{1,25},{2,4},{3,27},{4,2},{5,29},{6,0},{7,31},{8,14},{9,17},... | collective-permute-start | bytes 221192 | tf_op jit(solution)/shard_map/ppermute | solution.py:354
  22.7 0.0 collective-permute-done.11.got
  22.8 0.6 %collective-permute-start.12 = (s16[18,16,128]{2,1,0:T(8,128)(2,1)S(1)}, s16[18,16,128]{2,1,0:T(8,128)(2,1)S(1)}, u32[]{:S(2)}, u32[]{:S(2)}) collective-permute-start(s16[18,16,128]{2,1,0:T(8,128)(2,1)S(1)} %shard_map.93), channel_id=1, source_target_pairs={{0,4},{1,17},{2,6},{3,19},{4,0},{5,21},{6,2},{7,23},{8,12},{9,25},... | collective-permute-start | bytes 221192 | tf_op jit(solution)/shard_map/ppermute | solution.py:354
  23.4 0.0 collective-permute-done.9.got
  23.4 0.6 %collective-permute-start.10 = (s16[18,16,128]{2,1,0:T(8,128)(2,1)S(1)}, s16[18,16,128]{2,1,0:T(8,128)(2,1)S(1)}, u32[]{:S(2)}, u32[]{:S(2)}) collective-permute-start(s16[18,16,128]{2,1,0:T(8,128)(2,1)S(1)} %shard_map.92), channel_id=1, source_target_pairs={{0,2},{1,9},{2,0},{3,11},{4,6},{5,13},{6,4},{7,15},{8,10},{9,1},{1... | collective-permute-start | bytes 221192 | tf_op jit(solution)/shard_map/ppermute | solution.py:354
  24.0 0.4 %collective-permute-start.8 = (f32[8,16,128]{2,1,0:T(8,128)S(1)}, f32[8,16,128]{2,1,0:T(8,128)S(1)}, u32[]{:S(2)}, u32[]{:S(2)}) collective-permute-start(f32[8,16,128]{2,1,0:T(8,128)S(1)} %get-tuple-element.29), channel_id=1, source_target_pairs={{0,1},{1,0},{2,3},{3,2},{4,5},{5,4},{6,7},{7,6},{8,9},{9,8},{10,11... | collective-permute-start | bytes 196616 | tf_op jit(solution)/shard_map/ppermute | solution.py:351
  24.4 0.9 %collective-permute-done.8.got = f32[8,16,128]{2,1,0:T(8,128)S(1)} collective-permute-done((f32[8,16,128]{2,1,0:T(8,128)S(1)}, f32[8,16,128]{2,1,0:T(8,128)S(1)}, u32[]{:S(2)}, u32[]{:S(2)}) %collective-permute-start.8) | collective-permute-done | bytes 65568 | tf_op jit(solution)/shard_map/ppermute | solution.py:351
  25.3 0.2 collective-permute-done.14.refs_3_
  25.6 1.6 %collective-permute-done.12.refs_2_ = s16[18,16,128]{2,1,0:T(8,128)(2,1)S(1)} collective-permute-done((s16[18,16,128]{2,1,0:T(8,128)(2,1)S(1)}, s16[18,16,128]{2,1,0:T(8,128)(2,1)S(1)}, u32[]{:S(2)}, u32[]{:S(2)}) %collective-permute-start.12) | collective-permute-done | bytes 73760 | tf_op jit(solution)/shard_map/ppermute | solution.py:354
  27.2 0.6 %collective-permute-done.10.refs_1_ = s16[18,16,128]{2,1,0:T(8,128)(2,1)S(1)} collective-permute-done((s16[18,16,128]{2,1,0:T(8,128)(2,1)S(1)}, s16[18,16,128]{2,1,0:T(8,128)(2,1)S(1)}, u32[]{:S(2)}, u32[]{:S(2)}) %collective-permute-start.10) | collective-permute-done | bytes 73760 | tf_op jit(solution)/shard_map/ppermute | solution.py:354
  27.8 0.1 shard_map.95
  27.9 0.1 collective-permute-start.15
  28.0 1.2 %collective-permute-done.15.got = f32[8,16,128]{2,1,0:T(8,128)S(1)} collective-permute-done((f32[8,16,128]{2,1,0:T(8,128)S(1)}, f32[8,16,128]{2,1,0:T(8,128)S(1)}, u32[]{:S(2)}, u32[]{:S(2)}) %collective-permute-start.15) | collective-permute-done | bytes 65568 | tf_op jit(solution)/shard_map/ppermute | solution.py:351
  29.2 0.7 %shard_map.96 = (f32[16,1024]{1,0:T(8,128)}, f32[4,4096]{1,0:T(4,128)}) custom-call(f32[8,16,128]{2,1,0:T(8,128)S(1)} %get-tuple-element.36.keep, f32[8,16,128]{2,1,0:T(8,128)S(1)} %collective-permute-done.15.got), custom_call_target="tpu_custom_call" | custom-call | tf_op jit(solution)/shard_map/pallas_call | solution.py:439
  (6 shorter events, 0.1 us)
Async XLA Ops:
  0.6 1.9 %collective-permute-start.1 = (bf16[8,4096]{1,0:T(8,128)(2,1)}, bf16[8,4096]{1,0:T(8,128)(2,1)S(1)}, u32[]{:S(2)}, u32[]{:S(2)}) collective-permute-start(bf16[8,4096]{1,0:T(8,128)(2,1)} %table_there.1), channel_id=1, source_target_pairs={{0,1},{1,0},{2,3},{3,2},{4,5},{5,4},{6,7},{7,6},{8,9},{9,8},{10,11... | collective-permute-start | bytes 196616 | tf_op jit(solution)/shard_map/ppermute | solution.py:351
  1.1 1.4 %collective-permute-start = (bf16[16,1024]{1,0:T(8,128)(2,1)}, bf16[16,1024]{1,0:T(8,128)(2,1)S(1)}, u32[]{:S(2)}, u32[]{:S(2)}) collective-permute-start(bf16[16,1024]{1,0:T(8,128)(2,1)} %shard_there.1), channel_id=1, source_target_pairs={{0,1},{1,0},{2,3},{3,2},{4,5},{5,4},{6,7},{7,6},{8,9},{9,8},{10,11... | collective-permute-start | bytes 98312 | tf_op jit(solution)/shard_map/ppermute | solution.py:351
  2.6 6.5 %collective-permute-start.3 = (bf16[16,4096]{1,0:T(8,128)(2,1)S(1)}, bf16[16,4096]{1,0:T(8,128)(2,1)S(1)}, u32[]{:S(2)}, u32[]{:S(2)}) collective-permute-start(bf16[16,4096]{1,0:T(8,128)(2,1)S(1)} %get-tuple-element.22.after.refs_6_), channel_id=1, source_target_pairs={{0,4},{1,17},{2,6},{3,19},{4,0},{5,21},{6,2},{7,23},{8,12},{9,25},... | collective-permute-start | bytes 393224 | tf_op jit(solution)/shard_map/ppermute | solution.py:354
  5.3 5.0 %collective-permute-start.2 = (bf16[16,4096]{1,0:T(8,128)(2,1)S(1)}, bf16[16,4096]{1,0:T(8,128)(2,1)S(1)}, u32[]{:S(2)}, u32[]{:S(2)}) collective-permute-start(bf16[16,4096]{1,0:T(8,128)(2,1)S(1)} %get-tuple-element.22.after.refs_6_), channel_id=1, source_target_pairs={{0,2},{1,9},{2,0},{3,11},{4,6},{5,13},{6,4},{7,15},{8,10},{9,1},{1... | collective-permute-start | bytes 393224 | tf_op jit(solution)/shard_map/ppermute | solution.py:354
  6.8 5.9 %collective-permute-start.4 = (bf16[16,4096]{1,0:T(8,128)(2,1)S(1)}, bf16[16,4096]{1,0:T(8,128)(2,1)S(1)}, u32[]{:S(2)}, u32[]{:S(2)}) collective-permute-start(bf16[16,4096]{1,0:T(8,128)(2,1)S(1)} %get-tuple-element.22.after.refs_6_), channel_id=1, source_target_pairs={{0,6},{1,25},{2,4},{3,27},{4,2},{5,29},{6,0},{7,31},{8,14},{9,17},... | collective-permute-start | bytes 393224 | tf_op jit(solution)/shard_map/ppermute | solution.py:354
  9.1 5.0 %collective-permute-start.6 = (bf16[16,4096]{1,0:T(8,128)(2,1)S(1)}, bf16[16,4096]{1,0:T(8,128)(2,1)S(1)}, u32[]{:S(2)}, u32[]{:S(2)}) collective-permute-start(bf16[16,4096]{1,0:T(8,128)(2,1)S(1)} %collective-permute-done.3.refs_8_), channel_id=1, source_target_pairs={{0,1},{1,0},{2,3},{3,2},{4,5},{5,4},{6,7},{7,6},{8,9},{9,8},{10,11... | collective-permute-start | bytes 393224 | tf_op jit(solution)/shard_map/ppermute | solution.py:351
  10.3 3.8 %collective-permute-start.5 = (bf16[16,4096]{1,0:T(8,128)(2,1)S(1)}, bf16[16,4096]{1,0:T(8,128)(2,1)S(1)}, u32[]{:S(2)}, u32[]{:S(2)}) collective-permute-start(bf16[16,4096]{1,0:T(8,128)(2,1)S(1)} %collective-permute-done.2.refs_7_), channel_id=1, source_target_pairs={{0,1},{1,0},{2,3},{3,2},{4,5},{5,4},{6,7},{7,6},{8,9},{9,8},{10,11... | collective-permute-start | bytes 393224 | tf_op jit(solution)/shard_map/ppermute | solution.py:351
  12.7 1.7 %collective-permute-start.7 = (bf16[16,4096]{1,0:T(8,128)(2,1)S(1)}, bf16[16,4096]{1,0:T(8,128)(2,1)S(1)}, u32[]{:S(2)}, u32[]{:S(2)}) collective-permute-start(bf16[16,4096]{1,0:T(8,128)(2,1)S(1)} %shard_map.89), channel_id=1, source_target_pairs={{0,1},{1,0},{2,3},{3,2},{4,5},{5,4},{6,7},{7,6},{8,9},{9,8},{10,11... | collective-permute-start | bytes 393224 | tf_op jit(solution)/shard_map/ppermute | solution.py:351
  18.9 1.3 %collective-permute-start.13 = (s16[9,16,128]{2,1,0:T(8,128)(2,1)S(1)}, s16[9,16,128]{2,1,0:T(8,128)(2,1)S(1)}, u32[]{:S(2)}, u32[]{:S(2)}) collective-permute-start(s16[9,16,128]{2,1,0:T(8,128)(2,1)S(1)} %get-tuple-element.35), channel_id=1, source_target_pairs={{0,1},{1,0},{2,3},{3,2},{4,5},{5,4},{6,7},{7,6},{8,9},{9,8},{10,11... | collective-permute-start | bytes 110600 | tf_op jit(solution)/shard_map/ppermute | solution.py:351
  19.4 3.4 %collective-permute-start.11 = (s16[9,16,128]{2,1,0:T(8,128)(2,1)S(1)}, s16[9,16,128]{2,1,0:T(8,128)(2,1)S(1)}, u32[]{:S(2)}, u32[]{:S(2)}) collective-permute-start(s16[9,16,128]{2,1,0:T(8,128)(2,1)S(1)} %get-tuple-element.33), channel_id=1, source_target_pairs={{0,1},{1,0},{2,3},{3,2},{4,5},{5,4},{6,7},{7,6},{8,9},{9,8},{10,11... | collective-permute-start | bytes 110600 | tf_op jit(solution)/shard_map/ppermute | solution.py:351
  19.5 3.9 %collective-permute-start.9 = (s16[9,16,128]{2,1,0:T(8,128)(2,1)S(1)}, s16[9,16,128]{2,1,0:T(8,128)(2,1)S(1)}, u32[]{:S(2)}, u32[]{:S(2)}) collective-permute-start(s16[9,16,128]{2,1,0:T(8,128)(2,1)S(1)} %get-tuple-element.31), channel_id=1, source_target_pairs={{0,1},{1,0},{2,3},{3,2},{4,5},{5,4},{6,7},{7,6},{8,9},{9,8},{10,11... | collective-permute-start | bytes 110600 | tf_op jit(solution)/shard_map/ppermute | solution.py:351
  20.2 5.3 %collective-permute-start.14 = (s16[18,16,128]{2,1,0:T(8,128)(2,1)S(1)}, s16[18,16,128]{2,1,0:T(8,128)(2,1)S(1)}, u32[]{:S(2)}, u32[]{:S(2)}) collective-permute-start(s16[18,16,128]{2,1,0:T(8,128)(2,1)S(1)} %shard_map.94), channel_id=1, source_target_pairs={{0,6},{1,25},{2,4},{3,27},{4,2},{5,29},{6,0},{7,31},{8,14},{9,17},... | collective-permute-start | bytes 221192 | tf_op jit(solution)/shard_map/ppermute | solution.py:354
  22.8 4.4 %collective-permute-start.12 = (s16[18,16,128]{2,1,0:T(8,128)(2,1)S(1)}, s16[18,16,128]{2,1,0:T(8,128)(2,1)S(1)}, u32[]{:S(2)}, u32[]{:S(2)}) collective-permute-start(s16[18,16,128]{2,1,0:T(8,128)(2,1)S(1)} %shard_map.93), channel_id=1, source_target_pairs={{0,4},{1,17},{2,6},{3,19},{4,0},{5,21},{6,2},{7,23},{8,12},{9,25},... | collective-permute-start | bytes 221192 | tf_op jit(solution)/shard_map/ppermute | solution.py:354
  23.4 4.4 %collective-permute-start.10 = (s16[18,16,128]{2,1,0:T(8,128)(2,1)S(1)}, s16[18,16,128]{2,1,0:T(8,128)(2,1)S(1)}, u32[]{:S(2)}, u32[]{:S(2)}) collective-permute-start(s16[18,16,128]{2,1,0:T(8,128)(2,1)S(1)} %shard_map.92), channel_id=1, source_target_pairs={{0,2},{1,9},{2,0},{3,11},{4,6},{5,13},{6,4},{7,15},{8,10},{9,1},{1... | collective-permute-start | bytes 221192 | tf_op jit(solution)/shard_map/ppermute | solution.py:354
  24.0 1.3 %collective-permute-start.8 = (f32[8,16,128]{2,1,0:T(8,128)S(1)}, f32[8,16,128]{2,1,0:T(8,128)S(1)}, u32[]{:S(2)}, u32[]{:S(2)}) collective-permute-start(f32[8,16,128]{2,1,0:T(8,128)S(1)} %get-tuple-element.29), channel_id=1, source_target_pairs={{0,1},{1,0},{2,3},{3,2},{4,5},{5,4},{6,7},{7,6},{8,9},{9,8},{10,11... | collective-permute-start | bytes 196616 | tf_op jit(solution)/shard_map/ppermute | solution.py:351
  27.9 1.3 %collective-permute-start.15 = (f32[8,16,128]{2,1,0:T(8,128)S(1)}, f32[8,16,128]{2,1,0:T(8,128)S(1)}, u32[]{:S(2)}, u32[]{:S(2)}) collective-permute-start(f32[8,16,128]{2,1,0:T(8,128)S(1)} %get-tuple-element.37), channel_id=1, source_target_pairs={{0,1},{1,0},{2,3},{3,2},{4,5},{5,4},{6,7},{7,6},{8,9},{9,8},{10,11... | collective-permute-start | bytes 196616 | tf_op jit(solution)/shard_map/ppermute | solution.py:351

commit v6 on v5

--- a/solution.py
+++ b/solution.py
@@ -10,6 +10,7 @@
 BLK = 128
 REWARDS = 16
 LATE = 128
+PART = 64
 SUMS = 1
 GRAIN = 128
 MOST = 32767.0
@@ -22,25 +23,25 @@
     return [(here, here ^ step) for here in range(size)]
 
 
-def crossings(n_row, n_col, step):
+def far_order(n_row):
+    return (2, 1, *range(3, n_row))
+
+
+def crossings(n_row, n_col, first, second):
     pairs = []
     for row in range(n_row):
         for chip in range(n_col // 2):
-            if step < n_col // 2:
-                pairs.append((row * n_col + 2 * chip, row * n_col + 2 * (chip ^ step)))
-            if step < n_row:
-                pairs.append((row * n_col + 2 * chip + 1, (row ^ step) * n_col + 2 * chip + 1))
+            for core, step in enumerate((first, second)):
+                if step is not None:
+                    pairs.append(
+                        (row * n_col + 2 * chip + core, (row ^ step[0]) * n_col + 2 * (chip ^ step[1]) + core)
+                    )
     return pairs
 
 
 def by_core(here, there):
     first = lax.axis_index("col") % 2 == 0
     return jnp.where(first, here, there), jnp.where(first, there, here)
-
-
-def lay(table, width):
-    pieces = table.shape[1] // width
-    return jnp.concatenate([table[:, at * width : (at + 1) * width] for at in range(pieces)], axis=0)
 
 
 def load_kernel(shard_there, table_there, shard, table, sems):
@@ -82,26 +83,12 @@
         copy.wait()
 
 
-def after_kernel(part, after, out):
-    out[...] = part[...]
-
-
-def gather_kernel(shard, table, other_shard, other_table, mine, other):
-    core, span, width = lax.axis_index("col") % 2, shard.shape[1], mine.shape[1]
-
-    def write(shards, tables, shards_out, tables_out):
-        for half in range(2):
-            shards_out[:, half * span : (half + 1) * span] = shards[half][...]
-        lines = [lay(part[...].astype(jnp.float32), width) for part in tables]
-        tables_out[...] = jnp.concatenate(lines, axis=0).astype(tables_out.dtype)
-
-    @pl.when(core == 0)
-    def _():
-        write((shard, other_shard), (table, other_table), mine, other)
-
-    @pl.when(core == 1)
-    def _():
-        write((other_shard, shard), (other_table, table), other, mine)
+def gather_kernel(shard, other_shard, cots, cells):
+    span, owned, parity = shard.shape[1], cells.shape[0] // 2, lax.axis_index("col") % 2
+    cots[:, :span], cots[:, span:] = by_core(shard[...], other_shard[...])
+    for at in range(owned):
+        lane = pl.ds(pl.multiple_of((2 * at + parity) * BLK, BLK), BLK)
+        cells[at], cells[owned + at] = by_core(shard[:, lane], other_shard[:, lane])
 
 
 def spread(first, second):
@@ -113,11 +100,13 @@
 
 def products_kernel(n_row, n_col, *refs):
     n_chip = n_col // 2
-    steps = max(n_row, n_chip)
-    counts, slot_rows, slot_cols, blocks_there, pick, blocks = refs[:6]
-    mine, others = refs[6 : 6 + steps], refs[6 + steps : 6 + 2 * steps]
-    keeps, gives = refs[6 + 2 * steps : 6 + 3 * steps], refs[6 + 3 * steps : 6 + 4 * steps]
-    refs = refs[6 + 4 * steps :]
+    steps, rounds = max(n_row, n_chip), n_chip // 2 - 1
+    counts, slot_rows, slot_cols, blocks_there, pick, blocks, cots, cells = refs[:8]
+    mine, others = refs[8 : 8 + rounds], refs[8 + rounds : 8 + 2 * rounds]
+    tables = refs[8 + 2 * rounds : 8 + 2 * rounds + n_row]
+    refs = refs[8 + 2 * rounds + n_row :]
+    keeps, gives = refs[:steps], refs[steps : 2 * steps]
+    refs = refs[2 * steps :]
     table, weights, rewards = refs[:3]
     value_sums, grad_sums = refs[3 : 3 + SUMS], refs[3 + SUMS : 3 + 2 * SUMS]
     draft, late, late_sem = refs[3 + 2 * SUMS :]
@@ -126,39 +115,40 @@
     row_cells, col_cells = weights.shape[0] - SPARE, rewards.shape[0] - SPARE
 
     early = blocks.shape[2]
-    late_copy = pltpu.make_async_copy(blocks_there.at[:, :, pl.ds(early, LATE)], late, late_sem)
-    late_copy.start()
-    for sums in (*value_sums, *grad_sums):
-        sums[...] = jnp.zeros_like(sums)
+    late_copies = [
+        pltpu.make_async_copy(
+            blocks_there.at[:, :, pl.ds(early + at, PART)], late.at[:, :, pl.ds(at, PART)], late_sem.at[at // PART]
+        )
+        for at in range(0, LATE, PART)
+    ]
+    for copy in late_copies:
+        copy.start()
+    @pl.when(counts[0, 0] >= 0)
+    def _():
+        for sums in (*value_sums, *grad_sums):
+            sums[...] = jnp.zeros_like(sums)
+
     for spare in range(SPARE):
         weights[row_cells + spare] = jnp.zeros((REWARDS, BLK), jnp.bfloat16)
         rewards[col_cells + spare] = jnp.zeros((REWARDS, BLK), jnp.bfloat16)
 
     owned = row_cells // n_col
     group = table.shape[0] // n_row
-    pieces = REWARDS // 2 // group
-    width = col_cells * BLK // pieces
-
-    def take(shards, tables, my_half):
-        for step in range(n_chip):
-            for half in range(2):
-                first = (2 * (own_chip ^ step) + half) * owned
-                for at in range(owned):
-                    lane = (half * 2 * owned + 2 * at + my_half) * BLK
-                    weights[first + at] = shards[step][:, lane : lane + BLK]
-        for step in range(n_row):
-            for at in range(pieces):
-                part = tables[step][...].astype(jnp.float32)
-                line = my_half * (REWARDS // 2) + at * group
-                table[step * group : (step + 1) * group, at * width : (at + 1) * width] = part[line : line + group]
-
-    @pl.when(core == 0)
-    def _():
-        take(mine, others, 0)
-
-    @pl.when(core == 1)
-    def _():
-        take(others, mine, 1)
+
+    def take_shards(part, step):
+        for half in range(2):
+            first = (2 * (own_chip ^ step) + half) * owned
+            for at in range(owned):
+                lane = pl.multiple_of((half * 2 * owned + 2 * at + core) * BLK, BLK)
+                weights[first + at] = part[:, pl.ds(lane, BLK)]
+
+    take_shards(cots, 0)
+    for turn in range(rounds):
+        take_shards(mine[turn], 2 * turn + 1 + core)
+        take_shards(others[turn], 2 * turn + 2 - core)
+    weights[pl.ds((own_chip ^ (n_chip - 1)) * 2 * owned, 2 * owned)] = cells[...]
+    for step, part in zip((0, *far_order(n_row)), tables):
+        table[step * group : (step + 1) * group, :] = part[...].astype(jnp.float32)
 
     side = 2 * BLK
     bands = side // (group * n_row)
@@ -194,8 +184,8 @@
 
         for quad in range((early + LATE) // 4):
             start = quad * 4
-            if start == early:
-                late_copy.wait()
+            if start >= early and (start - early) % PART == 0:
+                late_copies[(start - early) // PART].wait()
             rows, cols = [], []
             for at in range(4):
                 live = start + at < live_count
@@ -350,10 +340,9 @@
     def swap(part):
         return lax.ppermute(part, "col", peers(n_col, 1))
 
-    def cross(part, step):
-        return lax.ppermute(part, ("row", "col"), crossings(n_row, n_col, step))
-
-    width = 2 * reward_table.shape[0] * reward_table.shape[1] // REWARDS
+    def cross(part, first, second):
+        return lax.ppermute(part, ("row", "col"), crossings(n_row, n_col, first, second))
+
     loaded = pl.pallas_call(
         load_kernel,
         out_shape=[jax.ShapeDtypeStruct(arg.shape, arg.dtype) for arg in (cotangent, reward_table)],
@@ -363,14 +352,20 @@
         compiler_params=small,
         cost_estimate=pl.CostEstimate(flops=0, bytes_accessed=4 * 2**20, transcendentals=0),
     )(in_hbm(cotangent), in_hbm(reward_table))
-    mine, other = pl.pallas_call(
+    cots, cells = pl.pallas_call(
         gather_kernel,
-        out_shape=[jax.ShapeDtypeStruct((REWARDS, width), cotangent.dtype)] * 2,
-        in_specs=[vmem] * 4,
+        out_shape=[
+            jax.ShapeDtypeStruct((REWARDS, 2 * cotangent.shape[1]), cotangent.dtype),
+            jax.ShapeDtypeStruct((row_cells // n_chip, REWARDS, BLK), cotangent.dtype),
+        ],
+        in_specs=[vmem] * 2,
         out_specs=[vmem] * 2,
         compiler_params=small,
-    )(*loaded, swap(cotangent), swap(reward_table))
-    mine = [mine] + [cross(mine, step) for step in range(1, steps)]
+    )(loaded[0], swap(cotangent))
+    mine = [cross(cots, (0, 2 * turn + 1), (0, 2 * turn + 2)) for turn in range(n_chip // 2 - 1)]
+    others = [swap(part) for part in mine]
+    tables = [loaded[1]] + [lax.ppermute(reward_table, "row", peers(n_row, step)) for step in far_order(n_row)]
+    opposite = lax.ppermute(cells, "col", peers(n_col, 2 * (n_chip - 1)))
     side = 2 * BLK
     rows, cols, pick, stored = pl.pallas_call(
         prefetch_kernel,
@@ -386,14 +381,6 @@
         compiler_params=pltpu.CompilerParams(vmem_limit_bytes=24 * 2**20),
         cost_estimate=pl.CostEstimate(flops=0, bytes_accessed=2 * blocks.size * 2, transcendentals=0),
     )(mine[0], *map(in_hbm, (slot_rows, slot_cols, reward_cols, blocks)))
-    first = pl.pallas_call(
-        after_kernel,
-        out_shape=jax.ShapeDtypeStruct(mine[-1].shape, mine[-1].dtype),
-        in_specs=[vmem] * 2,
-        out_specs=vmem,
-        compiler_params=small,
-    )(mine[-1], pick)
-    others = [other] + [swap(part) for part in (*mine[1:-1], first)]
 
     lines, part = REWARDS // n_row, row_cells // n_chip
     tiles = jax.ShapeDtypeStruct((max(part, col_cells * lines // REWARDS), REWARDS, BLK), jnp.float32)
@@ -401,7 +388,7 @@
     sums = pl.pallas_call(
         functools.partial(products_kernel, n_row, n_col),
         out_shape=[tiles, *[coded] * (steps - 1)] * 2,
-        in_specs=[smem] * 3 + [hbm] + [vmem] * (2 + 2 * steps),
+        in_specs=[smem] * 3 + [hbm] + [vmem] * (4 + 2 * len(mine) + n_row),
         out_specs=[vmem] * (2 * steps),
         scratch_shapes=[
             pltpu.VMEM((reward_table.shape[0] * n_row, col_cells * BLK), jnp.float32),
@@ -411,13 +398,13 @@
             *[pltpu.VMEM((col_cells + SPARE, REWARDS, BLK), jnp.float32)] * SUMS,
             pltpu.VMEM(tiles.shape, jnp.float32),
             pltpu.VMEM((1, 1, LATE, BLK, BLK), blocks.dtype),
-            pltpu.SemaphoreType.DMA,
+            pltpu.SemaphoreType.DMA((LATE // PART,)),
         ],
         compiler_params=pltpu.CompilerParams(vmem_limit_bytes=24 * 2**20),
         cost_estimate=pl.CostEstimate(
             flops=4 * REWARDS * blocks.size, bytes_accessed=4 * blocks.size, transcendentals=0
         ),
-    )(counts, *map(in_smem, (rows, cols)), in_hbm(blocks), pick, stored, *mine, *others)
+    )(counts, *map(in_smem, (rows, cols)), in_hbm(blocks), pick, stored, cots, opposite, *mine, *others, *tables)
     keeps, gives = sums[:steps], sums[steps:]
     parts = []
     for step in reversed(range(steps)):
@@ -428,7 +415,7 @@
             out_specs=vmem,
             compiler_params=small,
         )(keeps[step], swap(gives[step]))
-        parts.insert(0, cross(pair, step) if step else pair)
+        parts.insert(0, cross(pair, (0, step) if step < n_chip else None, (step, 0) if step < n_row else None) if step else pair)
     keep, give = pl.pallas_call(
         functools.partial(total_kernel, n_row, n_chip),
         out_shape=[tiles] * 2,

time: 30.1 us -> 29.7 us (0.987)
  waiting for transfers between devices: 7.93 us -> 5.79 us
  starting transfers between devices: 12.1 us -> 14 us
    ppermute x6 -> x8, starting transfers between devices: 7.97 us -> 12.2 us  [the longest x4 6.58 us: cross(): lax.ppermute(part, ('row', 'col'), crossings(n_row, n_col, first, second))]
    ppermute x10 -> x7, starting transfers between devices: 4.18 us -> 1.72 us  [swap(): return lax.ppermute(part, 'col', peers(n_col, 1))]
    ppermute x6 -> x8, waiting for transfers between devices: 4.65 us -> 2.95 us  [the longest x4 2.27 us: cross(): lax.ppermute(part, ('row', 'col'), crossings(n_row, n_col, first, second))]
    ppermute x10 -> x7, waiting for transfers between devices: 3.28 us -> 2.84 us  [swap(): return lax.ppermute(part, 'col', peers(n_col, 1))]
  transfers between devices with their start and end apart: 16 -> 15, of which waited for: 9 -> 9; matrix products, arithmetic and copies ran while one was open for 0% -> 0% of each run, Pallas kernels for 11% -> 11%
where the time goes in v6:
time: 29.7 us; the launch traced here: 29.5 us
  starting transfers between devices  14 us (47%)
  Pallas kernels  8.36 us (28%)
  waiting for transfers between devices  5.79 us (19%)
  between operations  1.37 us (5%)
    ppermute x4, starting transfers between devices, cross(): lax.ppermute(part, ('row', 'col'), crossings(n_row, n_col, first, second))  6.58 us
    pallas_call x1, Pallas kernels, on_device(): pl.pallas_call(functools.partial(products_kernel, n_row, n_col), out_shap...  4.44 us
    ppermute x3, starting transfers between devices, on_device(): lax.ppermute(reward_table, 'row', peers(n_row, step))  4.17 us
    ppermute x7, waiting for transfers between devices, swap(): return lax.ppermute(part, 'col', peers(n_col, 1))  2.84 us
    ppermute x4, waiting for transfers between devices, cross(): lax.ppermute(part, ('row', 'col'), crossings(n_row, n_col, first, second))  2.27 us
    pallas_call x1, Pallas kernels, on_device(): pl.pallas_call(prefetch_kernel, out_shape=[pltpu.SMEM(slot_rows.shape, sl...  2.23 us
    ppermute x7, starting transfers between devices, swap(): return lax.ppermute(part, 'col', peers(n_col, 1))  1.72 us
    ppermute x1, starting transfers between devices, on_device(): opposite = lax.ppermute(cells, 'col', peers(n_col, 2 * (n_chip - 1)))  1.49 us
  transfers between devices with their start and end apart: 15, of which 9 were waited for; matrix products, arithmetic and copies ran while one was open for 0% of the time, Pallas kernels for 11%

profile of v6, /device:TPU:0, one launch (start us, length us, event | category | flops | bytes accessed | tf_op | source)
XLA Modules:
  0.0 29.5 jit_solution(8556768400345844434)
XLA Ops:
  0.6 0.5 %collective-permute-start = (bf16[16,1024]{1,0:T(8,128)(2,1)}, bf16[16,1024]{1,0:T(8,128)(2,1)S(1)}, u32[]{:S(2)}, u32[]{:S(2)}) collective-permute-start(bf16[16,1024]{1,0:T(8,128)(2,1)} %shard_there.1), channel_id=1, source_target_pairs={{0,1},{1,0},{2,3},{3,2},{4,5},{5,4},{6,7},{7,6},{8,9},{9,8},{10,11... | collective-permute-start | bytes 98312 | tf_op jit(solution)/shard_map/ppermute | solution.py:341
  1.1 0.9 %shard_map.86 = (bf16[16,1024]{1,0:T(8,128)(2,1)S(1)}, bf16[8,4096]{1,0:T(8,128)(2,1)S(1)}) custom-call(bf16[16,1024]{1,0:T(8,128)(2,1)} %shard_there.1, bf16[8,4096]{1,0:T(8,128)(2,1)} %table_there.1), custom_call_target="tpu_custom_call" | custom-call | bytes 4194304 | tf_op jit(solution)/shard_map/pallas_call | solution.py:346
  2.0 0.2 collective-permute-done.other_shard
  2.2 2.9 %collective-permute-start.1 = (bf16[16,2048]{1,0:T(8,128)(2,1)S(1)}, bf16[16,2048]{1,0:T(8,128)(2,1)S(1)}, u32[]{:S(2)}, u32[]{:S(2)}) collective-permute-start(bf16[16,2048]{1,0:T(8,128)(2,1)S(1)} %get-tuple-element.21.refs_6_), channel_id=1, source_target_pairs={{0,2},{1,5},{2,0},{3,7},{4,6},{5,1},{6,4},{7,3},{8,10},{9,13},{10,... | collective-permute-start | bytes 196616 | tf_op jit(solution)/shard_map/ppermute | solution.py:344
  5.1 2.6 %collective-permute-start.4 = (bf16[8,4096]{1,0:T(8,128)(2,1)}, bf16[8,4096]{1,0:T(8,128)(2,1)S(1)}, u32[]{:S(2)}, u32[]{:S(2)}) collective-permute-start(bf16[8,4096]{1,0:T(8,128)(2,1)} %table_there.1), channel_id=1, source_target_pairs={{0,16},{8,24},{16,0},{24,8},{1,17},{9,25},{17,1},{25,9},{2,18},{10... | collective-permute-start | bytes 196616 | tf_op jit(solution)/shard_map/ppermute | solution.py:367
  7.7 1.3 %collective-permute-start.6 = (bf16[8,4096]{1,0:T(8,128)(2,1)}, bf16[8,4096]{1,0:T(8,128)(2,1)S(1)}, u32[]{:S(2)}, u32[]{:S(2)}) collective-permute-start(bf16[8,4096]{1,0:T(8,128)(2,1)} %table_there.1), channel_id=1, source_target_pairs={{0,24},{8,16},{16,8},{24,0},{1,25},{9,17},{17,9},{25,1},{2,26},{10... | collective-permute-start | bytes 196616 | tf_op jit(solution)/shard_map/ppermute | solution.py:367
  9.1 0.2 collective-permute-start.5
  9.3 0.0 collective-permute-done.1.after.refs_8_
  9.3 0.0 collective-permute-start.3
  9.3 1.5 %collective-permute-start.2 = (bf16[8,16,128]{2,1,0:T(8,128)(2,1)S(1)}, bf16[8,16,128]{2,1,0:T(8,128)(2,1)S(1)}, u32[]{:S(2)}, u32[]{:S(2)}) collective-permute-start(bf16[8,16,128]{2,1,0:T(8,128)(2,1)S(1)} %get-tuple-element.26), channel_id=1, source_target_pairs={{0,6},{1,7},{2,4},{3,5},{4,2},{5,3},{6,0},{7,1},{8,14},{9,15},{10,... | collective-permute-start | bytes 98312 | tf_op jit(solution)/shard_map/ppermute | solution.py:368
  11.5 2.2 %shard_map.88 = (s32[1,1,256]{2,1,0:T(1,128)S(4)}, s32[1,1,256]{2,1,0:T(1,128)S(4)}, bf16[128,256]{1,0:T(8,128)(2,1)S(1)}, bf16[1,1,128,128,128]{4,3,2,1,0:T(8,128)(2,1)S(1)}) custom-call(bf16[16,2048]{1,0:T(8,128)(2,1)S(1)} %collective-permute-done.1.after.refs_8_, s32[1,1,256]{2,1,0:T(1,128)} %rows_there.1, s32[1,1,256]{2,1,0:T(1,128)} %cols_there.1, ...), custom_call_target="tpu_custom_call" | custom-call | bytes 16777216 | tf_op jit(solution)/shard_map/pallas_call | solution.py:370
  13.7 0.0 collective-permute-done.4.refs_11_
  13.7 0.5 %collective-permute-done.6.refs_13_ = bf16[8,4096]{1,0:T(8,128)(2,1)S(1)} collective-permute-done((bf16[8,4096]{1,0:T(8,128)(2,1)}, bf16[8,4096]{1,0:T(8,128)(2,1)S(1)}, u32[]{:S(2)}, u32[]{:S(2)}) %collective-permute-start.6) | collective-permute-done | bytes 65568 | tf_op jit(solution)/shard_map/ppermute | solution.py:367
  14.2 0.2 collective-permute-done.5.refs_12_
  14.4 0.0 collective-permute-done.2.refs_7_
  14.4 0.0 collective-permute-done.3.refs_9_
  14.4 4.4 %shard_map.89 = (f32[8,16,128]{2,1,0:T(8,128)S(1)}, s16[9,16,128]{2,1,0:T(8,128)(2,1)S(1)}, s16[9,16,128]{2,1,0:T(8,128)(2,1)S(1)}, s16[9,16,128]{2,1,0:T(8,128)...) custom-call(s32[1,1]{1,0:T(1,128)S(6)} %copy.9.refs_0_, ...), custom_call_target="tpu_custom_call" | custom-call | flops 268435456 | bytes 16777216 | tf_op jit(solution)/shard_map/pallas_call | solution.py:388
  18.8 0.1 collective-permute-start.12
  18.9 0.5 %collective-permute-start.10 = (s16[9,16,128]{2,1,0:T(8,128)(2,1)S(1)}, s16[9,16,128]{2,1,0:T(8,128)(2,1)S(1)}, u32[]{:S(2)}, u32[]{:S(2)}) collective-permute-start(s16[9,16,128]{2,1,0:T(8,128)(2,1)S(1)} %get-tuple-element.33), channel_id=1, source_target_pairs={{0,1},{1,0},{2,3},{3,2},{4,5},{5,4},{6,7},{7,6},{8,9},{9,8},{10,11... | collective-permute-start | bytes 110600 | tf_op jit(solution)/shard_map/ppermute | solution.py:341
  19.4 0.1 collective-permute-start.8
  19.5 0.6 %collective-permute-done.12.got = s16[9,16,128]{2,1,0:T(8,128)(2,1)S(1)} collective-permute-done((s16[9,16,128]{2,1,0:T(8,128)(2,1)S(1)}, s16[9,16,128]{2,1,0:T(8,128)(2,1)S(1)}, u32[]{:S(2)}, u32[]{:S(2)}) %collective-permute-start.12) | collective-permute-done | bytes 36896 | tf_op jit(solution)/shard_map/ppermute | solution.py:341
  20.1 1.5 %collective-permute-start.13 = (s16[18,16,128]{2,1,0:T(8,128)(2,1)S(1)}, s16[18,16,128]{2,1,0:T(8,128)(2,1)S(1)}, u32[]{:S(2)}, u32[]{:S(2)}) collective-permute-start(s16[18,16,128]{2,1,0:T(8,128)(2,1)S(1)} %shard_map.93), channel_id=1, source_target_pairs={{0,6},{1,25},{2,4},{3,27},{4,2},{5,29},{6,0},{7,31},{8,14},{9,17},... | collective-permute-start | bytes 221192 | tf_op jit(solution)/shard_map/ppermute | solution.py:344
  21.6 0.0 collective-permute-done.10.got
  21.6 1.3 %collective-permute-start.11 = (s16[18,16,128]{2,1,0:T(8,128)(2,1)S(1)}, s16[18,16,128]{2,1,0:T(8,128)(2,1)S(1)}, u32[]{:S(2)}, u32[]{:S(2)}) collective-permute-start(s16[18,16,128]{2,1,0:T(8,128)(2,1)S(1)} %shard_map.92), channel_id=1, source_target_pairs={{0,4},{1,17},{2,6},{3,19},{4,0},{5,21},{6,2},{7,23},{8,12},{9,25},... | collective-permute-start | bytes 221192 | tf_op jit(solution)/shard_map/ppermute | solution.py:344
  23.0 0.0 collective-permute-done.8.got
  23.0 0.9 %collective-permute-start.9 = (s16[18,16,128]{2,1,0:T(8,128)(2,1)S(1)}, s16[18,16,128]{2,1,0:T(8,128)(2,1)S(1)}, u32[]{:S(2)}, u32[]{:S(2)}) collective-permute-start(s16[18,16,128]{2,1,0:T(8,128)(2,1)S(1)} %shard_map.91), channel_id=1, source_target_pairs={{0,2},{1,9},{2,0},{3,11},{4,6},{5,13},{6,4},{7,15},{8,10},{9,1},{1... | collective-permute-start | bytes 221192 | tf_op jit(solution)/shard_map/ppermute | solution.py:344
  23.9 0.2 collective-permute-start.7
  24.1 1.0 %collective-permute-done.7.got = f32[8,16,128]{2,1,0:T(8,128)S(1)} collective-permute-done((f32[8,16,128]{2,1,0:T(8,128)S(1)}, f32[8,16,128]{2,1,0:T(8,128)S(1)}, u32[]{:S(2)}, u32[]{:S(2)}) %collective-permute-start.7) | collective-permute-done | bytes 65568 | tf_op jit(solution)/shard_map/ppermute | solution.py:341
  25.2 0.3 %collective-permute-done.13.refs_3_ = s16[18,16,128]{2,1,0:T(8,128)(2,1)S(1)} collective-permute-done((s16[18,16,128]{2,1,0:T(8,128)(2,1)S(1)}, s16[18,16,128]{2,1,0:T(8,128)(2,1)S(1)}, u32[]{:S(2)}, u32[]{:S(2)}) %collective-permute-start.13) | collective-permute-done | bytes 73760 | tf_op jit(solution)/shard_map/ppermute | solution.py:344
  25.5 0.8 %collective-permute-done.11.refs_2_ = s16[18,16,128]{2,1,0:T(8,128)(2,1)S(1)} collective-permute-done((s16[18,16,128]{2,1,0:T(8,128)(2,1)S(1)}, s16[18,16,128]{2,1,0:T(8,128)(2,1)S(1)}, u32[]{:S(2)}, u32[]{:S(2)}) %collective-permute-start.11) | collective-permute-done | bytes 73760 | tf_op jit(solution)/shard_map/ppermute | solution.py:344
  26.2 1.2 %collective-permute-done.9.refs_1_ = s16[18,16,128]{2,1,0:T(8,128)(2,1)S(1)} collective-permute-done((s16[18,16,128]{2,1,0:T(8,128)(2,1)S(1)}, s16[18,16,128]{2,1,0:T(8,128)(2,1)S(1)}, u32[]{:S(2)}, u32[]{:S(2)}) %collective-permute-start.9) | collective-permute-done | bytes 73760 | tf_op jit(solution)/shard_map/ppermute | solution.py:344
  27.4 0.1 shard_map.94
  27.5 0.3 %collective-permute-start.14 = (f32[8,16,128]{2,1,0:T(8,128)S(1)}, f32[8,16,128]{2,1,0:T(8,128)S(1)}, u32[]{:S(2)}, u32[]{:S(2)}) collective-permute-start(f32[8,16,128]{2,1,0:T(8,128)S(1)} %get-tuple-element.37), channel_id=1, source_target_pairs={{0,1},{1,0},{2,3},{3,2},{4,5},{5,4},{6,7},{7,6},{8,9},{9,8},{10,11... | collective-permute-start | bytes 196616 | tf_op jit(solution)/shard_map/ppermute | solution.py:341
  27.8 1.0 %collective-permute-done.14.got = f32[8,16,128]{2,1,0:T(8,128)S(1)} collective-permute-done((f32[8,16,128]{2,1,0:T(8,128)S(1)}, f32[8,16,128]{2,1,0:T(8,128)S(1)}, u32[]{:S(2)}, u32[]{:S(2)}) %collective-permute-start.14) | collective-permute-done | bytes 65568 | tf_op jit(solution)/shard_map/ppermute | solution.py:341
  28.8 0.7 %shard_map.95 = (f32[16,1024]{1,0:T(8,128)}, f32[4,4096]{1,0:T(4,128)}) custom-call(f32[8,16,128]{2,1,0:T(8,128)S(1)} %get-tuple-element.36.keep, f32[8,16,128]{2,1,0:T(8,128)S(1)} %collective-permute-done.14.got), custom_call_target="tpu_custom_call" | custom-call | tf_op jit(solution)/shard_map/pallas_call | solution.py:426
  (5 shorter events, 0.1 us)
Async XLA Ops:
  0.6 1.6 %collective-permute-start = (bf16[16,1024]{1,0:T(8,128)(2,1)}, bf16[16,1024]{1,0:T(8,128)(2,1)S(1)}, u32[]{:S(2)}, u32[]{:S(2)}) collective-permute-start(bf16[16,1024]{1,0:T(8,128)(2,1)} %shard_there.1), channel_id=1, source_target_pairs={{0,1},{1,0},{2,3},{3,2},{4,5},{5,4},{6,7},{7,6},{8,9},{9,8},{10,11... | collective-permute-start | bytes 98312 | tf_op jit(solution)/shard_map/ppermute | solution.py:341
  2.2 7.1 %collective-permute-start.1 = (bf16[16,2048]{1,0:T(8,128)(2,1)S(1)}, bf16[16,2048]{1,0:T(8,128)(2,1)S(1)}, u32[]{:S(2)}, u32[]{:S(2)}) collective-permute-start(bf16[16,2048]{1,0:T(8,128)(2,1)S(1)} %get-tuple-element.21.refs_6_), channel_id=1, source_target_pairs={{0,2},{1,5},{2,0},{3,7},{4,6},{5,1},{6,4},{7,3},{8,10},{9,13},{10,... | collective-permute-start | bytes 196616 | tf_op jit(solution)/shard_map/ppermute | solution.py:344
  5.1 8.6 %collective-permute-start.4 = (bf16[8,4096]{1,0:T(8,128)(2,1)}, bf16[8,4096]{1,0:T(8,128)(2,1)S(1)}, u32[]{:S(2)}, u32[]{:S(2)}) collective-permute-start(bf16[8,4096]{1,0:T(8,128)(2,1)} %table_there.1), channel_id=1, source_target_pairs={{0,16},{8,24},{16,0},{24,8},{1,17},{9,25},{17,1},{25,9},{2,18},{10... | collective-permute-start | bytes 196616 | tf_op jit(solution)/shard_map/ppermute | solution.py:367
  7.7 6.5 %collective-permute-start.6 = (bf16[8,4096]{1,0:T(8,128)(2,1)}, bf16[8,4096]{1,0:T(8,128)(2,1)S(1)}, u32[]{:S(2)}, u32[]{:S(2)}) collective-permute-start(bf16[8,4096]{1,0:T(8,128)(2,1)} %table_there.1), channel_id=1, source_target_pairs={{0,24},{8,16},{16,8},{24,0},{1,25},{9,17},{17,9},{25,1},{2,26},{10... | collective-permute-start | bytes 196616 | tf_op jit(solution)/shard_map/ppermute | solution.py:367
  9.1 5.3 %collective-permute-start.5 = (bf16[8,4096]{1,0:T(8,128)(2,1)}, bf16[8,4096]{1,0:T(8,128)(2,1)S(1)}, u32[]{:S(2)}, u32[]{:S(2)}) collective-permute-start(bf16[8,4096]{1,0:T(8,128)(2,1)} %table_there.1), channel_id=1, source_target_pairs={{0,8},{8,0},{16,24},{24,16},{1,9},{9,1},{17,25},{25,17},{2,10},{10... | collective-permute-start | bytes 196616 | tf_op jit(solution)/shard_map/ppermute | solution.py:367
  9.3 5.1 %collective-permute-start.3 = (bf16[16,2048]{1,0:T(8,128)(2,1)S(1)}, bf16[16,2048]{1,0:T(8,128)(2,1)S(1)}, u32[]{:S(2)}, u32[]{:S(2)}) collective-permute-start(bf16[16,2048]{1,0:T(8,128)(2,1)S(1)} %collective-permute-done.1.after.refs_8_), channel_id=1, source_target_pairs={{0,1},{1,0},{2,3},{3,2},{4,5},{5,4},{6,7},{7,6},{8,9},{9,8},{10,11... | collective-permute-start | bytes 196616 | tf_op jit(solution)/shard_map/ppermute | solution.py:341
  9.3 5.1 %collective-permute-start.2 = (bf16[8,16,128]{2,1,0:T(8,128)(2,1)S(1)}, bf16[8,16,128]{2,1,0:T(8,128)(2,1)S(1)}, u32[]{:S(2)}, u32[]{:S(2)}) collective-permute-start(bf16[8,16,128]{2,1,0:T(8,128)(2,1)S(1)} %get-tuple-element.26), channel_id=1, source_target_pairs={{0,6},{1,7},{2,4},{3,5},{4,2},{5,3},{6,0},{7,1},{8,14},{9,15},{10,... | collective-permute-start | bytes 98312 | tf_op jit(solution)/shard_map/ppermute | solution.py:368
  18.8 1.3 %collective-permute-start.12 = (s16[9,16,128]{2,1,0:T(8,128)(2,1)S(1)}, s16[9,16,128]{2,1,0:T(8,128)(2,1)S(1)}, u32[]{:S(2)}, u32[]{:S(2)}) collective-permute-start(s16[9,16,128]{2,1,0:T(8,128)(2,1)S(1)} %get-tuple-element.35), channel_id=1, source_target_pairs={{0,1},{1,0},{2,3},{3,2},{4,5},{5,4},{6,7},{7,6},{8,9},{9,8},{10,11... | collective-permute-start | bytes 110600 | tf_op jit(solution)/shard_map/ppermute | solution.py:341
  18.9 2.7 %collective-permute-start.10 = (s16[9,16,128]{2,1,0:T(8,128)(2,1)S(1)}, s16[9,16,128]{2,1,0:T(8,128)(2,1)S(1)}, u32[]{:S(2)}, u32[]{:S(2)}) collective-permute-start(s16[9,16,128]{2,1,0:T(8,128)(2,1)S(1)} %get-tuple-element.33), channel_id=1, source_target_pairs={{0,1},{1,0},{2,3},{3,2},{4,5},{5,4},{6,7},{7,6},{8,9},{9,8},{10,11... | collective-permute-start | bytes 110600 | tf_op jit(solution)/shard_map/ppermute | solution.py:341
  19.4 3.6 %collective-permute-start.8 = (s16[9,16,128]{2,1,0:T(8,128)(2,1)S(1)}, s16[9,16,128]{2,1,0:T(8,128)(2,1)S(1)}, u32[]{:S(2)}, u32[]{:S(2)}) collective-permute-start(s16[9,16,128]{2,1,0:T(8,128)(2,1)S(1)} %get-tuple-element.31), channel_id=1, source_target_pairs={{0,1},{1,0},{2,3},{3,2},{4,5},{5,4},{6,7},{7,6},{8,9},{9,8},{10,11... | collective-permute-start | bytes 110600 | tf_op jit(solution)/shard_map/ppermute | solution.py:341
  20.1 5.3 %collective-permute-start.13 = (s16[18,16,128]{2,1,0:T(8,128)(2,1)S(1)}, s16[18,16,128]{2,1,0:T(8,128)(2,1)S(1)}, u32[]{:S(2)}, u32[]{:S(2)}) collective-permute-start(s16[18,16,128]{2,1,0:T(8,128)(2,1)S(1)} %shard_map.93), channel_id=1, source_target_pairs={{0,6},{1,25},{2,4},{3,27},{4,2},{5,29},{6,0},{7,31},{8,14},{9,17},... | collective-permute-start | bytes 221192 | tf_op jit(solution)/shard_map/ppermute | solution.py:344
  21.6 4.6 %collective-permute-start.11 = (s16[18,16,128]{2,1,0:T(8,128)(2,1)S(1)}, s16[18,16,128]{2,1,0:T(8,128)(2,1)S(1)}, u32[]{:S(2)}, u32[]{:S(2)}) collective-permute-start(s16[18,16,128]{2,1,0:T(8,128)(2,1)S(1)} %shard_map.92), channel_id=1, source_target_pairs={{0,4},{1,17},{2,6},{3,19},{4,0},{5,21},{6,2},{7,23},{8,12},{9,25},... | collective-permute-start | bytes 221192 | tf_op jit(solution)/shard_map/ppermute | solution.py:344
  23.0 4.4 %collective-permute-start.9 = (s16[18,16,128]{2,1,0:T(8,128)(2,1)S(1)}, s16[18,16,128]{2,1,0:T(8,128)(2,1)S(1)}, u32[]{:S(2)}, u32[]{:S(2)}) collective-permute-start(s16[18,16,128]{2,1,0:T(8,128)(2,1)S(1)} %shard_map.91), channel_id=1, source_target_pairs={{0,2},{1,9},{2,0},{3,11},{4,6},{5,13},{6,4},{7,15},{8,10},{9,1},{1... | collective-permute-start | bytes 221192 | tf_op jit(solution)/shard_map/ppermute | solution.py:344
  23.9 1.3 %collective-permute-start.7 = (f32[8,16,128]{2,1,0:T(8,128)S(1)}, f32[8,16,128]{2,1,0:T(8,128)S(1)}, u32[]{:S(2)}, u32[]{:S(2)}) collective-permute-start(f32[8,16,128]{2,1,0:T(8,128)S(1)} %get-tuple-element.29), channel_id=1, source_target_pairs={{0,1},{1,0},{2,3},{3,2},{4,5},{5,4},{6,7},{7,6},{8,9},{9,8},{10,11... | collective-permute-start | bytes 196616 | tf_op jit(solution)/shard_map/ppermute | solution.py:341
  27.5 1.3 %collective-permute-start.14 = (f32[8,16,128]{2,1,0:T(8,128)S(1)}, f32[8,16,128]{2,1,0:T(8,128)S(1)}, u32[]{:S(2)}, u32[]{:S(2)}) collective-permute-start(f32[8,16,128]{2,1,0:T(8,128)S(1)} %get-tuple-element.37), channel_id=1, source_target_pairs={{0,1},{1,0},{2,3},{3,2},{4,5},{5,4},{6,7},{7,6},{8,9},{9,8},{10,11... | collective-permute-start | bytes 196616 | tf_op jit(solution)/shard_map/ppermute | solution.py:341

commit v7 on v6

--- a/solution.py
+++ b/solution.py
@@ -9,8 +9,8 @@
 
 BLK = 128
 REWARDS = 16
-LATE = 128
-PART = 64
+LATE = 160
+PART = 32
 SUMS = 1
 GRAIN = 128
 MOST = 32767.0

time: 29.7 us -> 29.8 us (level)
    pallas_call x1, Pallas kernels: 2.23 us -> 1.93 us  [on_device(): pl.pallas_call(prefetch_kernel, out_shape=[pltpu.SMEM(slot_rows.shape, sl...]
    ppermute x3, waiting for transfers between devices: 0.68 us -> 0.97 us  [on_device(): lax.ppermute(reward_table, 'row', peers(n_row, step))]
  transfers between devices with their start and end apart: 15 -> 15, of which waited for: 9 -> 9; matrix products, arithmetic and copies ran while one was open for 0% -> 0% of each run, Pallas kernels for 11% -> 10%
where the time goes in v7:
time: 29.8 us; the launch traced here: 29.6 us
  starting transfers between devices  14 us (47%)
  Pallas kernels  8.15 us (27%)
  waiting for transfers between devices  6.06 us (20%)
  between operations  1.37 us (5%)
    ppermute x4, starting transfers between devices, cross(): lax.ppermute(part, ('row', 'col'), crossings(n_row, n_col, first, second))  6.58 us
    pallas_call x1, Pallas kernels, on_device(): pl.pallas_call(functools.partial(products_kernel, n_row, n_col), out_shap...  4.53 us
    ppermute x3, starting transfers between devices, on_device(): lax.ppermute(reward_table, 'row', peers(n_row, step))  4.17 us
    ppermute x7, waiting for transfers between devices, swap(): return lax.ppermute(part, 'col', peers(n_col, 1))  2.82 us
    ppermute x4, waiting for transfers between devices, cross(): lax.ppermute(part, ('row', 'col'), crossings(n_row, n_col, first, second))  2.26 us
    pallas_call x1, Pallas kernels, on_device(): pl.pallas_call(prefetch_kernel, out_shape=[pltpu.SMEM(slot_rows.shape, sl...  1.93 us
    ppermute x7, starting transfers between devices, swap(): return lax.ppermute(part, 'col', peers(n_col, 1))  1.74 us
    ppermute x1, starting transfers between devices, on_device(): opposite = lax.ppermute(cells, 'col', peers(n_col, 2 * (n_chip - 1)))  1.49 us
  transfers between devices with their start and end apart: 15, of which 9 were waited for; matrix products, arithmetic and copies ran while one was open for 0% of the time, Pallas kernels for 10%

profile of v7, /device:TPU:0, one launch (start us, length us, event | category | flops | bytes accessed | tf_op | source)
XLA Modules:
  0.0 29.6 jit_solution(13580129412098341391)
XLA Ops:
  0.6 0.5 %collective-permute-start = (bf16[16,1024]{1,0:T(8,128)(2,1)}, bf16[16,1024]{1,0:T(8,128)(2,1)S(1)}, u32[]{:S(2)}, u32[]{:S(2)}) collective-permute-start(bf16[16,1024]{1,0:T(8,128)(2,1)} %shard_there.1), channel_id=1, source_target_pairs={{0,1},{1,0},{2,3},{3,2},{4,5},{5,4},{6,7},{7,6},{8,9},{9,8},{10,11... | collective-permute-start | bytes 98312 | tf_op jit(solution)/shard_map/ppermute | solution.py:341
  1.1 0.9 %shard_map.86 = (bf16[16,1024]{1,0:T(8,128)(2,1)S(1)}, bf16[8,4096]{1,0:T(8,128)(2,1)S(1)}) custom-call(bf16[16,1024]{1,0:T(8,128)(2,1)} %shard_there.1, bf16[8,4096]{1,0:T(8,128)(2,1)} %table_there.1), custom_call_target="tpu_custom_call" | custom-call | bytes 4194304 | tf_op jit(solution)/shard_map/pallas_call | solution.py:346
  2.0 0.2 collective-permute-done.other_shard
  2.2 2.9 %collective-permute-start.1 = (bf16[16,2048]{1,0:T(8,128)(2,1)S(1)}, bf16[16,2048]{1,0:T(8,128)(2,1)S(1)}, u32[]{:S(2)}, u32[]{:S(2)}) collective-permute-start(bf16[16,2048]{1,0:T(8,128)(2,1)S(1)} %get-tuple-element.21.refs_6_), channel_id=1, source_target_pairs={{0,2},{1,5},{2,0},{3,7},{4,6},{5,1},{6,4},{7,3},{8,10},{9,13},{10,... | collective-permute-start | bytes 196616 | tf_op jit(solution)/shard_map/ppermute | solution.py:344
  5.1 2.6 %collective-permute-start.4 = (bf16[8,4096]{1,0:T(8,128)(2,1)}, bf16[8,4096]{1,0:T(8,128)(2,1)S(1)}, u32[]{:S(2)}, u32[]{:S(2)}) collective-permute-start(bf16[8,4096]{1,0:T(8,128)(2,1)} %table_there.1), channel_id=1, source_target_pairs={{0,16},{8,24},{16,0},{24,8},{1,17},{9,25},{17,1},{25,9},{2,18},{10... | collective-permute-start | bytes 196616 | tf_op jit(solution)/shard_map/ppermute | solution.py:367
  7.7 1.3 %collective-permute-start.6 = (bf16[8,4096]{1,0:T(8,128)(2,1)}, bf16[8,4096]{1,0:T(8,128)(2,1)S(1)}, u32[]{:S(2)}, u32[]{:S(2)}) collective-permute-start(bf16[8,4096]{1,0:T(8,128)(2,1)} %table_there.1), channel_id=1, source_target_pairs={{0,24},{8,16},{16,8},{24,0},{1,25},{9,17},{17,9},{25,1},{2,26},{10... | collective-permute-start | bytes 196616 | tf_op jit(solution)/shard_map/ppermute | solution.py:367
  9.1 0.2 collective-permute-start.5
  9.3 0.0 collective-permute-done.1.after.refs_8_
  9.3 0.0 collective-permute-start.3
  9.3 1.5 %collective-permute-start.2 = (bf16[8,16,128]{2,1,0:T(8,128)(2,1)S(1)}, bf16[8,16,128]{2,1,0:T(8,128)(2,1)S(1)}, u32[]{:S(2)}, u32[]{:S(2)}) collective-permute-start(bf16[8,16,128]{2,1,0:T(8,128)(2,1)S(1)} %get-tuple-element.26), channel_id=1, source_target_pairs={{0,6},{1,7},{2,4},{3,5},{4,2},{5,3},{6,0},{7,1},{8,14},{9,15},{10,... | collective-permute-start | bytes 98312 | tf_op jit(solution)/shard_map/ppermute | solution.py:368
  11.5 1.9 %shard_map.88 = (s32[1,1,256]{2,1,0:T(1,128)S(4)}, s32[1,1,256]{2,1,0:T(1,128)S(4)}, bf16[128,256]{1,0:T(8,128)(2,1)S(1)}, bf16[1,1,96,128,128]{4,3,2,1,0:T(8,128)(2,1)S(1)}) custom-call(bf16[16,2048]{1,0:T(8,128)(2,1)S(1)} %collective-permute-done.1.after.refs_8_, s32[1,1,256]{2,1,0:T(1,128)} %rows_there.1, s32[1,1,256]{2,1,0:T(1,128)} %cols_there.1, ...), custom_call_target="tpu_custom_call" | custom-call | bytes 16777216 | tf_op jit(solution)/shard_map/pallas_call | solution.py:370
  13.4 0.0 collective-permute-done.4.refs_11_
  13.4 0.8 %collective-permute-done.6.refs_13_ = bf16[8,4096]{1,0:T(8,128)(2,1)S(1)} collective-permute-done((bf16[8,4096]{1,0:T(8,128)(2,1)}, bf16[8,4096]{1,0:T(8,128)(2,1)S(1)}, u32[]{:S(2)}, u32[]{:S(2)}) %collective-permute-start.6) | collective-permute-done | bytes 65568 | tf_op jit(solution)/shard_map/ppermute | solution.py:367
  14.2 0.2 collective-permute-done.5.refs_12_
  14.4 0.0 collective-permute-done.2.refs_7_
  14.4 0.0 collective-permute-done.3.refs_9_
  14.4 4.5 %shard_map.89 = (f32[8,16,128]{2,1,0:T(8,128)S(1)}, s16[9,16,128]{2,1,0:T(8,128)(2,1)S(1)}, s16[9,16,128]{2,1,0:T(8,128)(2,1)S(1)}, s16[9,16,128]{2,1,0:T(8,128)...) custom-call(s32[1,1]{1,0:T(1,128)S(6)} %copy.9.refs_0_, ...), custom_call_target="tpu_custom_call" | custom-call | flops 268435456 | bytes 16777216 | tf_op jit(solution)/shard_map/pallas_call | solution.py:388
  18.9 0.1 collective-permute-start.12
  19.0 0.5 %collective-permute-start.10 = (s16[9,16,128]{2,1,0:T(8,128)(2,1)S(1)}, s16[9,16,128]{2,1,0:T(8,128)(2,1)S(1)}, u32[]{:S(2)}, u32[]{:S(2)}) collective-permute-start(s16[9,16,128]{2,1,0:T(8,128)(2,1)S(1)} %get-tuple-element.33), channel_id=1, source_target_pairs={{0,1},{1,0},{2,3},{3,2},{4,5},{5,4},{6,7},{7,6},{8,9},{9,8},{10,11... | collective-permute-start | bytes 110600 | tf_op jit(solution)/shard_map/ppermute | solution.py:341
  19.5 0.1 collective-permute-start.8
  19.6 0.6 %collective-permute-done.12.got = s16[9,16,128]{2,1,0:T(8,128)(2,1)S(1)} collective-permute-done((s16[9,16,128]{2,1,0:T(8,128)(2,1)S(1)}, s16[9,16,128]{2,1,0:T(8,128)(2,1)S(1)}, u32[]{:S(2)}, u32[]{:S(2)}) %collective-permute-start.12) | collective-permute-done | bytes 36896 | tf_op jit(solution)/shard_map/ppermute | solution.py:341
  20.2 1.4 %collective-permute-start.13 = (s16[18,16,128]{2,1,0:T(8,128)(2,1)S(1)}, s16[18,16,128]{2,1,0:T(8,128)(2,1)S(1)}, u32[]{:S(2)}, u32[]{:S(2)}) collective-permute-start(s16[18,16,128]{2,1,0:T(8,128)(2,1)S(1)} %shard_map.93), channel_id=1, source_target_pairs={{0,6},{1,25},{2,4},{3,27},{4,2},{5,29},{6,0},{7,31},{8,14},{9,17},... | collective-permute-start | bytes 221192 | tf_op jit(solution)/shard_map/ppermute | solution.py:344
  21.7 0.0 collective-permute-done.10.got
  21.7 1.4 %collective-permute-start.11 = (s16[18,16,128]{2,1,0:T(8,128)(2,1)S(1)}, s16[18,16,128]{2,1,0:T(8,128)(2,1)S(1)}, u32[]{:S(2)}, u32[]{:S(2)}) collective-permute-start(s16[18,16,128]{2,1,0:T(8,128)(2,1)S(1)} %shard_map.92), channel_id=1, source_target_pairs={{0,4},{1,17},{2,6},{3,19},{4,0},{5,21},{6,2},{7,23},{8,12},{9,25},... | collective-permute-start | bytes 221192 | tf_op jit(solution)/shard_map/ppermute | solution.py:344
  23.1 0.0 collective-permute-done.8.got
  23.1 0.9 %collective-permute-start.9 = (s16[18,16,128]{2,1,0:T(8,128)(2,1)S(1)}, s16[18,16,128]{2,1,0:T(8,128)(2,1)S(1)}, u32[]{:S(2)}, u32[]{:S(2)}) collective-permute-start(s16[18,16,128]{2,1,0:T(8,128)(2,1)S(1)} %shard_map.91), channel_id=1, source_target_pairs={{0,2},{1,9},{2,0},{3,11},{4,6},{5,13},{6,4},{7,15},{8,10},{9,1},{1... | collective-permute-start | bytes 221192 | tf_op jit(solution)/shard_map/ppermute | solution.py:344
  24.0 0.2 collective-permute-start.7
  24.2 1.0 %collective-permute-done.7.got = f32[8,16,128]{2,1,0:T(8,128)S(1)} collective-permute-done((f32[8,16,128]{2,1,0:T(8,128)S(1)}, f32[8,16,128]{2,1,0:T(8,128)S(1)}, u32[]{:S(2)}, u32[]{:S(2)}) %collective-permute-start.7) | collective-permute-done | bytes 65568 | tf_op jit(solution)/shard_map/ppermute | solution.py:341
  25.2 0.3 %collective-permute-done.13.refs_3_ = s16[18,16,128]{2,1,0:T(8,128)(2,1)S(1)} collective-permute-done((s16[18,16,128]{2,1,0:T(8,128)(2,1)S(1)}, s16[18,16,128]{2,1,0:T(8,128)(2,1)S(1)}, u32[]{:S(2)}, u32[]{:S(2)}) %collective-permute-start.13) | collective-permute-done | bytes 73760 | tf_op jit(solution)/shard_map/ppermute | solution.py:344
  25.6 0.8 %collective-permute-done.11.refs_2_ = s16[18,16,128]{2,1,0:T(8,128)(2,1)S(1)} collective-permute-done((s16[18,16,128]{2,1,0:T(8,128)(2,1)S(1)}, s16[18,16,128]{2,1,0:T(8,128)(2,1)S(1)}, u32[]{:S(2)}, u32[]{:S(2)}) %collective-permute-start.11) | collective-permute-done | bytes 73760 | tf_op jit(solution)/shard_map/ppermute | solution.py:344
  26.3 1.2 %collective-permute-done.9.refs_1_ = s16[18,16,128]{2,1,0:T(8,128)(2,1)S(1)} collective-permute-done((s16[18,16,128]{2,1,0:T(8,128)(2,1)S(1)}, s16[18,16,128]{2,1,0:T(8,128)(2,1)S(1)}, u32[]{:S(2)}, u32[]{:S(2)}) %collective-permute-start.9) | collective-permute-done | bytes 73760 | tf_op jit(solution)/shard_map/ppermute | solution.py:344
  27.5 0.1 shard_map.94
  27.6 0.4 %collective-permute-start.14 = (f32[8,16,128]{2,1,0:T(8,128)S(1)}, f32[8,16,128]{2,1,0:T(8,128)S(1)}, u32[]{:S(2)}, u32[]{:S(2)}) collective-permute-start(f32[8,16,128]{2,1,0:T(8,128)S(1)} %get-tuple-element.37), channel_id=1, source_target_pairs={{0,1},{1,0},{2,3},{3,2},{4,5},{5,4},{6,7},{7,6},{8,9},{9,8},{10,11... | collective-permute-start | bytes 196616 | tf_op jit(solution)/shard_map/ppermute | solution.py:341
  27.9 1.0 %collective-permute-done.14.got = f32[8,16,128]{2,1,0:T(8,128)S(1)} collective-permute-done((f32[8,16,128]{2,1,0:T(8,128)S(1)}, f32[8,16,128]{2,1,0:T(8,128)S(1)}, u32[]{:S(2)}, u32[]{:S(2)}) %collective-permute-start.14) | collective-permute-done | bytes 65568 | tf_op jit(solution)/shard_map/ppermute | solution.py:341
  28.9 0.7 %shard_map.95 = (f32[16,1024]{1,0:T(8,128)}, f32[4,4096]{1,0:T(4,128)}) custom-call(f32[8,16,128]{2,1,0:T(8,128)S(1)} %get-tuple-element.36.keep, f32[8,16,128]{2,1,0:T(8,128)S(1)} %collective-permute-done.14.got), custom_call_target="tpu_custom_call" | custom-call | tf_op jit(solution)/shard_map/pallas_call | solution.py:426
  (5 shorter events, 0.1 us)
Async XLA Ops:
  0.6 1.6 %collective-permute-start = (bf16[16,1024]{1,0:T(8,128)(2,1)}, bf16[16,1024]{1,0:T(8,128)(2,1)S(1)}, u32[]{:S(2)}, u32[]{:S(2)}) collective-permute-start(bf16[16,1024]{1,0:T(8,128)(2,1)} %shard_there.1), channel_id=1, source_target_pairs={{0,1},{1,0},{2,3},{3,2},{4,5},{5,4},{6,7},{7,6},{8,9},{9,8},{10,11... | collective-permute-start | bytes 98312 | tf_op jit(solution)/shard_map/ppermute | solution.py:341
  2.2 7.1 %collective-permute-start.1 = (bf16[16,2048]{1,0:T(8,128)(2,1)S(1)}, bf16[16,2048]{1,0:T(8,128)(2,1)S(1)}, u32[]{:S(2)}, u32[]{:S(2)}) collective-permute-start(bf16[16,2048]{1,0:T(8,128)(2,1)S(1)} %get-tuple-element.21.refs_6_), channel_id=1, source_target_pairs={{0,2},{1,5},{2,0},{3,7},{4,6},{5,1},{6,4},{7,3},{8,10},{9,13},{10,... | collective-permute-start | bytes 196616 | tf_op jit(solution)/shard_map/ppermute | solution.py:344
  5.1 8.3 %collective-permute-start.4 = (bf16[8,4096]{1,0:T(8,128)(2,1)}, bf16[8,4096]{1,0:T(8,128)(2,1)S(1)}, u32[]{:S(2)}, u32[]{:S(2)}) collective-permute-start(bf16[8,4096]{1,0:T(8,128)(2,1)} %table_there.1), channel_id=1, source_target_pairs={{0,16},{8,24},{16,0},{24,8},{1,17},{9,25},{17,1},{25,9},{2,18},{10... | collective-permute-start | bytes 196616 | tf_op jit(solution)/shard_map/ppermute | solution.py:367
  7.7 6.5 %collective-permute-start.6 = (bf16[8,4096]{1,0:T(8,128)(2,1)}, bf16[8,4096]{1,0:T(8,128)(2,1)S(1)}, u32[]{:S(2)}, u32[]{:S(2)}) collective-permute-start(bf16[8,4096]{1,0:T(8,128)(2,1)} %table_there.1), channel_id=1, source_target_pairs={{0,24},{8,16},{16,8},{24,0},{1,25},{9,17},{17,9},{25,1},{2,26},{10... | collective-permute-start | bytes 196616 | tf_op jit(solution)/shard_map/ppermute | solution.py:367
  9.1 5.3 %collective-permute-start.5 = (bf16[8,4096]{1,0:T(8,128)(2,1)}, bf16[8,4096]{1,0:T(8,128)(2,1)S(1)}, u32[]{:S(2)}, u32[]{:S(2)}) collective-permute-start(bf16[8,4096]{1,0:T(8,128)(2,1)} %table_there.1), channel_id=1, source_target_pairs={{0,8},{8,0},{16,24},{24,16},{1,9},{9,1},{17,25},{25,17},{2,10},{10... | collective-permute-start | bytes 196616 | tf_op jit(solution)/shard_map/ppermute | solution.py:367
  9.3 5.1 %collective-permute-start.3 = (bf16[16,2048]{1,0:T(8,128)(2,1)S(1)}, bf16[16,2048]{1,0:T(8,128)(2,1)S(1)}, u32[]{:S(2)}, u32[]{:S(2)}) collective-permute-start(bf16[16,2048]{1,0:T(8,128)(2,1)S(1)} %collective-permute-done.1.after.refs_8_), channel_id=1, source_target_pairs={{0,1},{1,0},{2,3},{3,2},{4,5},{5,4},{6,7},{7,6},{8,9},{9,8},{10,11... | collective-permute-start | bytes 196616 | tf_op jit(solution)/shard_map/ppermute | solution.py:341
  9.3 5.1 %collective-permute-start.2 = (bf16[8,16,128]{2,1,0:T(8,128)(2,1)S(1)}, bf16[8,16,128]{2,1,0:T(8,128)(2,1)S(1)}, u32[]{:S(2)}, u32[]{:S(2)}) collective-permute-start(bf16[8,16,128]{2,1,0:T(8,128)(2,1)S(1)} %get-tuple-element.26), channel_id=1, source_target_pairs={{0,6},{1,7},{2,4},{3,5},{4,2},{5,3},{6,0},{7,1},{8,14},{9,15},{10,... | collective-permute-start | bytes 98312 | tf_op jit(solution)/shard_map/ppermute | solution.py:368
  18.9 1.3 %collective-permute-start.12 = (s16[9,16,128]{2,1,0:T(8,128)(2,1)S(1)}, s16[9,16,128]{2,1,0:T(8,128)(2,1)S(1)}, u32[]{:S(2)}, u32[]{:S(2)}) collective-permute-start(s16[9,16,128]{2,1,0:T(8,128)(2,1)S(1)} %get-tuple-element.35), channel_id=1, source_target_pairs={{0,1},{1,0},{2,3},{3,2},{4,5},{5,4},{6,7},{7,6},{8,9},{9,8},{10,11... | collective-permute-start | bytes 110600 | tf_op jit(solution)/shard_map/ppermute | solution.py:341
  19.0 2.7 %collective-permute-start.10 = (s16[9,16,128]{2,1,0:T(8,128)(2,1)S(1)}, s16[9,16,128]{2,1,0:T(8,128)(2,1)S(1)}, u32[]{:S(2)}, u32[]{:S(2)}) collective-permute-start(s16[9,16,128]{2,1,0:T(8,128)(2,1)S(1)} %get-tuple-element.33), channel_id=1, source_target_pairs={{0,1},{1,0},{2,3},{3,2},{4,5},{5,4},{6,7},{7,6},{8,9},{9,8},{10,11... | collective-permute-start | bytes 110600 | tf_op jit(solution)/shard_map/ppermute | solution.py:341
  19.5 3.6 %collective-permute-start.8 = (s16[9,16,128]{2,1,0:T(8,128)(2,1)S(1)}, s16[9,16,128]{2,1,0:T(8,128)(2,1)S(1)}, u32[]{:S(2)}, u32[]{:S(2)}) collective-permute-start(s16[9,16,128]{2,1,0:T(8,128)(2,1)S(1)} %get-tuple-element.31), channel_id=1, source_target_pairs={{0,1},{1,0},{2,3},{3,2},{4,5},{5,4},{6,7},{7,6},{8,9},{9,8},{10,11... | collective-permute-start | bytes 110600 | tf_op jit(solution)/shard_map/ppermute | solution.py:341
  20.2 5.3 %collective-permute-start.13 = (s16[18,16,128]{2,1,0:T(8,128)(2,1)S(1)}, s16[18,16,128]{2,1,0:T(8,128)(2,1)S(1)}, u32[]{:S(2)}, u32[]{:S(2)}) collective-permute-start(s16[18,16,128]{2,1,0:T(8,128)(2,1)S(1)} %shard_map.93), channel_id=1, source_target_pairs={{0,6},{1,25},{2,4},{3,27},{4,2},{5,29},{6,0},{7,31},{8,14},{9,17},... | collective-permute-start | bytes 221192 | tf_op jit(solution)/shard_map/ppermute | solution.py:344
  21.7 4.6 %collective-permute-start.11 = (s16[18,16,128]{2,1,0:T(8,128)(2,1)S(1)}, s16[18,16,128]{2,1,0:T(8,128)(2,1)S(1)}, u32[]{:S(2)}, u32[]{:S(2)}) collective-permute-start(s16[18,16,128]{2,1,0:T(8,128)(2,1)S(1)} %shard_map.92), channel_id=1, source_target_pairs={{0,4},{1,17},{2,6},{3,19},{4,0},{5,21},{6,2},{7,23},{8,12},{9,25},... | collective-permute-start | bytes 221192 | tf_op jit(solution)/shard_map/ppermute | solution.py:344
  23.1 4.4 %collective-permute-start.9 = (s16[18,16,128]{2,1,0:T(8,128)(2,1)S(1)}, s16[18,16,128]{2,1,0:T(8,128)(2,1)S(1)}, u32[]{:S(2)}, u32[]{:S(2)}) collective-permute-start(s16[18,16,128]{2,1,0:T(8,128)(2,1)S(1)} %shard_map.91), channel_id=1, source_target_pairs={{0,2},{1,9},{2,0},{3,11},{4,6},{5,13},{6,4},{7,15},{8,10},{9,1},{1... | collective-permute-start | bytes 221192 | tf_op jit(solution)/shard_map/ppermute | solution.py:344
  24.0 1.3 %collective-permute-start.7 = (f32[8,16,128]{2,1,0:T(8,128)S(1)}, f32[8,16,128]{2,1,0:T(8,128)S(1)}, u32[]{:S(2)}, u32[]{:S(2)}) collective-permute-start(f32[8,16,128]{2,1,0:T(8,128)S(1)} %get-tuple-element.29), channel_id=1, source_target_pairs={{0,1},{1,0},{2,3},{3,2},{4,5},{5,4},{6,7},{7,6},{8,9},{9,8},{10,11... | collective-permute-start | bytes 196616 | tf_op jit(solution)/shard_map/ppermute | solution.py:341
  27.6 1.3 %collective-permute-start.14 = (f32[8,16,128]{2,1,0:T(8,128)S(1)}, f32[8,16,128]{2,1,0:T(8,128)S(1)}, u32[]{:S(2)}, u32[]{:S(2)}) collective-permute-start(f32[8,16,128]{2,1,0:T(8,128)S(1)} %get-tuple-element.37), channel_id=1, source_target_pairs={{0,1},{1,0},{2,3},{3,2},{4,5},{5,4},{6,7},{7,6},{8,9},{9,8},{10,11... | collective-permute-start | bytes 196616 | tf_op jit(solution)/shard_map/ppermute | solution.py:341
